TPU v7x, 256 devices: a whole 4x4x8 slice. The times are simulated.
256 devices in a mesh: grp: 8 (over z_hi, core), shard: 32 (over y, x, z_lo).
Axes of the slice: x: 4, y: 4, z: 8 (z_hi: 4, z_lo: 2; z = z_hi * 2 + z_lo), core: 2. Of those that a mesh axis runs over, the one named last changes fastest.
Arguments:
- embeddings: bfloat16 [262144, 768], P(('grp', 'shard')), may hold values from -0.26 to 0.26
- centers: bfloat16 [2048, 768], P('shard'), may hold values from -0.26 to 0.26
- assignment: int32 [262144, 1], P(('grp', 'shard')), may hold values from 0 to 2047, as said below
Outputs:
- old_min: float32 [262144], P(('grp', 'shard'))
- refined_centers: float32 [2048, 768], P('shard')
- new_min: float32 [262144], P(('grp', 'shard'))
Inputs may be any that keep to these rules, and one draw needn't show every extreme that they name: `assignment`: every cluster is named by at least one row; cluster k belongs to the index of shard that holds centers[k]; the rows of one device name clusters belonging to any one index of shard at least 16 and at most 64 times, and in every group one index of shard is named 64 times by the rows of each device of that group.
All inputs are finite; a program needn't handle non-finite values.
Results may differ from a plain program's by a relative error of at most 0.0003.
Values may be sent and summed in bfloat16 or wider, within the bound.
No kernel may reach another device: no remote copies, remote signals or barrier semaphores. Data moves between devices by JAX's collectives and lax.ppermute only.
A program may use at most 64 MiB of HBM per device.

v0:
```python
import jax
import jax.numpy as jnp
from jax import lax
from jax.experimental import pallas as pl
from jax.experimental.pallas import tpu as pltpu
from jax.sharding import Mesh, PartitionSpec as P

AXES = ("zh", "core", "y", "x", "zl")
SIZES = (4, 2, 4, 4, 2)
SHARD = ("y", "x", "zl")

D = 768
HALF = 32
CHUNKS = 32
COLS = D // 128
BODY = COLS * HALF
CODED = BODY + 16
LIMIT = 32700.0
VMEM = 16 * 1024 * 1024


def diagonal(rows):
    r = lax.broadcasted_iota(jnp.int32, (rows, 128), 0) % HALF
    c = lax.broadcasted_iota(jnp.int32, (rows, 128), 1)
    return r == c


def to_lanes(column):
    return jnp.sum(jnp.where(diagonal(HALF), column, 0.0), 0, keepdims=True)


def to_column(row):
    return jnp.sum(jnp.where(diagonal(HALF), row, 0.0), 1, keepdims=True)


def code_of(values):
    most = jnp.max(jnp.abs(values), 1, keepdims=True)
    return jnp.ceil(jnp.log2(jnp.maximum(most, 1e-30)) * 256.0)


def quantize(values, code):
    scaled = values * (LIMIT * jnp.exp2(code * (-1.0 / 256.0)))
    return jnp.floor(scaled + 0.5).astype(jnp.int32).astype(jnp.int16)


def scale_of(code):
    return jnp.exp2(code * (1.0 / 256.0)) * (1.0 / LIMIT)


def footer(counts, codes):
    r = lax.broadcasted_iota(jnp.int32, (16, 128), 0)
    both = jnp.where(r == 0, counts, jnp.where(r == 1, codes, 0.0))
    return both.astype(jnp.int32).astype(jnp.int16)


TILE = 256
EACH = TILE // HALF


def is_named(t, place, labels):
    first, second, half = (place[i] for i in range(3))
    j = lax.broadcasted_iota(jnp.int32, (TILE, 1), 0)
    c = j // HALF
    shard = (c // 2) * first + t * second + c % 2
    k = shard * (2 * HALF) + half + j % HALF
    return jnp.where(k == labels, 1.0, 0.0)


def own_sums_kernel(place, labels, rows, out_ref):
    for t in range(4):
        hot = is_named(t, place, labels[...]).astype(jnp.bfloat16)
        out_ref[t * TILE : (t + 1) * TILE, :] = jnp.dot(
            hot, rows[...], preferred_element_type=jnp.float32
        )


def chip_sums_kernel(place, own_labels, labels, own_sums, rows, out_ref):
    for t in range(4):
        hot = is_named(t, place, labels[...])
        sums = own_sums[t * TILE : (t + 1) * TILE, :] + jnp.dot(
            hot.astype(jnp.bfloat16), rows[...], preferred_element_type=jnp.float32
        )
        hot = hot + is_named(t, place, own_labels[...])
        counts = jnp.sum(hot, 1, keepdims=True)
        code = code_of(sums)
        coded = quantize(sums, code)
        for c in range(EACH):
            part = slice(c * HALF, (c + 1) * HALF)
            for b in range(COLS):
                out_ref[t * EACH + c, block(b), :] = coded[part, b * 128 : (b + 1) * 128]
            out_ref[t * EACH + c, BODY:CODED, :] = footer(
                to_lanes(counts[part]), to_lanes(code[part])
            )


def block(b):
    return slice(b * HALF, (b + 1) * HALF)


def add_coded(ref, at, blocks, counts):
    foot = ref[at, BODY:CODED, :].astype(jnp.float32)
    scale = scale_of(to_column(foot[1:2, :]))
    blocks = [
        blocks[b] + ref[at, block(b), :].astype(jnp.float32) * scale
        for b in range(COLS)
    ]
    return blocks, counts + foot[0:1, :]


def nothing():
    zeros = [jnp.zeros((HALF, 128), jnp.float32) for _ in range(COLS)]
    return zeros, jnp.zeros((1, 128), jnp.float32)


def code_blocks(blocks):
    most = jnp.abs(blocks[0])
    for b in range(1, COLS):
        most = jnp.maximum(most, jnp.abs(blocks[b]))
    code = code_of(most)
    return [quantize(blocks[b], code) for b in range(COLS)], to_lanes(code)


def add_and_code(ref, sources, out_ref, to):
    blocks, counts = nothing()
    for at in sources:
        blocks, counts = add_coded(ref, at, blocks, counts)
    coded, codes = code_blocks(blocks)
    for b in range(COLS):
        out_ref[to, block(b), :] = coded[b]
    out_ref[to, BODY:CODED, :] = footer(counts, codes)


def first_sums_kernel(in_ref, c0, c1, c2, c3, out_ref, centers_ref):
    for c in range(EACH):
        add_and_code(in_ref, range(c, 4 * EACH, EACH), out_ref, c)
    for i, ref in enumerate((c0, c1, c2, c3)):
        n = ref.shape[0]
        centers_ref[i * n : (i + 1) * n] = ref[...]


def second_sums_kernel(in_ref, out_ref):
    add_and_code(in_ref, range(EACH), out_ref, 0)


def refine_kernel(own, one, two, three, refined_ref, coded_ref):
    even = add_coded(two, 0, *add_coded(own, 0, *nothing()))
    odd = add_coded(three, 0, *add_coded(one, 0, *nothing()))
    counts = to_column(even[1] + odd[1])
    refined = [(even[0][b] + odd[0][b]) / counts for b in range(COLS)]
    for b in range(COLS):
        refined_ref[:, b * 128 : (b + 1) * 128] = refined[b]
    coded, codes = code_blocks(refined)
    foot = footer(jnp.zeros_like(codes), codes)
    for c in range(EACH):
        for b in range(COLS):
            coded_ref[c, block(b), :] = coded[b]
        coded_ref[c, BODY:CODED, :] = foot


def nearest(value, least):
    n = value.shape[0]
    return jnp.minimum(least, jnp.min(value.reshape(n // 8, 8, value.shape[1]), 0))


def old_kernel(norms_ref, rows_ref, *refs):
    *centers, out_ref, turned_ref = refs
    turned_ref[...] = (rows_ref[...] * jnp.bfloat16(-2.0)).T
    turned = turned_ref[...]
    least = jnp.full((8, turned.shape[1]), jnp.inf, jnp.float32)
    for ref in centers:
        wide = ref[...].astype(jnp.float32)
        norm = jnp.sum(wide * wide, 1, keepdims=True)
        product = jnp.dot(ref[...], turned, preferred_element_type=jnp.float32)
        least = nearest(product + norm, least)
    out_ref[...] = norms_ref[...] + jnp.min(least, 0, keepdims=True)


def new_kernel(turned_ref, norms_ref, least_ref, *refs):
    *pieces, out_ref = refs
    turned = turned_ref[...]
    least = least_ref[...]
    for ref, t in [(ref, t) for ref in pieces for t in range(CHUNKS // EACH)]:
        high, low, scale, norm = [], [], [], []
        for c in range(t * EACH, (t + 1) * EACH):
            wide = jnp.concatenate(
                [ref[c, block(b), :].astype(jnp.float32) for b in range(COLS)], 1
            )
            top = wide.astype(jnp.bfloat16)
            high.append(top)
            low.append((wide - top.astype(jnp.float32)).astype(jnp.bfloat16))
            foot = ref[c, BODY:CODED, :].astype(jnp.float32)
            s = scale_of(to_column(foot[1:2, :]))
            scale.append(s)
            norm.append(jnp.sum(wide * wide, 1, keepdims=True) * (s * s))
        product = jnp.dot(
            jnp.concatenate(high, 0), turned, preferred_element_type=jnp.float32
        ) + jnp.dot(jnp.concatenate(low, 0), turned, preferred_element_type=jnp.float32)
        value = product * jnp.concatenate(scale, 0) + jnp.concatenate(norm, 0)
        least = nearest(value, least)
    if out_ref.shape == least.shape:
        out_ref[...] = least
    else:
        out_ref[...] = norms_ref[...] + jnp.min(least, 0, keepdims=True)


def call(kernel, out_shape, *args, flops=0, moved=0, smem=0):
    specs = [
        pl.BlockSpec(memory_space=pltpu.SMEM if i < smem else pltpu.VMEM)
        for i in range(len(args))
    ]
    many = isinstance(out_shape, tuple)
    out_specs = pl.BlockSpec(memory_space=pltpu.VMEM)
    return pl.pallas_call(
        kernel,
        out_shape=out_shape,
        in_specs=specs,
        out_specs=tuple([out_specs] * len(out_shape)) if many else out_specs,
        compiler_params=pltpu.CompilerParams(vmem_limit_bytes=VMEM),
        cost_estimate=pl.CostEstimate(
            flops=flops, bytes_accessed=moved, transcendentals=0
        ),
    )(*args)


def swap(value, axis):
    return lax.ppermute(value, axis, [(0, 1), (1, 0)])


def around_z(part):
    return [part] + [
        lax.ppermute(part, "zh", [(i, (i + k) % 4) for i in range(4)])
        for k in (1, 2, 3)
    ]


def spot(core, a, b, zl):
    y, x = (b, a) if core == 0 else (a, b)
    return ((core * 4 + y) * 4 + x) * 2 + zl


def fours():
    return [
        [spot(core, a, b, 0) // 2 for a in range(4)]
        for core in range(2)
        for b in range(4)
    ]


def eights():
    return [
        [spot(core, a, b, z) for b in range(4) for z in range(2)]
        for core in range(2)
        for a in range(4)
    ]


def exchange_four(value):
    return lax.all_to_all(
        value.reshape(4, -1, 128), ("core", "y", "x"), 0, 0, axis_index_groups=fours()
    ).reshape(value.shape)


def exchange_eight(value):
    return lax.all_to_all(
        value, ("core", "y", "x", "zl"), 0, 0, axis_index_groups=eights()
    )


def around(part, turn):
    parts = [part]
    for k in (1, 3, 2):
        pairs = []
        for core in range(2):
            for a in range(4):
                for b in range(4):
                    to = ((a + k) % 4, b) if turn == 0 else (a, (b + k) % 4)
                    pairs.append((spot(core, a, b, 0) // 2, spot(core, *to, 0) // 2))
        parts.append(lax.ppermute(part, ("core", "y", "x"), pairs))
    return parts


def after(first, values):
    return lax.optimization_barrier((first, *values))[1:]


def on_device(embeddings, centers, assignment):
    n = embeddings.shape[0]
    f32, bf16, i16 = jnp.float32, jnp.bfloat16, jnp.int16
    shape = jax.ShapeDtypeStruct

    def coded(chunks):
        return shape((chunks, CODED, 128), i16)

    core = lax.axis_index("core")
    first = core == 0
    place = jnp.stack(
        [jnp.where(first, 8, 2), jnp.where(first, 2, 8), core * HALF]
    ).astype(jnp.int32)

    labels = assignment.reshape(1, n)
    other_labels = swap(labels, "core")
    other_rows = swap(embeddings, "core")

    mine = lax.dynamic_slice(centers, (core * HALF, 0), (HALF, D))
    current = jnp.concatenate([mine, swap(mine, "zl")])
    (other_rows, current) = lax.optimization_barrier((other_rows, current))

    wide = embeddings.astype(f32)
    norms = jnp.sum(wide * wide, 1).reshape(1, n)

    sums = call(
        own_sums_kernel,
        shape((4 * TILE, D), f32),
        place, labels, embeddings,
        flops=2 * 1024 * n * D, moved=5 << 20, smem=1,
    )
    sums = call(
        chip_sums_kernel,
        coded(CHUNKS),
        place, labels, other_labels, sums, other_rows,
        flops=2 * 1024 * n * D, moved=6 << 20, smem=1,
    )

    (current,) = after(sums, (current,))
    sums, current = call(
        first_sums_kernel,
        (coded(EACH), shape((8 * HALF, D), bf16)),
        exchange_four(sums), *around(current, 0),
        flops=1 << 22, moved=3 << 20,
    )
    group = call(
        second_sums_kernel,
        coded(1),
        exchange_eight(sums),
        flops=1 << 20, moved=1 << 20,
    )
    (current,) = after(group, (current,))
    groups, current = lax.optimization_barrier((around_z(group), around(current, 1)))
    refined, code = call(
        refine_kernel,
        (shape((HALF, D), f32), coded(EACH)),
        *groups,
        flops=1 << 20, moved=1 << 20,
    )

    new = exchange_eight(code)
    new = exchange_four(
        jnp.broadcast_to(new[None], (4, *new.shape)).reshape(CHUNKS, CODED, 128)
    )

    current = list(after(refined, current))
    current_other = [swap(part, "core") for part in current]
    old_min, turned = call(
        old_kernel,
        (shape((1, n), f32), shape((D, n), bf16)),
        norms, embeddings, *current, *current_other,
        flops=2 * 2048 * n * D, moved=5 << 20,
    )

    refined_other = swap(refined, "core")
    refined_centers = jnp.concatenate(
        [
            jnp.where(first, refined, refined_other),
            jnp.where(first, refined_other, refined),
        ]
    )

    new, turned, refined_centers = lax.optimization_barrier(
        (new, turned, refined_centers)
    )
    new_other = swap(new, "core")
    least = jnp.full((8, n), jnp.inf, f32)
    for piece, result in ((new, 8), (new_other, 1)):
        least = call(
            new_kernel,
            shape((result, n), f32),
            turned, norms, least, piece,
            flops=4 * 1024 * n * D, moved=3 << 20,
        )
    return old_min.reshape(n), refined_centers, least.reshape(n)


def solution(mesh):
    fine = Mesh(mesh.devices.reshape(SIZES), AXES)
    rows = ("zh", "core") + SHARD
    return jax.shard_map(
        on_device,
        mesh=fine,
        in_specs=(P(rows, None), P(SHARD, None), P(rows, None)),
        out_specs=(P(rows), P(SHARD, None), P(rows)),
        check_vma=False,
    )
```

profile of v0, /device:TPU:1, one launch (start us, length us, event | category | flops | bytes accessed | tf_op | source)
XLA Modules:
  0.0 108.8 jit_solution(13738703863029158510)
XLA Ops:
  0.6 3.3 %collective-permute-start.1 = (bf16[1024,768]{1,0:T(8,128)(2,1)}, bf16[1024,768]{1,0:T(8,128)(2,1)S(1)}, u32[]{:S(2)}, u32[]{:S(2)}) collective-permute-start(bf16[1024,768]{1,0:T(8,128)(2,1)} %rows_ref.1), channel_id=1, source_target_pairs={{0,32},{32,0},{1,33},{33,1},{2,34},{34,2},{3,35},{35,3},{4,36},{36... | collective-permute-start | bytes 4718600 | tf_op jit(solution)/shard_map/ppermute | solution.py:226
  4.0 1.0 collective-permute-start
  5.0 1.4 %copy-done.1 = bf16[1024,768]{1,0:T(8,128)(2,1)S(1)} copy-done((bf16[1024,768]{1,0:T(8,128)(2,1)S(1)}, bf16[1024,768]{1,0:T(8,128)(2,1)}, u32[]{:S(2)}) %copy-start.1) | copy-done | bytes 1572888
  7.1 2.4 %shard_map.58.own_sums = f32[1024,768]{1,0:T(8,128)S(1)} custom-call(s32[3]{0:T(128)S(1)} %pad_add_fusion.place, s32[1,1024]{1,0:T(1,128)S(1)} %bitcast.15, bf16[1024,768]{1,0:T(8,128)(2,1)S(1)} %copy-done.1), custom_call_target="tpu_custom_call" | custom-call | flops 1610612736 | bytes 5242880 | tf_op jit(solution)/shard_map/pallas_call | solution.py:213
  9.6 4.8 %shard_map.59 = s16[32,208,128]{2,1,0:T(8,128)(2,1)} custom-call(s32[3]{0:T(128)S(1)} %pad_add_fusion.place, s32[1,1024]{1,0:T(1,128)S(1)} %bitcast.16, s32[1,1024]{1,0:T(1,128)S(1)} %collective-permute-done.labels, f32[1024,768]{1,0:T(8,128)S(1)} %shard_map.58.own_sums, bf16[1024,768]{1,0:T(8,128)(2,1)S(1)} %collective-permute-done.1.rows), custom_call_target="tpu_custom_call" | custom-call | flops 1610612736 | bytes 6291456 | tf_op jit(solution)/shard_map/pallas_call | solution.py:213
  14.4 4.2 %all-to-all-start = ((s16[4,1664,128]{2,1,0:T(8,128)(2,1)}), s16[4,1664,128]{2,1,0:T(8,128)(2,1)S(1)}, u32[]{:S(2)}, u32[]{:S(2)}) async-start(s16[4,1664,128]{2,1,0:T(8,128)(2,1)} %bitcast.5), calls=%async_computation | async-start | bytes 3407872 | tf_op jit(solution)/shard_map/all_to_all | solution.py:258
  18.6 1.5 %collective-permute-start.3 = (bf16[64,768]{1,0:T(8,128)(2,1)S(1)}, bf16[64,768]{1,0:T(8,128)(2,1)S(1)}, u32[]{:S(2)}, u32[]{:S(2)}) collective-permute-start(bf16[64,768]{1,0:T(8,128)(2,1)S(1)} %pad_maximum_fusion.1.c0), channel_id=1, source_target_pairs={{0,2},{8,10},{16,18},{24,26},{2,4},{10,12},{18,20},{26,28},{4,6},{... | collective-permute-start | bytes 294920 | tf_op jit(solution)/shard_map/ppermute | solution.py:278
  20.0 1.2 %collective-permute-start.4 = (bf16[64,768]{1,0:T(8,128)(2,1)S(1)}, bf16[64,768]{1,0:T(8,128)(2,1)S(1)}, u32[]{:S(2)}, u32[]{:S(2)}) collective-permute-start(bf16[64,768]{1,0:T(8,128)(2,1)S(1)} %pad_maximum_fusion.1.c0), channel_id=1, source_target_pairs={{0,6},{8,14},{16,22},{24,30},{2,0},{10,8},{18,16},{26,24},{4,2},{1... | collective-permute-start | bytes 294920 | tf_op jit(solution)/shard_map/ppermute | solution.py:278
  21.3 1.7 %collective-permute-start.5 = (bf16[64,768]{1,0:T(8,128)(2,1)S(1)}, bf16[64,768]{1,0:T(8,128)(2,1)S(1)}, u32[]{:S(2)}, u32[]{:S(2)}) collective-permute-start(bf16[64,768]{1,0:T(8,128)(2,1)S(1)} %pad_maximum_fusion.1.c0), channel_id=1, source_target_pairs={{0,4},{8,12},{16,20},{24,28},{2,6},{10,14},{18,22},{26,30},{4,0},{... | collective-permute-start | bytes 294920 | tf_op jit(solution)/shard_map/ppermute | solution.py:278
  23.0 9.9 %collective-permute-done.3.c1 = bf16[64,768]{1,0:T(8,128)(2,1)S(1)} collective-permute-done((bf16[64,768]{1,0:T(8,128)(2,1)S(1)}, bf16[64,768]{1,0:T(8,128)(2,1)S(1)}, u32[]{:S(2)}, u32[]{:S(2)}) %collective-permute-start.3) | collective-permute-done | bytes 98336 | tf_op jit(solution)/shard_map/ppermute | solution.py:278
  32.9 1.4 %collective-permute-done.5.c3 = bf16[64,768]{1,0:T(8,128)(2,1)S(1)} collective-permute-done((bf16[64,768]{1,0:T(8,128)(2,1)S(1)}, bf16[64,768]{1,0:T(8,128)(2,1)S(1)}, u32[]{:S(2)}, u32[]{:S(2)}) %collective-permute-start.5) | collective-permute-done | bytes 98336 | tf_op jit(solution)/shard_map/ppermute | solution.py:278
  34.3 0.8 shard_map.60
  35.1 12.5 %all_to_all.20.in_ref = s16[8,208,128]{2,1,0:T(8,128)(2,1)S(1)} all-to-all(s16[8,208,128]{2,1,0:T(8,128)(2,1)S(1)} %get-tuple-element.31), channel_id=1, replica_groups={{0,1,8,9,16,17,24,25},{2,3,10,11,18,19,26,27},{4,5,12,13,20,21,28,29},{..., dimensions={0} | all-to-all | bytes 851968 | tf_op jit(solution)/shard_map/all_to_all | solution.py:264
  47.9 1.0 collective-permute-start.10
  48.9 1.0 collective-permute-start.11
  49.8 3.0 %collective-permute-start.6 = (s16[1,208,128]{2,1,0:T(8,128)(2,1)S(1)}, s16[1,208,128]{2,1,0:T(8,128)(2,1)S(1)}, u32[]{:S(2)}, u32[]{:S(2)}) collective-permute-start(s16[1,208,128]{2,1,0:T(8,128)(2,1)S(1)} %shard_map.61.own), channel_id=1, source_target_pairs={{0,64},{64,128},{128,192},{192,0},{1,65},{65,129},{129,193},{193,1... | collective-permute-start | bytes 159752 | tf_op jit(solution)/shard_map/ppermute | solution.py:231
  52.8 4.7 %collective-permute-start.7 = (s16[1,208,128]{2,1,0:T(8,128)(2,1)S(1)}, s16[1,208,128]{2,1,0:T(8,128)(2,1)S(1)}, u32[]{:S(2)}, u32[]{:S(2)}) collective-permute-start(s16[1,208,128]{2,1,0:T(8,128)(2,1)S(1)} %shard_map.61.own), channel_id=1, source_target_pairs={{0,128},{64,192},{128,0},{192,64},{1,129},{65,193},{129,1},{193,65... | collective-permute-start | bytes 159752 | tf_op jit(solution)/shard_map/ppermute | solution.py:231
  57.5 2.4 %collective-permute-start.8 = (s16[1,208,128]{2,1,0:T(8,128)(2,1)S(1)}, s16[1,208,128]{2,1,0:T(8,128)(2,1)S(1)}, u32[]{:S(2)}, u32[]{:S(2)}) collective-permute-start(s16[1,208,128]{2,1,0:T(8,128)(2,1)S(1)} %shard_map.61.own), channel_id=1, source_target_pairs={{0,192},{64,0},{128,64},{192,128},{1,193},{65,1},{129,65},{193,129... | collective-permute-start | bytes 159752 | tf_op jit(solution)/shard_map/ppermute | solution.py:231
  59.9 3.5 %collective-permute-done.8.three = s16[1,208,128]{2,1,0:T(8,128)(2,1)S(1)} collective-permute-done((s16[1,208,128]{2,1,0:T(8,128)(2,1)S(1)}, s16[1,208,128]{2,1,0:T(8,128)(2,1)S(1)}, u32[]{:S(2)}, u32[]{:S(2)}) %collective-permute-start.8) | collective-permute-done | bytes 53280 | tf_op jit(solution)/shard_map/ppermute | solution.py:231
  63.4 0.7 copy-done.6
  64.2 0.8 copy-done.8
  65.2 11.0 %all_to_all.21 = s16[8,208,128]{2,1,0:T(8,128)(2,1)S(1)} all-to-all(s16[8,208,128]{2,1,0:T(8,128)(2,1)S(1)} %get-tuple-element.48), channel_id=1, replica_groups={{0,1,8,9,16,17,24,25},{2,3,10,11,18,19,26,27},{4,5,12,13,20,21,28,29},{..., dimensions={0} | all-to-all | bytes 851968 | tf_op jit(solution)/shard_map/all_to_all | solution.py:264
  76.2 1.4 %broadcast_in_dim.12 = s16[4,1664,128]{2,1,0:T(8,128)(2,1)} broadcast(s16[1664,128]{1,0:T(8,128)(2,1)S(1)} %bitcast.20), dimensions={1,2} | broadcast | bytes 2129920 | tf_op jit(solution)/shard_map/broadcast_in_dim | solution.py:348
  77.6 3.7 %all-to-all-start.3 = ((s16[4,1664,128]{2,1,0:T(8,128)(2,1)}), s16[4,1664,128]{2,1,0:T(8,128)(2,1)S(1)}, u32[]{:S(2)}, u32[]{:S(2)}) async-start(s16[4,1664,128]{2,1,0:T(8,128)(2,1)} %broadcast_in_dim.12), calls=%async_computation.3 | async-start | bytes 3407872 | tf_op jit(solution)/shard_map/all_to_all | solution.py:258
  81.4 4.1 %collective-permute-start.16 = (f32[32,768]{1,0:T(8,128)S(1)}, f32[32,768]{1,0:T(8,128)S(1)}, u32[]{:S(2)}, u32[]{:S(2)}) collective-permute-start(f32[32,768]{1,0:T(8,128)S(1)} %get-tuple-element.38), channel_id=1, source_target_pairs={{0,32},{32,0},{1,33},{33,1},{2,34},{34,2},{3,35},{35,3},{4,36},{36... | collective-permute-start | bytes 294920 | tf_op jit(solution)/shard_map/ppermute | solution.py:226
  86.9 0.7 pad_maximum_fusion
  89.1 5.3 %shard_map.63 = (f32[1,1024]{1,0:T(1,128)}, bf16[768,1024]{1,0:T(8,128)(2,1)S(1)}) custom-call(f32[1,1024]{1,0:T(1,128)S(1)} %bitcast.17, bf16[1024,768]{1,0:T(8,128)(2,1)S(1)} %copy-done.2, bf16[256,768]{1,0:T(8,128)(2,1)S(1)} %copy-done.5, bf16[256,768]{1,0:T(8,128)(2,1)} %collective-permute-done.9.refs_1_, bf16[256,768]{1,0:T(8,128)(2,1)S(1)} %copy-done.7, ...), custom_call_target="tpu_custom_call" | custom-call | flops 3221225472 | bytes 5242880 | tf_op jit(solution)/shard_map/pallas_call | solution.py:213
  94.3 1.2 %copy-done.10 = bf16[768,1024]{1,0:T(8,128)(2,1)} copy-done((bf16[768,1024]{1,0:T(8,128)(2,1)}, bf16[768,1024]{1,0:T(8,128)(2,1)S(1)}, u32[]{:S(2)}) %copy-start.10) | copy-done | bytes 1572888
  95.5 4.2 %collective-permute-start.17 = (s16[32,208,128]{2,1,0:T(8,128)(2,1)S(1)}, s16[32,208,128]{2,1,0:T(8,128)(2,1)S(1)}, u32[]{:S(2)}, u32[]{:S(2)}) collective-permute-start(s16[32,208,128]{2,1,0:T(8,128)(2,1)S(1)} %bitcast.12), channel_id=1, source_target_pairs={{0,32},{32,0},{1,33},{33,1},{2,34},{34,2},{3,35},{35,3},{4,36},{36... | collective-permute-start | bytes 5111816 | tf_op jit(solution)/shard_map/ppermute | solution.py:226
  99.7 1.4 %copy-done.11 = bf16[768,1024]{1,0:T(8,128)(2,1)S(1)} copy-done((bf16[768,1024]{1,0:T(8,128)(2,1)S(1)}, bf16[768,1024]{1,0:T(8,128)(2,1)}, u32[]{:S(2)}) %copy-start.11) | copy-done | bytes 1572888
  101.1 3.6 %shard_map.64.least_ref = f32[8,1024]{1,0:T(8,128)S(1)} custom-call(bf16[768,1024]{1,0:T(8,128)(2,1)S(1)} %copy-done.11, f32[1,1024]{1,0:T(1,128)S(1)} %bitcast.18, f32[8,1024]{1,0:T(8,128)S(1)} %broadcast_in_dim.13.least_ref, s16[32,208,128]{2,1,0:T(8,128)(2,1)S(1)} %bitcast.13), custom_call_target="tpu_custom_call" | custom-call | flops 3221225472 | bytes 3145728 | tf_op jit(solution)/shard_map/pallas_call | solution.py:213
  104.7 4.1 %shard_map.65 = f32[1,1024]{1,0:T(1,128)} custom-call(bf16[768,1024]{1,0:T(8,128)(2,1)S(1)} %copy-done.11, f32[1,1024]{1,0:T(1,128)S(1)} %bitcast.19, f32[8,1024]{1,0:T(8,128)S(1)} %shard_map.64.least_ref, s16[32,208,128]{2,1,0:T(8,128)(2,1)S(1)} %collective-permute-done.17.refs_0_), custom_call_target="tpu_custom_call" | custom-call | flops 3221225472 | bytes 3145728 | tf_op jit(solution)/shard_map/pallas_call | solution.py:213
  (50 shorter events, 4.3 us)
Async XLA Ops:
  0.6 3.3 %copy-start = (bf16[64,768]{1,0:T(8,128)(2,1)S(1)}, bf16[64,768]{1,0:T(8,128)(2,1)}, u32[]{:S(2)}) copy-start(bf16[64,768]{1,0:T(8,128)(2,1)} %param.4) | copy-start | bytes 294916
  0.6 8.9 %collective-permute-start.1 = (bf16[1024,768]{1,0:T(8,128)(2,1)}, bf16[1024,768]{1,0:T(8,128)(2,1)S(1)}, u32[]{:S(2)}, u32[]{:S(2)}) collective-permute-start(bf16[1024,768]{1,0:T(8,128)(2,1)} %rows_ref.1), channel_id=1, source_target_pairs={{0,32},{32,0},{1,33},{33,1},{2,34},{34,2},{3,35},{35,3},{4,36},{36... | collective-permute-start | bytes 4718600 | tf_op jit(solution)/shard_map/ppermute | solution.py:226
  4.0 5.6 %collective-permute-start.2 = (bf16[32,768]{1,0:T(8,128)(2,1)S(1)}, bf16[32,768]{1,0:T(8,128)(2,1)S(1)}, u32[]{:S(2)}, u32[]{:S(2)}) collective-permute-start(bf16[32,768]{1,0:T(8,128)(2,1)S(1)} %constant_dynamic-slice_fusion), channel_id=1, source_target_pairs={{0,1},{1,0},{2,3},{3,2},{4,5},{5,4},{6,7},{7,6},{8,9},{9,8},{10,11... | collective-permute-start | bytes 147464 | tf_op jit(solution)/shard_map/ppermute | solution.py:226
  4.0 5.6 %collective-permute-start = (s32[1,1024]{1,0:T(1,128)}, s32[1,1024]{1,0:T(1,128)S(1)}, u32[]{:S(2)}, u32[]{:S(2)}) collective-permute-start(s32[1,1024]{1,0:T(1,128)} %bitcast.14), channel_id=1, source_target_pairs={{0,32},{32,0},{1,33},{33,1},{2,34},{34,2},{3,35},{35,3},{4,36},{36... | collective-permute-start | bytes 12296 | tf_op jit(solution)/shard_map/ppermute | solution.py:226
  5.0 1.4 %copy-start.1 = (bf16[1024,768]{1,0:T(8,128)(2,1)S(1)}, bf16[1024,768]{1,0:T(8,128)(2,1)}, u32[]{:S(2)}) copy-start(bf16[1024,768]{1,0:T(8,128)(2,1)} %rows_ref.1) | copy-start | bytes 4718596
  6.4 0.7 copy-start.3
  14.4 19.9 %all-to-all-start = ((s16[4,1664,128]{2,1,0:T(8,128)(2,1)}), s16[4,1664,128]{2,1,0:T(8,128)(2,1)S(1)}, u32[]{:S(2)}, u32[]{:S(2)}) async-start(s16[4,1664,128]{2,1,0:T(8,128)(2,1)} %bitcast.5), calls=%async_computation | async-start | bytes 3407872 | tf_op jit(solution)/shard_map/all_to_all | solution.py:258
  18.6 14.3 %collective-permute-start.3 = (bf16[64,768]{1,0:T(8,128)(2,1)S(1)}, bf16[64,768]{1,0:T(8,128)(2,1)S(1)}, u32[]{:S(2)}, u32[]{:S(2)}) collective-permute-start(bf16[64,768]{1,0:T(8,128)(2,1)S(1)} %pad_maximum_fusion.1.c0), channel_id=1, source_target_pairs={{0,2},{8,10},{16,18},{24,26},{2,4},{10,12},{18,20},{26,28},{4,6},{... | collective-permute-start | bytes 294920 | tf_op jit(solution)/shard_map/ppermute | solution.py:278
  20.0 12.8 %collective-permute-start.4 = (bf16[64,768]{1,0:T(8,128)(2,1)S(1)}, bf16[64,768]{1,0:T(8,128)(2,1)S(1)}, u32[]{:S(2)}, u32[]{:S(2)}) collective-permute-start(bf16[64,768]{1,0:T(8,128)(2,1)S(1)} %pad_maximum_fusion.1.c0), channel_id=1, source_target_pairs={{0,6},{8,14},{16,22},{24,30},{2,0},{10,8},{18,16},{26,24},{4,2},{1... | collective-permute-start | bytes 294920 | tf_op jit(solution)/shard_map/ppermute | solution.py:278
  21.3 13.0 %collective-permute-start.5 = (bf16[64,768]{1,0:T(8,128)(2,1)S(1)}, bf16[64,768]{1,0:T(8,128)(2,1)S(1)}, u32[]{:S(2)}, u32[]{:S(2)}) collective-permute-start(bf16[64,768]{1,0:T(8,128)(2,1)S(1)} %pad_maximum_fusion.1.c0), channel_id=1, source_target_pairs={{0,4},{8,12},{16,20},{24,28},{2,6},{10,14},{18,22},{26,30},{4,0},{... | collective-permute-start | bytes 294920 | tf_op jit(solution)/shard_map/ppermute | solution.py:278
  35.1 42.5 %copy-start.4 = (bf16[256,768]{1,0:T(8,128)(2,1)}, bf16[256,768]{1,0:T(8,128)(2,1)S(1)}, u32[]{:S(2)}) copy-start(bf16[256,768]{1,0:T(8,128)(2,1)S(1)} %get-tuple-element.43.refs_0_) | copy-start | bytes 1179652
  47.9 15.5 %collective-permute-start.10 = (bf16[256,768]{1,0:T(8,128)(2,1)S(1)}, bf16[256,768]{1,0:T(8,128)(2,1)S(1)}, u32[]{:S(2)}, u32[]{:S(2)}) collective-permute-start(bf16[256,768]{1,0:T(8,128)(2,1)S(1)} %get-tuple-element.43.refs_0_), channel_id=1, source_target_pairs={{0,24},{8,0},{16,8},{24,16},{2,26},{10,2},{18,10},{26,18},{4,28},{... | collective-permute-start | bytes 1179656 | tf_op jit(solution)/shard_map/ppermute | solution.py:278
  48.9 14.5 %collective-permute-start.11 = (bf16[256,768]{1,0:T(8,128)(2,1)S(1)}, bf16[256,768]{1,0:T(8,128)(2,1)S(1)}, u32[]{:S(2)}, u32[]{:S(2)}) collective-permute-start(bf16[256,768]{1,0:T(8,128)(2,1)S(1)} %get-tuple-element.43.refs_0_), channel_id=1, source_target_pairs={{0,16},{8,24},{16,0},{24,8},{2,18},{10,26},{18,2},{26,10},{4,20},{... | collective-permute-start | bytes 1179656 | tf_op jit(solution)/shard_map/ppermute | solution.py:278
  49.8 15.1 %collective-permute-start.9 = (bf16[256,768]{1,0:T(8,128)(2,1)S(1)}, bf16[256,768]{1,0:T(8,128)(2,1)}, u32[]{:S(2)}, u32[]{:S(2)}) collective-permute-start(bf16[256,768]{1,0:T(8,128)(2,1)S(1)} %get-tuple-element.43.refs_0_), channel_id=1, source_target_pairs={{0,8},{8,16},{16,24},{24,0},{2,10},{10,18},{18,26},{26,2},{4,12},{... | collective-permute-start | bytes 1179656 | tf_op jit(solution)/shard_map/ppermute | solution.py:278
  49.8 7.7 %collective-permute-start.6 = (s16[1,208,128]{2,1,0:T(8,128)(2,1)S(1)}, s16[1,208,128]{2,1,0:T(8,128)(2,1)S(1)}, u32[]{:S(2)}, u32[]{:S(2)}) collective-permute-start(s16[1,208,128]{2,1,0:T(8,128)(2,1)S(1)} %shard_map.61.own), channel_id=1, source_target_pairs={{0,64},{64,128},{128,192},{192,0},{1,65},{65,129},{129,193},{193,1... | collective-permute-start | bytes 159752 | tf_op jit(solution)/shard_map/ppermute | solution.py:231
  52.8 7.1 %collective-permute-start.7 = (s16[1,208,128]{2,1,0:T(8,128)(2,1)S(1)}, s16[1,208,128]{2,1,0:T(8,128)(2,1)S(1)}, u32[]{:S(2)}, u32[]{:S(2)}) collective-permute-start(s16[1,208,128]{2,1,0:T(8,128)(2,1)S(1)} %shard_map.61.own), channel_id=1, source_target_pairs={{0,128},{64,192},{128,0},{192,64},{1,129},{65,193},{129,1},{193,65... | collective-permute-start | bytes 159752 | tf_op jit(solution)/shard_map/ppermute | solution.py:231
  57.5 5.9 %collective-permute-start.8 = (s16[1,208,128]{2,1,0:T(8,128)(2,1)S(1)}, s16[1,208,128]{2,1,0:T(8,128)(2,1)S(1)}, u32[]{:S(2)}, u32[]{:S(2)}) collective-permute-start(s16[1,208,128]{2,1,0:T(8,128)(2,1)S(1)} %shard_map.61.own), channel_id=1, source_target_pairs={{0,192},{64,0},{128,64},{192,128},{1,193},{65,1},{129,65},{193,129... | collective-permute-start | bytes 159752 | tf_op jit(solution)/shard_map/ppermute | solution.py:231
  63.4 0.8 copy-start.6
  64.1 0.8 copy-start.8
  77.6 8.9 %copy-start.2 = (bf16[1024,768]{1,0:T(8,128)(2,1)S(1)}, bf16[1024,768]{1,0:T(8,128)(2,1)}, u32[]{:S(2)}) copy-start(bf16[1024,768]{1,0:T(8,128)(2,1)} %rows_ref.1) | copy-start | bytes 4718596
  77.6 17.9 %all-to-all-start.3 = ((s16[4,1664,128]{2,1,0:T(8,128)(2,1)}), s16[4,1664,128]{2,1,0:T(8,128)(2,1)S(1)}, u32[]{:S(2)}, u32[]{:S(2)}) async-start(s16[4,1664,128]{2,1,0:T(8,128)(2,1)} %broadcast_in_dim.12), calls=%async_computation.3 | async-start | bytes 3407872 | tf_op jit(solution)/shard_map/all_to_all | solution.py:258
  81.3 7.7 %copy-start.5 = (bf16[256,768]{1,0:T(8,128)(2,1)S(1)}, bf16[256,768]{1,0:T(8,128)(2,1)}, u32[]{:S(2)}) copy-start(bf16[256,768]{1,0:T(8,128)(2,1)} %copy-done.4) | copy-start | bytes 1179652
  81.3 7.7 %copy-start.7 = (bf16[256,768]{1,0:T(8,128)(2,1)S(1)}, bf16[256,768]{1,0:T(8,128)(2,1)}, u32[]{:S(2)}) copy-start(bf16[256,768]{1,0:T(8,128)(2,1)} %copy-done.6) | copy-start | bytes 1179652
  81.4 7.7 %copy-start.9 = (bf16[256,768]{1,0:T(8,128)(2,1)S(1)}, bf16[256,768]{1,0:T(8,128)(2,1)}, u32[]{:S(2)}) copy-start(bf16[256,768]{1,0:T(8,128)(2,1)} %copy-done.8) | copy-start | bytes 1179652
  81.4 5.5 %collective-permute-start.16 = (f32[32,768]{1,0:T(8,128)S(1)}, f32[32,768]{1,0:T(8,128)S(1)}, u32[]{:S(2)}, u32[]{:S(2)}) collective-permute-start(f32[32,768]{1,0:T(8,128)S(1)} %get-tuple-element.38), channel_id=1, source_target_pairs={{0,32},{32,0},{1,33},{33,1},{2,34},{34,2},{3,35},{35,3},{4,36},{36... | collective-permute-start | bytes 294920 | tf_op jit(solution)/shard_map/ppermute | solution.py:226
  85.5 2.1 %collective-permute-start.12 = (bf16[256,768]{1,0:T(8,128)(2,1)}, bf16[256,768]{1,0:T(8,128)(2,1)S(1)}, u32[]{:S(2)}, u32[]{:S(2)}) collective-permute-start(bf16[256,768]{1,0:T(8,128)(2,1)} %copy-done.4), channel_id=1, source_target_pairs={{0,32},{32,0},{1,33},{33,1},{2,34},{34,2},{3,35},{35,3},{4,36},{36... | collective-permute-start | bytes 1179656 | tf_op jit(solution)/shard_map/ppermute | solution.py:226
  85.6 2.4 %collective-permute-start.13 = (bf16[256,768]{1,0:T(8,128)(2,1)}, bf16[256,768]{1,0:T(8,128)(2,1)S(1)}, u32[]{:S(2)}, u32[]{:S(2)}) collective-permute-start(bf16[256,768]{1,0:T(8,128)(2,1)} %collective-permute-done.9.refs_1_), channel_id=1, source_target_pairs={{0,32},{32,0},{1,33},{33,1},{2,34},{34,2},{3,35},{35,3},{4,36},{36... | collective-permute-start | bytes 1179656 | tf_op jit(solution)/shard_map/ppermute | solution.py:226
  86.0 2.5 %collective-permute-start.14 = (bf16[256,768]{1,0:T(8,128)(2,1)}, bf16[256,768]{1,0:T(8,128)(2,1)S(1)}, u32[]{:S(2)}, u32[]{:S(2)}) collective-permute-start(bf16[256,768]{1,0:T(8,128)(2,1)} %copy-done.6), channel_id=1, source_target_pairs={{0,32},{32,0},{1,33},{33,1},{2,34},{34,2},{3,35},{35,3},{4,36},{36... | collective-permute-start | bytes 1179656 | tf_op jit(solution)/shard_map/ppermute | solution.py:226
  86.1 3.0 %collective-permute-start.15 = (bf16[256,768]{1,0:T(8,128)(2,1)}, bf16[256,768]{1,0:T(8,128)(2,1)S(1)}, u32[]{:S(2)}, u32[]{:S(2)}) collective-permute-start(bf16[256,768]{1,0:T(8,128)(2,1)} %copy-done.8), channel_id=1, source_target_pairs={{0,32},{32,0},{1,33},{33,1},{2,34},{34,2},{3,35},{35,3},{4,36},{36... | collective-permute-start | bytes 1179656 | tf_op jit(solution)/shard_map/ppermute | solution.py:226
  94.3 1.2 %copy-start.10 = (bf16[768,1024]{1,0:T(8,128)(2,1)}, bf16[768,1024]{1,0:T(8,128)(2,1)S(1)}, u32[]{:S(2)}) copy-start(bf16[768,1024]{1,0:T(8,128)(2,1)S(1)} %get-tuple-element.51.turned_ref) | copy-start | bytes 4718596
  95.5 9.2 %collective-permute-start.17 = (s16[32,208,128]{2,1,0:T(8,128)(2,1)S(1)}, s16[32,208,128]{2,1,0:T(8,128)(2,1)S(1)}, u32[]{:S(2)}, u32[]{:S(2)}) collective-permute-start(s16[32,208,128]{2,1,0:T(8,128)(2,1)S(1)} %bitcast.12), channel_id=1, source_target_pairs={{0,32},{32,0},{1,33},{33,1},{2,34},{34,2},{3,35},{35,3},{4,36},{36... | collective-permute-start | bytes 5111816 | tf_op jit(solution)/shard_map/ppermute | solution.py:226
  99.7 1.4 %copy-start.11 = (bf16[768,1024]{1,0:T(8,128)(2,1)S(1)}, bf16[768,1024]{1,0:T(8,128)(2,1)}, u32[]{:S(2)}) copy-start(bf16[768,1024]{1,0:T(8,128)(2,1)} %copy-done.10) | copy-start | bytes 4718596
where the time goes:
time: 109 us
  starting transfers between devices  37.9 us (35%)
  blocking collectives  23.5 us (22%)
  Pallas kernels  21.5 us (20%)
  waiting for transfers between devices  16.3 us (15%)
  local copies, waits for them, and re-layouts  7.66 us (7%)
  other arithmetic  1.17 us (1%)
    all_to_all x2, blocking collectives, exchange_eight(): lax.all_to_all(value, ('core', 'y', 'x', 'zl'), 0, 0, axis_index_groups=e...  23.5 us
    pallas_call x8, Pallas kernels, call(): pl.pallas_call(kernel, out_shape=out_shape, in_specs=specs, out_specs=tup...  21.5 us
    ppermute x9, starting transfers between devices, swap(): return lax.ppermute(value, axis, [(0, 1), (1, 0)])  13.6 us
    ppermute x6, waiting for transfers between devices, around(): parts.append(lax.ppermute(part, ('core', 'y', 'x'), pairs))  11.3 us
    ppermute x3, starting transfers between devices, around_z(): lax.ppermute(part, 'zh', [(i, (i + k) % 4) for i in range(4)])  10 us
    all_to_all x2, starting transfers between devices, exchange_four(): lax.all_to_all(value.reshape(4, -1, 128), ('core', 'y', 'x'), 0, 0, axis_...  7.89 us
    ppermute x6, starting transfers between devices, around(): parts.append(lax.ppermute(part, ('core', 'y', 'x'), pairs))  6.38 us
    unnamed x24, local copies, waits for them, and re-layouts  6.22 us
  transfers between devices with their start and end apart: 20, of which 6 were waited for; matrix products, arithmetic and copies ran while one was open for 1% of the time, Pallas kernels for 10%

commit v1 on v0

--- a/solution.py
+++ b/solution.py
@@ -130,16 +130,16 @@
     out_ref[to, BODY:CODED, :] = footer(counts, codes)
 
 
-def first_sums_kernel(in_ref, c0, c1, c2, c3, out_ref, centers_ref):
+def first_sums_kernel(in_ref, out_ref):
     for c in range(EACH):
         add_and_code(in_ref, range(c, 4 * EACH, EACH), out_ref, c)
+
+
+def second_sums_kernel(in_ref, c0, c1, c2, c3, out_ref, centers_ref):
+    add_and_code(in_ref, range(EACH), out_ref, 0)
     for i, ref in enumerate((c0, c1, c2, c3)):
         n = ref.shape[0]
         centers_ref[i * n : (i + 1) * n] = ref[...]
-
-
-def second_sums_kernel(in_ref, out_ref):
-    add_and_code(in_ref, range(EACH), out_ref, 0)
 
 
 def refine_kernel(own, one, two, three, refined_ref, coded_ref):
@@ -321,17 +321,17 @@
         flops=2 * 1024 * n * D, moved=6 << 20, smem=1,
     )
 
+    sums = call(
+        first_sums_kernel,
+        coded(EACH),
+        exchange_four(sums),
+        flops=1 << 22, moved=3 << 20,
+    )
     (current,) = after(sums, (current,))
-    sums, current = call(
-        first_sums_kernel,
-        (coded(EACH), shape((8 * HALF, D), bf16)),
-        exchange_four(sums), *around(current, 0),
-        flops=1 << 22, moved=3 << 20,
-    )
-    group = call(
+    group, current = call(
         second_sums_kernel,
-        coded(1),
-        exchange_eight(sums),
+        (coded(1), shape((8 * HALF, D), bf16)),
+        exchange_eight(sums), *around(current, 0),
         flops=1 << 20, moved=1 << 20,
     )
     (current,) = after(group, (current,))
@@ -344,9 +344,6 @@
     )
 
     new = exchange_eight(code)
-    new = exchange_four(
-        jnp.broadcast_to(new[None], (4, *new.shape)).reshape(CHUNKS, CODED, 128)
-    )
 
     current = list(after(refined, current))
     current_other = [swap(part, "core") for part in current]
@@ -367,6 +364,9 @@
 
     new, turned, refined_centers = lax.optimization_barrier(
         (new, turned, refined_centers)
+    )
+    new = exchange_four(
+        jnp.broadcast_to(new[None], (4, *new.shape)).reshape(CHUNKS, CODED, 128)
     )
     new_other = swap(new, "core")
     least = jnp.full((8, n), jnp.inf, f32)

time: 109 us -> 110 us (level)
  blocking collectives: 23.5 us -> 34.4 us
  waiting for transfers between devices: 16.3 us -> 10.4 us
  local copies, waits for them, and re-layouts: 7.66 us -> 4.53 us
  starting transfers between devices: 37.9 us -> 35.7 us
    all_to_all x2, blocking collectives: 23.5 us -> 34.4 us  [exchange_four(): lax.all_to_all(value.reshape(4, -1, 128), ('core', 'y', 'x'), 0, 0, axis_...]
    ppermute x6, waiting for transfers between devices: 11.3 us -> 7.26 us  [around(): parts.append(lax.ppermute(part, ('core', 'y', 'x'), pairs))]
    unnamed x24 -> x12, local copies, waits for them, and re-layouts: 6.22 us -> 3.3 us
    ppermute x3, waiting for transfers between devices: 3.51 us -> 1.91 us  [around_z(): lax.ppermute(part, 'zh', [(i, (i + k) % 4) for i in range(4)])]
    ppermute x9, waiting for transfers between devices: 1.5 us -> 0.02 us  [swap(): return lax.ppermute(value, axis, [(0, 1), (1, 0)])]
    ppermute x6, starting transfers between devices: 6.38 us -> 4.91 us  [around(): parts.append(lax.ppermute(part, ('core', 'y', 'x'), pairs))]
    all_to_all x2, waiting for transfers between devices: 0.01 us -> 1.23 us  [exchange_eight(): lax.all_to_all(value, ('core', 'y', 'x', 'zl'), 0, 0, axis_index_groups=e...]
  transfers between devices with their start and end apart: 20 -> 20, of which waited for: 6 -> 5; matrix products, arithmetic and copies ran while one was open for 1% -> 1% of each run, Pallas kernels for 10% -> 11%
where the time goes in v1:
time: 110 us; the launch traced here: 109 us
  starting transfers between devices  35.7 us (32%)
  blocking collectives  34.4 us (31%)
  Pallas kernels  22.3 us (20%)
  waiting for transfers between devices  10.4 us (9%)
  local copies, waits for them, and re-layouts  4.53 us (4%)
  other arithmetic  1.17 us (1%)
    all_to_all x2, blocking collectives, exchange_four(): lax.all_to_all(value.reshape(4, -1, 128), ('core', 'y', 'x'), 0, 0, axis_...  34.4 us
    pallas_call x8, Pallas kernels, call(): pl.pallas_call(kernel, out_shape=out_shape, in_specs=specs, out_specs=tup...  22.3 us
    ppermute x9, starting transfers between devices, swap(): return lax.ppermute(value, axis, [(0, 1), (1, 0)])  12.7 us
    ppermute x3, starting transfers between devices, around_z(): lax.ppermute(part, 'zh', [(i, (i + k) % 4) for i in range(4)])  10 us
    all_to_all x2, starting transfers between devices, exchange_eight(): lax.all_to_all(value, ('core', 'y', 'x', 'zl'), 0, 0, axis_index_groups=e...  8.07 us
    ppermute x6, waiting for transfers between devices, around(): parts.append(lax.ppermute(part, ('core', 'y', 'x'), pairs))  7.26 us
    ppermute x6, starting transfers between devices, around(): parts.append(lax.ppermute(part, ('core', 'y', 'x'), pairs))  4.91 us
    unnamed x12, local copies, waits for them, and re-layouts  3.3 us
  transfers between devices with their start and end apart: 20, of which 5 were waited for; matrix products, arithmetic and copies ran while one was open for 1% of the time, Pallas kernels for 11%

profile of v1, /device:TPU:1, one launch (start us, length us, event | category | flops | bytes accessed | tf_op | source)
XLA Modules:
  0.0 109.4 jit_solution(10592608825374309193)
XLA Ops:
  0.6 3.3 %collective-permute-start.1 = (bf16[1024,768]{1,0:T(8,128)(2,1)}, bf16[1024,768]{1,0:T(8,128)(2,1)S(1)}, u32[]{:S(2)}, u32[]{:S(2)}) collective-permute-start(bf16[1024,768]{1,0:T(8,128)(2,1)} %rows_ref.1), channel_id=1, source_target_pairs={{0,32},{32,0},{1,33},{33,1},{2,34},{34,2},{3,35},{35,3},{4,36},{36... | collective-permute-start | bytes 4718600 | tf_op jit(solution)/shard_map/ppermute | solution.py:226
  4.0 1.0 collective-permute-start
  5.0 1.4 %copy-done.1 = bf16[1024,768]{1,0:T(8,128)(2,1)S(1)} copy-done((bf16[1024,768]{1,0:T(8,128)(2,1)S(1)}, bf16[1024,768]{1,0:T(8,128)(2,1)}, u32[]{:S(2)}) %copy-start.1) | copy-done | bytes 1572888
  6.4 0.7 copy-done.3
  7.1 2.4 %shard_map.58.own_sums = f32[1024,768]{1,0:T(8,128)S(1)} custom-call(s32[3]{0:T(128)S(1)} %pad_add_fusion.place, s32[1,1024]{1,0:T(1,128)S(1)} %bitcast.16, bf16[1024,768]{1,0:T(8,128)(2,1)S(1)} %copy-done.1), custom_call_target="tpu_custom_call" | custom-call | flops 1610612736 | bytes 5242880 | tf_op jit(solution)/shard_map/pallas_call | solution.py:213
  9.6 3.6 %shard_map.59 = s16[32,208,128]{2,1,0:T(8,128)(2,1)S(1)} custom-call(s32[3]{0:T(128)S(1)} %pad_add_fusion.place, s32[1,1024]{1,0:T(1,128)S(1)} %bitcast.17, s32[1,1024]{1,0:T(1,128)S(1)} %collective-permute-done.labels, f32[1024,768]{1,0:T(8,128)S(1)} %shard_map.58.own_sums, bf16[1024,768]{1,0:T(8,128)(2,1)S(1)} %collective-permute-done.1.rows), custom_call_target="tpu_custom_call" | custom-call | flops 1610612736 | bytes 6291456 | tf_op jit(solution)/shard_map/pallas_call | solution.py:213
  13.2 17.4 %all_to_all.20 = s16[4,1664,128]{2,1,0:T(8,128)(2,1)S(1)} all-to-all(s16[4,1664,128]{2,1,0:T(8,128)(2,1)S(1)} %bitcast.11), channel_id=1, replica_groups={{0,2,4,6},{8,10,12,14},{16,18,20,22},{24,26,28,30},{32,40,48,56},{34,42..., dimensions={0} | all-to-all | bytes 3407872 | tf_op jit(solution)/shard_map/all_to_all | solution.py:258
  30.6 1.6 %shard_map.60 = s16[8,208,128]{2,1,0:T(8,128)(2,1)} custom-call(s16[32,208,128]{2,1,0:T(8,128)(2,1)S(1)} %bitcast.12), custom_call_target="tpu_custom_call" | custom-call | flops 4194304 | bytes 3145728 | tf_op jit(solution)/shard_map/pallas_call | solution.py:213
  32.2 4.0 %all-to-all-start.1 = ((s16[8,208,128]{2,1,0:T(8,128)(2,1)}), s16[8,208,128]{2,1,0:T(8,128)(2,1)S(1)}, u32[]{:S(2)}, u32[]{:S(2)}) async-start(s16[8,208,128]{2,1,0:T(8,128)(2,1)} %shard_map.60), calls=%async_computation.1 | async-start | bytes 851968 | tf_op jit(solution)/shard_map/all_to_all | solution.py:264
  36.5 2.4 %collective-permute-start.4 = (bf16[64,768]{1,0:T(8,128)(2,1)S(1)}, bf16[64,768]{1,0:T(8,128)(2,1)S(1)}, u32[]{:S(2)}, u32[]{:S(2)}) collective-permute-start(bf16[64,768]{1,0:T(8,128)(2,1)S(1)} %pad_maximum_fusion.1.c0), channel_id=1, source_target_pairs={{0,6},{8,14},{16,22},{24,30},{2,0},{10,8},{18,16},{26,24},{4,2},{1... | collective-permute-start | bytes 294920 | tf_op jit(solution)/shard_map/ppermute | solution.py:278
  38.8 2.0 %collective-permute-done.3.c1 = bf16[64,768]{1,0:T(8,128)(2,1)S(1)} collective-permute-done((bf16[64,768]{1,0:T(8,128)(2,1)S(1)}, bf16[64,768]{1,0:T(8,128)(2,1)S(1)}, u32[]{:S(2)}, u32[]{:S(2)}) %collective-permute-start.3) | collective-permute-done | bytes 98336 | tf_op jit(solution)/shard_map/ppermute | solution.py:278
  40.8 0.6 collective-permute-done.4.c2
  41.4 4.6 %collective-permute-done.5.c3 = bf16[64,768]{1,0:T(8,128)(2,1)S(1)} collective-permute-done((bf16[64,768]{1,0:T(8,128)(2,1)S(1)}, bf16[64,768]{1,0:T(8,128)(2,1)S(1)}, u32[]{:S(2)}, u32[]{:S(2)}) %collective-permute-start.5) | collective-permute-done | bytes 98336 | tf_op jit(solution)/shard_map/ppermute | solution.py:278
  46.4 1.0 collective-permute-start.10
  47.4 1.1 %collective-permute-start.11 = (bf16[256,768]{1,0:T(8,128)(2,1)S(1)}, bf16[256,768]{1,0:T(8,128)(2,1)S(1)}, u32[]{:S(2)}, u32[]{:S(2)}) collective-permute-start(bf16[256,768]{1,0:T(8,128)(2,1)S(1)} %get-tuple-element.42.refs_0_), channel_id=1, source_target_pairs={{0,16},{8,24},{16,0},{24,8},{2,18},{10,26},{18,2},{26,10},{4,20},{... | collective-permute-start | bytes 1179656 | tf_op jit(solution)/shard_map/ppermute | solution.py:278
  48.6 3.0 %collective-permute-start.6 = (s16[1,208,128]{2,1,0:T(8,128)(2,1)S(1)}, s16[1,208,128]{2,1,0:T(8,128)(2,1)S(1)}, u32[]{:S(2)}, u32[]{:S(2)}) collective-permute-start(s16[1,208,128]{2,1,0:T(8,128)(2,1)S(1)} %get-tuple-element.33.own), channel_id=1, source_target_pairs={{0,64},{64,128},{128,192},{192,0},{1,65},{65,129},{129,193},{193,1... | collective-permute-start | bytes 159752 | tf_op jit(solution)/shard_map/ppermute | solution.py:231
  51.6 4.7 %collective-permute-start.7 = (s16[1,208,128]{2,1,0:T(8,128)(2,1)S(1)}, s16[1,208,128]{2,1,0:T(8,128)(2,1)S(1)}, u32[]{:S(2)}, u32[]{:S(2)}) collective-permute-start(s16[1,208,128]{2,1,0:T(8,128)(2,1)S(1)} %get-tuple-element.33.own), channel_id=1, source_target_pairs={{0,128},{64,192},{128,0},{192,64},{1,129},{65,193},{129,1},{193,65... | collective-permute-start | bytes 159752 | tf_op jit(solution)/shard_map/ppermute | solution.py:231
  56.2 2.4 %collective-permute-start.8 = (s16[1,208,128]{2,1,0:T(8,128)(2,1)S(1)}, s16[1,208,128]{2,1,0:T(8,128)(2,1)S(1)}, u32[]{:S(2)}, u32[]{:S(2)}) collective-permute-start(s16[1,208,128]{2,1,0:T(8,128)(2,1)S(1)} %get-tuple-element.33.own), channel_id=1, source_target_pairs={{0,192},{64,0},{128,64},{192,128},{1,193},{65,1},{129,65},{193,129... | collective-permute-start | bytes 159752 | tf_op jit(solution)/shard_map/ppermute | solution.py:231
  58.6 1.9 %collective-permute-done.8.three = s16[1,208,128]{2,1,0:T(8,128)(2,1)S(1)} collective-permute-done((s16[1,208,128]{2,1,0:T(8,128)(2,1)S(1)}, s16[1,208,128]{2,1,0:T(8,128)(2,1)S(1)}, u32[]{:S(2)}, u32[]{:S(2)}) %collective-permute-start.8) | collective-permute-done | bytes 53280 | tf_op jit(solution)/shard_map/ppermute | solution.py:231
  60.5 1.0 shard_map.62
  61.6 5.3 %collective-permute-start.16 = (f32[32,768]{1,0:T(8,128)S(1)}, f32[32,768]{1,0:T(8,128)S(1)}, u32[]{:S(2)}, u32[]{:S(2)}) collective-permute-start(f32[32,768]{1,0:T(8,128)S(1)} %get-tuple-element.37), channel_id=1, source_target_pairs={{0,32},{32,0},{1,33},{33,1},{2,34},{34,2},{3,35},{35,3},{4,36},{36... | collective-permute-start | bytes 294920 | tf_op jit(solution)/shard_map/ppermute | solution.py:226
  66.9 0.5 collective-permute-start.13
  67.9 4.1 %all-to-all-start.2 = ((s16[8,208,128]{2,1,0:T(8,128)(2,1)}), s16[8,208,128]{2,1,0:T(8,128)(2,1)}, u32[]{:S(2)}, u32[]{:S(2)}) async-start(s16[8,208,128]{2,1,0:T(8,128)(2,1)} %get-tuple-element.47), calls=%async_computation.2 | async-start | bytes 851968 | tf_op jit(solution)/shard_map/all_to_all | solution.py:264
  72.5 0.7 pad_maximum_fusion
  73.2 5.6 %shard_map.63 = (f32[1,1024]{1,0:T(1,128)}, bf16[768,1024]{1,0:T(8,128)(2,1)S(1)}) custom-call(f32[1,1024]{1,0:T(1,128)S(1)} %bitcast.18, bf16[1024,768]{1,0:T(8,128)(2,1)S(1)} %copy-done.2, bf16[256,768]{1,0:T(8,128)(2,1)S(1)} %get-tuple-element.42.refs_0_, bf16[256,768]{1,0:T(8,128)(2,1)} %collective-permute-done.9.refs_1_, ...), custom_call_target="tpu_custom_call" | custom-call | flops 3221225472 | bytes 5242880 | tf_op jit(solution)/shard_map/pallas_call | solution.py:213
  78.8 1.2 %copy-done.4 = bf16[768,1024]{1,0:T(8,128)(2,1)} copy-done((bf16[768,1024]{1,0:T(8,128)(2,1)}, bf16[768,1024]{1,0:T(8,128)(2,1)S(1)}, u32[]{:S(2)}) %copy-start.4) | copy-done | bytes 1572888
  80.0 1.2 %all-to-all-done.2 = s16[8,208,128]{2,1,0:T(8,128)(2,1)} async-done(((s16[8,208,128]{2,1,0:T(8,128)(2,1)}), s16[8,208,128]{2,1,0:T(8,128)(2,1)}, u32[]{:S(2)}, u32[]{:S(2)}) %all-to-all-start.2) | async-done | bytes 426016 | tf_op jit(solution)/shard_map/all_to_all | solution.py:264
  81.2 1.2 %broadcast_in_dim.13 = s16[4,1664,128]{2,1,0:T(8,128)(2,1)S(1)} broadcast(s16[1664,128]{1,0:T(8,128)(2,1)} %bitcast.8), dimensions={1,2} | broadcast | bytes 2129920 | tf_op jit(solution)/shard_map/broadcast_in_dim | solution.py:369
  82.5 17.0 %all_to_all.21 = s16[4,1664,128]{2,1,0:T(8,128)(2,1)S(1)} all-to-all(s16[4,1664,128]{2,1,0:T(8,128)(2,1)S(1)} %broadcast_in_dim.13), channel_id=1, replica_groups={{0,2,4,6},{8,10,12,14},{16,18,20,22},{24,26,28,30},{32,40,48,56},{34,42..., dimensions={0} | all-to-all | bytes 3407872 | tf_op jit(solution)/shard_map/all_to_all | solution.py:258
  99.5 2.0 %collective-permute-start.17 = (s16[32,208,128]{2,1,0:T(8,128)(2,1)S(1)}, s16[32,208,128]{2,1,0:T(8,128)(2,1)S(1)}, u32[]{:S(2)}, u32[]{:S(2)}) collective-permute-start(s16[32,208,128]{2,1,0:T(8,128)(2,1)S(1)} %bitcast.13), channel_id=1, source_target_pairs={{0,32},{32,0},{1,33},{33,1},{2,34},{34,2},{3,35},{35,3},{4,36},{36... | collective-permute-start | bytes 5111816 | tf_op jit(solution)/shard_map/ppermute | solution.py:226
  101.5 3.6 %shard_map.64.least_ref = f32[8,1024]{1,0:T(8,128)S(1)} custom-call(bf16[768,1024]{1,0:T(8,128)(2,1)S(1)} %copy-done.5, f32[1,1024]{1,0:T(1,128)S(1)} %bitcast.19, f32[8,1024]{1,0:T(8,128)S(1)} %broadcast_in_dim.11.least_ref, s16[32,208,128]{2,1,0:T(8,128)(2,1)S(1)} %bitcast.14), custom_call_target="tpu_custom_call" | custom-call | flops 3221225472 | bytes 3145728 | tf_op jit(solution)/shard_map/pallas_call | solution.py:213
  105.2 4.2 %shard_map.65 = f32[1,1024]{1,0:T(1,128)} custom-call(bf16[768,1024]{1,0:T(8,128)(2,1)S(1)} %copy-done.5, f32[1,1024]{1,0:T(1,128)S(1)} %bitcast.20, f32[8,1024]{1,0:T(8,128)S(1)} %shard_map.64.least_ref, s16[32,208,128]{2,1,0:T(8,128)(2,1)S(1)} %collective-permute-done.17.refs_0_), custom_call_target="tpu_custom_call" | custom-call | flops 3221225472 | bytes 3145728 | tf_op jit(solution)/shard_map/pallas_call | solution.py:213
  (38 shorter events, 1.7 us)
Async XLA Ops:
  0.6 3.3 %copy-start = (bf16[64,768]{1,0:T(8,128)(2,1)S(1)}, bf16[64,768]{1,0:T(8,128)(2,1)}, u32[]{:S(2)}) copy-start(bf16[64,768]{1,0:T(8,128)(2,1)} %param.4) | copy-start | bytes 294916
  0.6 8.9 %collective-permute-start.1 = (bf16[1024,768]{1,0:T(8,128)(2,1)}, bf16[1024,768]{1,0:T(8,128)(2,1)S(1)}, u32[]{:S(2)}, u32[]{:S(2)}) collective-permute-start(bf16[1024,768]{1,0:T(8,128)(2,1)} %rows_ref.1), channel_id=1, source_target_pairs={{0,32},{32,0},{1,33},{33,1},{2,34},{34,2},{3,35},{35,3},{4,36},{36... | collective-permute-start | bytes 4718600 | tf_op jit(solution)/shard_map/ppermute | solution.py:226
  4.0 5.6 %collective-permute-start.2 = (bf16[32,768]{1,0:T(8,128)(2,1)S(1)}, bf16[32,768]{1,0:T(8,128)(2,1)S(1)}, u32[]{:S(2)}, u32[]{:S(2)}) collective-permute-start(bf16[32,768]{1,0:T(8,128)(2,1)S(1)} %constant_dynamic-slice_fusion), channel_id=1, source_target_pairs={{0,1},{1,0},{2,3},{3,2},{4,5},{5,4},{6,7},{7,6},{8,9},{9,8},{10,11... | collective-permute-start | bytes 147464 | tf_op jit(solution)/shard_map/ppermute | solution.py:226
  4.0 5.6 %collective-permute-start = (s32[1,1024]{1,0:T(1,128)}, s32[1,1024]{1,0:T(1,128)S(1)}, u32[]{:S(2)}, u32[]{:S(2)}) collective-permute-start(s32[1,1024]{1,0:T(1,128)} %bitcast.15), channel_id=1, source_target_pairs={{0,32},{32,0},{1,33},{33,1},{2,34},{34,2},{3,35},{35,3},{4,36},{36... | collective-permute-start | bytes 12296 | tf_op jit(solution)/shard_map/ppermute | solution.py:226
  5.0 1.4 %copy-start.1 = (bf16[1024,768]{1,0:T(8,128)(2,1)S(1)}, bf16[1024,768]{1,0:T(8,128)(2,1)}, u32[]{:S(2)}) copy-start(bf16[1024,768]{1,0:T(8,128)(2,1)} %rows_ref.1) | copy-start | bytes 4718596
  6.4 0.7 copy-start.3
  32.2 39.9 %copy-start.2 = (bf16[1024,768]{1,0:T(8,128)(2,1)S(1)}, bf16[1024,768]{1,0:T(8,128)(2,1)}, u32[]{:S(2)}) copy-start(bf16[1024,768]{1,0:T(8,128)(2,1)} %rows_ref.1) | copy-start | bytes 4718596
  32.2 13.9 %all-to-all-start.1 = ((s16[8,208,128]{2,1,0:T(8,128)(2,1)}), s16[8,208,128]{2,1,0:T(8,128)(2,1)S(1)}, u32[]{:S(2)}, u32[]{:S(2)}) async-start(s16[8,208,128]{2,1,0:T(8,128)(2,1)} %shard_map.60), calls=%async_computation.1 | async-start | bytes 851968 | tf_op jit(solution)/shard_map/all_to_all | solution.py:264
  36.2 4.7 %collective-permute-start.3 = (bf16[64,768]{1,0:T(8,128)(2,1)S(1)}, bf16[64,768]{1,0:T(8,128)(2,1)S(1)}, u32[]{:S(2)}, u32[]{:S(2)}) collective-permute-start(bf16[64,768]{1,0:T(8,128)(2,1)S(1)} %pad_maximum_fusion.1.c0), channel_id=1, source_target_pairs={{0,2},{8,10},{16,18},{24,26},{2,4},{10,12},{18,20},{26,28},{4,6},{... | collective-permute-start | bytes 294920 | tf_op jit(solution)/shard_map/ppermute | solution.py:278
  36.5 5.0 %collective-permute-start.4 = (bf16[64,768]{1,0:T(8,128)(2,1)S(1)}, bf16[64,768]{1,0:T(8,128)(2,1)S(1)}, u32[]{:S(2)}, u32[]{:S(2)}) collective-permute-start(bf16[64,768]{1,0:T(8,128)(2,1)S(1)} %pad_maximum_fusion.1.c0), channel_id=1, source_target_pairs={{0,6},{8,14},{16,22},{24,30},{2,0},{10,8},{18,16},{26,24},{4,2},{1... | collective-permute-start | bytes 294920 | tf_op jit(solution)/shard_map/ppermute | solution.py:278
  38.8 7.3 %collective-permute-start.5 = (bf16[64,768]{1,0:T(8,128)(2,1)S(1)}, bf16[64,768]{1,0:T(8,128)(2,1)S(1)}, u32[]{:S(2)}, u32[]{:S(2)}) collective-permute-start(bf16[64,768]{1,0:T(8,128)(2,1)S(1)} %pad_maximum_fusion.1.c0), channel_id=1, source_target_pairs={{0,4},{8,12},{16,20},{24,28},{2,6},{10,14},{18,22},{26,30},{4,0},{... | collective-permute-start | bytes 294920 | tf_op jit(solution)/shard_map/ppermute | solution.py:278
  46.4 14.2 %collective-permute-start.10 = (bf16[256,768]{1,0:T(8,128)(2,1)S(1)}, bf16[256,768]{1,0:T(8,128)(2,1)S(1)}, u32[]{:S(2)}, u32[]{:S(2)}) collective-permute-start(bf16[256,768]{1,0:T(8,128)(2,1)S(1)} %get-tuple-element.42.refs_0_), channel_id=1, source_target_pairs={{0,24},{8,0},{16,8},{24,16},{2,26},{10,2},{18,10},{26,18},{4,28},{... | collective-permute-start | bytes 1179656 | tf_op jit(solution)/shard_map/ppermute | solution.py:278
  47.4 13.1 %collective-permute-start.11 = (bf16[256,768]{1,0:T(8,128)(2,1)S(1)}, bf16[256,768]{1,0:T(8,128)(2,1)S(1)}, u32[]{:S(2)}, u32[]{:S(2)}) collective-permute-start(bf16[256,768]{1,0:T(8,128)(2,1)S(1)} %get-tuple-element.42.refs_0_), channel_id=1, source_target_pairs={{0,16},{8,24},{16,0},{24,8},{2,18},{10,26},{18,2},{26,10},{4,20},{... | collective-permute-start | bytes 1179656 | tf_op jit(solution)/shard_map/ppermute | solution.py:278
  48.5 12.0 %collective-permute-start.9 = (bf16[256,768]{1,0:T(8,128)(2,1)S(1)}, bf16[256,768]{1,0:T(8,128)(2,1)}, u32[]{:S(2)}, u32[]{:S(2)}) collective-permute-start(bf16[256,768]{1,0:T(8,128)(2,1)S(1)} %get-tuple-element.42.refs_0_), channel_id=1, source_target_pairs={{0,8},{8,16},{16,24},{24,0},{2,10},{10,18},{18,26},{26,2},{4,12},{... | collective-permute-start | bytes 1179656 | tf_op jit(solution)/shard_map/ppermute | solution.py:278
  48.6 7.7 %collective-permute-start.6 = (s16[1,208,128]{2,1,0:T(8,128)(2,1)S(1)}, s16[1,208,128]{2,1,0:T(8,128)(2,1)S(1)}, u32[]{:S(2)}, u32[]{:S(2)}) collective-permute-start(s16[1,208,128]{2,1,0:T(8,128)(2,1)S(1)} %get-tuple-element.33.own), channel_id=1, source_target_pairs={{0,64},{64,128},{128,192},{192,0},{1,65},{65,129},{129,193},{193,1... | collective-permute-start | bytes 159752 | tf_op jit(solution)/shard_map/ppermute | solution.py:231
  51.6 7.0 %collective-permute-start.7 = (s16[1,208,128]{2,1,0:T(8,128)(2,1)S(1)}, s16[1,208,128]{2,1,0:T(8,128)(2,1)S(1)}, u32[]{:S(2)}, u32[]{:S(2)}) collective-permute-start(s16[1,208,128]{2,1,0:T(8,128)(2,1)S(1)} %get-tuple-element.33.own), channel_id=1, source_target_pairs={{0,128},{64,192},{128,0},{192,64},{1,129},{65,193},{129,1},{193,65... | collective-permute-start | bytes 159752 | tf_op jit(solution)/shard_map/ppermute | solution.py:231
  56.2 4.3 %collective-permute-start.8 = (s16[1,208,128]{2,1,0:T(8,128)(2,1)S(1)}, s16[1,208,128]{2,1,0:T(8,128)(2,1)S(1)}, u32[]{:S(2)}, u32[]{:S(2)}) collective-permute-start(s16[1,208,128]{2,1,0:T(8,128)(2,1)S(1)} %get-tuple-element.33.own), channel_id=1, source_target_pairs={{0,192},{64,0},{128,64},{192,128},{1,193},{65,1},{129,65},{193,129... | collective-permute-start | bytes 159752 | tf_op jit(solution)/shard_map/ppermute | solution.py:231
  61.6 10.9 %collective-permute-start.16 = (f32[32,768]{1,0:T(8,128)S(1)}, f32[32,768]{1,0:T(8,128)S(1)}, u32[]{:S(2)}, u32[]{:S(2)}) collective-permute-start(f32[32,768]{1,0:T(8,128)S(1)} %get-tuple-element.37), channel_id=1, source_target_pairs={{0,32},{32,0},{1,33},{33,1},{2,34},{34,2},{3,35},{35,3},{4,36},{36... | collective-permute-start | bytes 294920 | tf_op jit(solution)/shard_map/ppermute | solution.py:226
  66.9 6.2 %collective-permute-start.12 = (bf16[256,768]{1,0:T(8,128)(2,1)S(1)}, bf16[256,768]{1,0:T(8,128)(2,1)}, u32[]{:S(2)}, u32[]{:S(2)}) collective-permute-start(bf16[256,768]{1,0:T(8,128)(2,1)S(1)} %get-tuple-element.42.refs_0_), channel_id=1, source_target_pairs={{0,32},{32,0},{1,33},{33,1},{2,34},{34,2},{3,35},{35,3},{4,36},{36... | collective-permute-start | bytes 1179656 | tf_op jit(solution)/shard_map/ppermute | solution.py:226
  66.9 6.2 %collective-permute-start.13 = (bf16[256,768]{1,0:T(8,128)(2,1)}, bf16[256,768]{1,0:T(8,128)(2,1)}, u32[]{:S(2)}, u32[]{:S(2)}) collective-permute-start(bf16[256,768]{1,0:T(8,128)(2,1)} %collective-permute-done.9.refs_1_), channel_id=1, source_target_pairs={{0,32},{32,0},{1,33},{33,1},{2,34},{34,2},{3,35},{35,3},{4,36},{36... | collective-permute-start | bytes 1179656 | tf_op jit(solution)/shard_map/ppermute | solution.py:226
  67.4 5.7 %collective-permute-start.14 = (bf16[256,768]{1,0:T(8,128)(2,1)S(1)}, bf16[256,768]{1,0:T(8,128)(2,1)}, u32[]{:S(2)}, u32[]{:S(2)}) collective-permute-start(bf16[256,768]{1,0:T(8,128)(2,1)S(1)} %collective-permute-done.10.refs_2_), channel_id=1, source_target_pairs={{0,32},{32,0},{1,33},{33,1},{2,34},{34,2},{3,35},{35,3},{4,36},{36... | collective-permute-start | bytes 1179656 | tf_op jit(solution)/shard_map/ppermute | solution.py:226
  67.4 5.7 %collective-permute-start.15 = (bf16[256,768]{1,0:T(8,128)(2,1)S(1)}, bf16[256,768]{1,0:T(8,128)(2,1)}, u32[]{:S(2)}, u32[]{:S(2)}) collective-permute-start(bf16[256,768]{1,0:T(8,128)(2,1)S(1)} %collective-permute-done.11.refs_3_), channel_id=1, source_target_pairs={{0,32},{32,0},{1,33},{33,1},{2,34},{34,2},{3,35},{35,3},{4,36},{36... | collective-permute-start | bytes 1179656 | tf_op jit(solution)/shard_map/ppermute | solution.py:226
  67.9 13.3 %all-to-all-start.2 = ((s16[8,208,128]{2,1,0:T(8,128)(2,1)}), s16[8,208,128]{2,1,0:T(8,128)(2,1)}, u32[]{:S(2)}, u32[]{:S(2)}) async-start(s16[8,208,128]{2,1,0:T(8,128)(2,1)} %get-tuple-element.47), calls=%async_computation.2 | async-start | bytes 851968 | tf_op jit(solution)/shard_map/all_to_all | solution.py:264
  78.8 1.2 %copy-start.4 = (bf16[768,1024]{1,0:T(8,128)(2,1)}, bf16[768,1024]{1,0:T(8,128)(2,1)S(1)}, u32[]{:S(2)}) copy-start(bf16[768,1024]{1,0:T(8,128)(2,1)S(1)} %get-tuple-element.50.turned_ref) | copy-start | bytes 4718596
  82.5 19.1 %copy-start.5 = (bf16[768,1024]{1,0:T(8,128)(2,1)S(1)}, bf16[768,1024]{1,0:T(8,128)(2,1)}, u32[]{:S(2)}) copy-start(bf16[768,1024]{1,0:T(8,128)(2,1)} %copy-done.4) | copy-start | bytes 4718596
  99.5 5.6 %collective-permute-start.17 = (s16[32,208,128]{2,1,0:T(8,128)(2,1)S(1)}, s16[32,208,128]{2,1,0:T(8,128)(2,1)S(1)}, u32[]{:S(2)}, u32[]{:S(2)}) collective-permute-start(s16[32,208,128]{2,1,0:T(8,128)(2,1)S(1)} %bitcast.13), channel_id=1, source_target_pairs={{0,32},{32,0},{1,33},{33,1},{2,34},{34,2},{3,35},{35,3},{4,36},{36... | collective-permute-start | bytes 5111816 | tf_op jit(solution)/shard_map/ppermute | solution.py:226

commit v2 on v1

--- a/solution.py
+++ b/solution.py
@@ -15,6 +15,8 @@
 COLS = D // 128
 BODY = COLS * HALF
 CODED = BODY + 16
+EIGHTH = 8
+SMALL = COLS * EIGHTH + 16
 LIMIT = 32700.0
 VMEM = 16 * 1024 * 1024
 
@@ -38,9 +40,16 @@
     return jnp.ceil(jnp.log2(jnp.maximum(most, 1e-30)) * 256.0)
 
 
+def scaled(values, code):
+    return jnp.floor(values * (LIMIT * jnp.exp2(code * (-1.0 / 256.0))) + 0.5)
+
+
+def whole(values):
+    return values.astype(jnp.int32).astype(jnp.int16)
+
+
 def quantize(values, code):
-    scaled = values * (LIMIT * jnp.exp2(code * (-1.0 / 256.0)))
-    return jnp.floor(scaled + 0.5).astype(jnp.int32).astype(jnp.int16)
+    return whole(scaled(values, code))
 
 
 def scale_of(code):
@@ -112,49 +121,95 @@
     return zeros, jnp.zeros((1, 128), jnp.float32)
 
 
-def code_blocks(blocks):
-    most = jnp.abs(blocks[0])
-    for b in range(1, COLS):
-        most = jnp.maximum(most, jnp.abs(blocks[b]))
-    code = code_of(most)
-    return [quantize(blocks[b], code) for b in range(COLS)], to_lanes(code)
-
-
-def add_and_code(ref, sources, out_ref, to):
-    blocks, counts = nothing()
-    for at in sources:
-        blocks, counts = add_coded(ref, at, blocks, counts)
-    coded, codes = code_blocks(blocks)
-    for b in range(COLS):
-        out_ref[to, block(b), :] = coded[b]
-    out_ref[to, BODY:CODED, :] = footer(counts, codes)
-
-
 def first_sums_kernel(in_ref, out_ref):
     for c in range(EACH):
-        add_and_code(in_ref, range(c, 4 * EACH, EACH), out_ref, c)
-
-
-def second_sums_kernel(in_ref, c0, c1, c2, c3, out_ref, centers_ref):
-    add_and_code(in_ref, range(EACH), out_ref, 0)
+        blocks, counts = nothing()
+        for at in range(c, 4 * EACH, EACH):
+            blocks, counts = add_coded(in_ref, at, blocks, counts)
+        most = jnp.abs(blocks[0])
+        for b in range(1, COLS):
+            most = jnp.maximum(most, jnp.abs(blocks[b]))
+        code = code_of(most)
+        values = [scaled(blocks[b], code) for b in range(COLS)]
+        last = [jnp.broadcast_to(v, (HALF, 128)) for v in (code, to_column(counts))]
+        for z in range(4):
+            part = slice(z * EIGHTH, (z + 1) * EIGHTH)
+            for t, pair in enumerate(
+                (values[0:2], values[2:4], values[4:6], last)
+            ):
+                both = jnp.concatenate([v[part] for v in pair], 0)
+                out_ref[z * EACH + c, tile_of(t), :] = whole(both)
+
+
+def tile_of(t):
+    return slice(t * 16, (t + 1) * 16)
+
+
+def refine_kernel(place, in_ref, c0, c1, c2, c3, out_ref, centers_ref):
+    total = [jnp.zeros((16, 128), jnp.float32) for _ in range(3)]
+    counts = jnp.zeros((EIGHTH, 128), jnp.float32)
+    for at in range(CHUNKS):
+        foot = in_ref[at, tile_of(3), :].astype(jnp.float32)
+        scale = scale_of(foot[:EIGHTH])
+        scale = jnp.concatenate([scale, scale], 0)
+        for t in range(3):
+            total[t] += in_ref[at, tile_of(t), :].astype(jnp.float32) * scale
+        counts = counts + foot[EIGHTH:]
+    counts = jnp.concatenate([counts, counts], 0)
+    lane = lax.broadcasted_iota(jnp.int32, (16, 128), 1)
+    foot = jnp.zeros((16, 128), jnp.float32)
+    coded = []
+    for t in range(3):
+        refined = total[t] / counts
+        code = code_of(refined)
+        coded.append(whole(scaled(refined, code)))
+        foot = jnp.where(lane == place[3] * 3 + t, code, foot)
+    coded.append(whole(foot))
+    for at in range(CHUNKS):
+        for t in range(4):
+            out_ref[at, tile_of(t), :] = coded[t]
     for i, ref in enumerate((c0, c1, c2, c3)):
         n = ref.shape[0]
         centers_ref[i * n : (i + 1) * n] = ref[...]
 
 
-def refine_kernel(own, one, two, three, refined_ref, coded_ref):
-    even = add_coded(two, 0, *add_coded(own, 0, *nothing()))
-    odd = add_coded(three, 0, *add_coded(one, 0, *nothing()))
-    counts = to_column(even[1] + odd[1])
-    refined = [(even[0][b] + odd[0][b]) / counts for b in range(COLS)]
-    for b in range(COLS):
-        refined_ref[:, b * 128 : (b + 1) * 128] = refined[b]
-    coded, codes = code_blocks(refined)
-    foot = footer(jnp.zeros_like(codes), codes)
+def decode(load, scales):
+    rows = []
+    for z in range(4):
+        tiles = [
+            load(z, t).astype(jnp.float32) * scales[:, z * 3 + t : z * 3 + t + 1]
+            for t in range(3)
+        ]
+        rows.append(
+            jnp.concatenate(
+                [tile[h * EIGHTH : (h + 1) * EIGHTH] for tile in tiles for h in range(2)],
+                1,
+            )
+        )
+    return jnp.concatenate(rows, 0)
+
+
+def merged_foot(ref, c):
+    foot = ref[c, tile_of(3), :].astype(jnp.float32)
+    for z in range(1, 4):
+        foot = foot + ref[z * EACH + c, tile_of(3), :].astype(jnp.float32)
+    return foot
+
+
+def repack_kernel(place, in_ref, out_ref, refined_ref):
     for c in range(EACH):
-        for b in range(COLS):
-            coded_ref[c, block(b), :] = coded[b]
-        coded_ref[c, BODY:CODED, :] = foot
+        foot = whole(merged_foot(in_ref, c))
+        for k in range(4):
+            for z in range(4):
+                out_ref[k * EACH + c, z * 48 : (z + 1) * 48, :] = in_ref[
+                    z * EACH + c, 0:48, :
+                ]
+            out_ref[k * EACH + c, BODY:CODED, :] = foot
+    own = place[4]
+    refined_ref[...] = decode(
+        lambda z, t: in_ref[z * EACH + own, tile_of(t), :],
+        scale_of(merged_foot(in_ref, own)),
+    )
 
 
 def nearest(value, least):
@@ -175,32 +230,39 @@
     out_ref[...] = norms_ref[...] + jnp.min(least, 0, keepdims=True)
 
 
-def new_kernel(turned_ref, norms_ref, least_ref, *refs):
-    *pieces, out_ref = refs
+def new_min(turned_ref, piece, least_ref):
     turned = turned_ref[...]
     least = least_ref[...]
-    for ref, t in [(ref, t) for ref in pieces for t in range(CHUNKS // EACH)]:
-        high, low, scale, norm = [], [], [], []
+    for t in range(CHUNKS // EACH):
+        high, low, norm = [], [], []
         for c in range(t * EACH, (t + 1) * EACH):
-            wide = jnp.concatenate(
-                [ref[c, block(b), :].astype(jnp.float32) for b in range(COLS)], 1
+            wide = decode(
+                lambda z, i, c=c: piece[c, z * 48 + i * 16 : z * 48 + i * 16 + 16, :],
+                scale_of(piece[c, BODY:CODED, :].astype(jnp.float32)),
             )
             top = wide.astype(jnp.bfloat16)
             high.append(top)
             low.append((wide - top.astype(jnp.float32)).astype(jnp.bfloat16))
-            foot = ref[c, BODY:CODED, :].astype(jnp.float32)
-            s = scale_of(to_column(foot[1:2, :]))
-            scale.append(s)
-            norm.append(jnp.sum(wide * wide, 1, keepdims=True) * (s * s))
+            norm.append(jnp.sum(wide * wide, 1, keepdims=True))
         product = jnp.dot(
             jnp.concatenate(high, 0), turned, preferred_element_type=jnp.float32
         ) + jnp.dot(jnp.concatenate(low, 0), turned, preferred_element_type=jnp.float32)
-        value = product * jnp.concatenate(scale, 0) + jnp.concatenate(norm, 0)
-        least = nearest(value, least)
-    if out_ref.shape == least.shape:
-        out_ref[...] = least
-    else:
-        out_ref[...] = norms_ref[...] + jnp.min(least, 0, keepdims=True)
+        least = nearest(product + jnp.concatenate(norm, 0), least)
+    return least
+
+
+def new_own_kernel(turned_ref, piece, least_ref, out_ref):
+    out_ref[...] = new_min(turned_ref, piece, least_ref)
+
+
+def new_other_kernel(
+    place, turned_ref, piece, least_ref, norms_ref, own, other, out_ref, refined_ref
+):
+    least = new_min(turned_ref, piece, least_ref)
+    out_ref[...] = norms_ref[...] + jnp.min(least, 0, keepdims=True)
+    half = place[2]
+    refined_ref[pl.ds(pl.multiple_of(half, HALF), HALF), :] = own[...]
+    refined_ref[pl.ds(pl.multiple_of(HALF - half, HALF), HALF), :] = other[...]
 
 
 def call(kernel, out_shape, *args, flops=0, moved=0, smem=0):
@@ -226,13 +288,6 @@
     return lax.ppermute(value, axis, [(0, 1), (1, 0)])
 
 
-def around_z(part):
-    return [part] + [
-        lax.ppermute(part, "zh", [(i, (i + k) % 4) for i in range(4)])
-        for k in (1, 2, 3)
-    ]
-
-
 def spot(core, a, b, zl):
     y, x = (b, a) if core == 0 else (a, b)
     return ((core * 4 + y) * 4 + x) * 2 + zl
@@ -246,9 +301,9 @@
     ]
 
 
-def eights():
+def many():
     return [
-        [spot(core, a, b, z) for b in range(4) for z in range(2)]
+        [zh * 64 + spot(core, a, b, z) for zh in range(4) for b in range(4) for z in range(2)]
         for core in range(2)
         for a in range(4)
     ]
@@ -260,10 +315,8 @@
     ).reshape(value.shape)
 
 
-def exchange_eight(value):
-    return lax.all_to_all(
-        value, ("core", "y", "x", "zl"), 0, 0, axis_index_groups=eights()
-    )
+def exchange_many(value):
+    return lax.all_to_all(value, AXES, 0, 0, axis_index_groups=many())
 
 
 def around(part, turn):
@@ -291,10 +344,16 @@
     def coded(chunks):
         return shape((chunks, CODED, 128), i16)
 
-    core = lax.axis_index("core")
+    zh, core, y, x, zl = (lax.axis_index(name) for name in AXES)
     first = core == 0
     place = jnp.stack(
-        [jnp.where(first, 8, 2), jnp.where(first, 2, 8), core * HALF]
+        [
+            jnp.where(first, 8, 2),
+            jnp.where(first, 2, 8),
+            core * HALF,
+            zh,
+            jnp.where(first, y, x) * 2 + zl,
+        ]
     ).astype(jnp.int32)
 
     labels = assignment.reshape(1, n)
@@ -321,30 +380,29 @@
         flops=2 * 1024 * n * D, moved=6 << 20, smem=1,
     )
 
+    small = shape((CHUNKS, SMALL, 128), i16)
     sums = call(
         first_sums_kernel,
-        coded(EACH),
+        small,
         exchange_four(sums),
         flops=1 << 22, moved=3 << 20,
     )
     (current,) = after(sums, (current,))
-    group, current = call(
-        second_sums_kernel,
-        (coded(1), shape((8 * HALF, D), bf16)),
-        exchange_eight(sums), *around(current, 0),
-        flops=1 << 20, moved=1 << 20,
-    )
-    (current,) = after(group, (current,))
-    groups, current = lax.optimization_barrier((around_z(group), around(current, 1)))
-    refined, code = call(
+    code, current = call(
         refine_kernel,
-        (shape((HALF, D), f32), coded(EACH)),
-        *groups,
-        flops=1 << 20, moved=1 << 20,
-    )
-
-    new = exchange_eight(code)
-
+        (small, shape((8 * HALF, D), bf16)),
+        place, exchange_many(sums), *around(current, 0),
+        flops=1 << 20, moved=2 << 20, smem=1,
+    )
+
+    code, current = lax.optimization_barrier((exchange_many(code), around(current, 1)))
+    code, refined = call(
+        repack_kernel,
+        (coded(CHUNKS), shape((HALF, D), f32)),
+        place, code,
+        flops=1 << 20, moved=3 << 20, smem=1,
+    )
+    new = exchange_four(code)
     current = list(after(refined, current))
     current_other = [swap(part, "core") for part in current]
     old_min, turned = call(
@@ -353,31 +411,22 @@
         norms, embeddings, *current, *current_other,
         flops=2 * 2048 * n * D, moved=5 << 20,
     )
-
     refined_other = swap(refined, "core")
-    refined_centers = jnp.concatenate(
-        [
-            jnp.where(first, refined, refined_other),
-            jnp.where(first, refined_other, refined),
-        ]
-    )
-
-    new, turned, refined_centers = lax.optimization_barrier(
-        (new, turned, refined_centers)
-    )
-    new = exchange_four(
-        jnp.broadcast_to(new[None], (4, *new.shape)).reshape(CHUNKS, CODED, 128)
-    )
+    new, turned, refined_other = lax.optimization_barrier((new, turned, refined_other))
     new_other = swap(new, "core")
-    least = jnp.full((8, n), jnp.inf, f32)
-    for piece, result in ((new, 8), (new_other, 1)):
-        least = call(
-            new_kernel,
-            shape((result, n), f32),
-            turned, norms, least, piece,
-            flops=4 * 1024 * n * D, moved=3 << 20,
-        )
-    return old_min.reshape(n), refined_centers, least.reshape(n)
+    least = call(
+        new_own_kernel,
+        shape((8, n), f32),
+        turned, new, jnp.full((8, n), jnp.inf, f32),
+        flops=4 * 1024 * n * D, moved=3 << 20,
+    )
+    new_min, refined_centers = call(
+        new_other_kernel,
+        (shape((1, n), f32), shape((2 * HALF, D), f32)),
+        place, turned, new_other, least, norms, refined, refined_other,
+        flops=4 * 1024 * n * D, moved=3 << 20, smem=1,
+    )
+    return old_min.reshape(n), refined_centers, new_min.reshape(n)
 
 
 def solution(mesh):

time: 110 us -> 116 us (1.055)
  blocking collectives: 34.4 us -> 17.4 us
  waiting for transfers between devices: 10.4 us -> 26.4 us
  local copies, waits for them, and re-layouts: 4.53 us -> 9.18 us
  Pallas kernels: 22.3 us -> 25.2 us
    all_to_all x2 -> x1, blocking collectives: 34.4 us -> 17.4 us  [exchange_four(): lax.all_to_all(value.reshape(4, -1, 128), ('core', 'y', 'x'), 0, 0, axis_...]
    all_to_all x2 -> x3, starting transfers between devices: 8.07 us -> 19.7 us  [the longest x2 16 us: exchange_many(): return lax.all_to_all(value, AXES, 0, 0, axis_index_groups=many())]
    ppermute x3 -> x0, starting transfers between devices: 10 us -> none  [around_z(): lax.ppermute(part, 'zh', [(i, (i + k) % 4) for i in range(4)])]
    ppermute x6, waiting for transfers between devices: 7.26 us -> 15.7 us  [around(): parts.append(lax.ppermute(part, ('core', 'y', 'x'), pairs))]
    all_to_all x2 -> x3, waiting for transfers between devices: 1.23 us -> 8.81 us  [the longest x2 8.81 us: exchange_many(): return lax.all_to_all(value, AXES, 0, 0, axis_index_groups=many())]
    unnamed x12 -> x28, local copies, waits for them, and re-layouts: 3.3 us -> 9.08 us
    ppermute x9, starting transfers between devices: 12.7 us -> 8.89 us  [swap(): return lax.ppermute(value, axis, [(0, 1), (1, 0)])]
    pallas_call x8, Pallas kernels: 22.3 us -> 25.2 us  [call(): pl.pallas_call(kernel, out_shape=out_shape, in_specs=specs, out_specs=tup...]
  transfers between devices with their start and end apart: 20 -> 18, of which waited for: 5 -> 12; matrix products, arithmetic and copies ran while one was open for 1% -> 0% of each run, Pallas kernels for 11% -> 10%
where the time goes in v2:
time: 116 us; the launch traced here: 115 us
  starting transfers between devices  35.6 us (31%)
  waiting for transfers between devices  26.4 us (23%)
  Pallas kernels  25.2 us (22%)
  blocking collectives  17.4 us (15%)
  local copies, waits for them, and re-layouts  9.18 us (8%)
    pallas_call x8, Pallas kernels, call(): pl.pallas_call(kernel, out_shape=out_shape, in_specs=specs, out_specs=tup...  25.2 us
    all_to_all x1, blocking collectives, exchange_four(): lax.all_to_all(value.reshape(4, -1, 128), ('core', 'y', 'x'), 0, 0, axis_...  17.4 us
    all_to_all x2, starting transfers between devices, exchange_many(): return lax.all_to_all(value, AXES, 0, 0, axis_index_groups=many())  16 us
    ppermute x6, waiting for transfers between devices, around(): parts.append(lax.ppermute(part, ('core', 'y', 'x'), pairs))  15.7 us
    unnamed x28, local copies, waits for them, and re-layouts  9.08 us
    ppermute x9, starting transfers between devices, swap(): return lax.ppermute(value, axis, [(0, 1), (1, 0)])  8.89 us
    all_to_all x2, waiting for transfers between devices, exchange_many(): return lax.all_to_all(value, AXES, 0, 0, axis_index_groups=many())  8.81 us
    ppermute x6, starting transfers between devices, around(): parts.append(lax.ppermute(part, ('core', 'y', 'x'), pairs))  7.04 us
  transfers between devices with their start and end apart: 18, of which 12 were waited for; matrix products, arithmetic and copies ran while one was open for 0% of the time, Pallas kernels for 10%

profile of v2, /device:TPU:1, one launch (start us, length us, event | category | flops | bytes accessed | tf_op | source)
XLA Modules:
  0.0 115.0 jit_solution(8333683781264847971)
XLA Ops:
  0.6 3.3 %collective-permute-start.1 = (bf16[1024,768]{1,0:T(8,128)(2,1)}, bf16[1024,768]{1,0:T(8,128)(2,1)S(1)}, u32[]{:S(2)}, u32[]{:S(2)}) collective-permute-start(bf16[1024,768]{1,0:T(8,128)(2,1)} %rows_ref.1), channel_id=1, source_target_pairs={{0,32},{32,0},{1,33},{33,1},{2,34},{34,2},{3,35},{35,3},{4,36},{36... | collective-permute-start | bytes 4718600 | tf_op jit(solution)/shard_map/ppermute | solution.py:288
  4.0 1.0 collective-permute-start
  5.0 1.4 %copy-done.1 = bf16[1024,768]{1,0:T(8,128)(2,1)S(1)} copy-done((bf16[1024,768]{1,0:T(8,128)(2,1)S(1)}, bf16[1024,768]{1,0:T(8,128)(2,1)}, u32[]{:S(2)}) %copy-start.1) | copy-done | bytes 1572888
  7.1 2.4 %shard_map.58.own_sums = f32[1024,768]{1,0:T(8,128)S(1)} custom-call(s32[5]{0:T(128)S(1)} %stack.23.place, s32[1,1024]{1,0:T(1,128)S(1)} %bitcast.18, bf16[1024,768]{1,0:T(8,128)(2,1)S(1)} %copy-done.1), custom_call_target="tpu_custom_call" | custom-call | flops 1610612736 | bytes 5242880 | tf_op jit(solution)/shard_map/pallas_call | solution.py:275
  9.6 3.7 %shard_map.59 = s16[32,208,128]{2,1,0:T(8,128)(2,1)S(1)} custom-call(s32[5]{0:T(128)S(1)} %stack.23.place, s32[1,1024]{1,0:T(1,128)S(1)} %bitcast.19, s32[1,1024]{1,0:T(1,128)S(1)} %collective-permute-done.labels, f32[1024,768]{1,0:T(8,128)S(1)} %shard_map.58.own_sums, bf16[1024,768]{1,0:T(8,128)(2,1)S(1)} %collective-permute-done.1.rows), custom_call_target="tpu_custom_call" | custom-call | flops 1610612736 | bytes 6291456 | tf_op jit(solution)/shard_map/pallas_call | solution.py:275
  13.3 17.4 %all_to_all.20 = s16[4,1664,128]{2,1,0:T(8,128)(2,1)S(1)} all-to-all(s16[4,1664,128]{2,1,0:T(8,128)(2,1)S(1)} %bitcast.13), channel_id=1, replica_groups={{0,2,4,6},{8,10,12,14},{16,18,20,22},{24,26,28,30},{32,40,48,56},{34,42..., dimensions={0} | all-to-all | bytes 3407872 | tf_op jit(solution)/shard_map/all_to_all | solution.py:313
  30.7 1.6 %shard_map.60 = s16[32,64,128]{2,1,0:T(8,128)(2,1)} custom-call(s16[32,208,128]{2,1,0:T(8,128)(2,1)S(1)} %bitcast.14), custom_call_target="tpu_custom_call" | custom-call | flops 4194304 | bytes 3145728 | tf_op jit(solution)/shard_map/pallas_call | solution.py:275
  32.3 10.0 %all-to-all-start.1 = ((s16[32,64,128]{2,1,0:T(8,128)(2,1)}), s16[32,64,128]{2,1,0:T(8,128)(2,1)S(1)}, u32[]{:S(2)}, u32[]{:S(2)}) async-start(s16[32,64,128]{2,1,0:T(8,128)(2,1)} %shard_map.60), calls=%async_computation.1 | async-start | bytes 1048576 | tf_op jit(solution)/shard_map/all_to_all | solution.py:319
  42.6 2.4 %collective-permute-start.4 = (bf16[64,768]{1,0:T(8,128)(2,1)S(1)}, bf16[64,768]{1,0:T(8,128)(2,1)S(1)}, u32[]{:S(2)}, u32[]{:S(2)}) collective-permute-start(bf16[64,768]{1,0:T(8,128)(2,1)S(1)} %pad_maximum_fusion.c0), channel_id=1, source_target_pairs={{0,6},{8,14},{16,22},{24,30},{2,0},{10,8},{18,16},{26,24},{4,2},{1... | collective-permute-start | bytes 294920 | tf_op jit(solution)/shard_map/ppermute | solution.py:331
  45.0 2.0 %collective-permute-done.3.c1 = bf16[64,768]{1,0:T(8,128)(2,1)S(1)} collective-permute-done((bf16[64,768]{1,0:T(8,128)(2,1)S(1)}, bf16[64,768]{1,0:T(8,128)(2,1)S(1)}, u32[]{:S(2)}, u32[]{:S(2)}) %collective-permute-start.3) | collective-permute-done | bytes 98336 | tf_op jit(solution)/shard_map/ppermute | solution.py:331
  47.8 2.2 %collective-permute-done.5.c3 = bf16[64,768]{1,0:T(8,128)(2,1)S(1)} collective-permute-done((bf16[64,768]{1,0:T(8,128)(2,1)S(1)}, bf16[64,768]{1,0:T(8,128)(2,1)S(1)}, u32[]{:S(2)}, u32[]{:S(2)}) %collective-permute-start.5) | collective-permute-done | bytes 98336 | tf_op jit(solution)/shard_map/ppermute | solution.py:331
  50.0 8.3 %all-to-all-done.1.in_ref = s16[32,64,128]{2,1,0:T(8,128)(2,1)S(1)} async-done(((s16[32,64,128]{2,1,0:T(8,128)(2,1)}), s16[32,64,128]{2,1,0:T(8,128)(2,1)S(1)}, u32[]{:S(2)}, u32[]{:S(2)}) %all-to-all-start.1) | async-done | bytes 524320 | tf_op jit(solution)/shard_map/all_to_all | solution.py:319
  58.3 1.7 %shard_map.61 = (s16[32,64,128]{2,1,0:T(8,128)(2,1)}, bf16[256,768]{1,0:T(8,128)(2,1)S(1)}) custom-call(s32[5]{0:T(128)S(1)} %stack.23.place, s16[32,64,128]{2,1,0:T(8,128)(2,1)S(1)} %all-to-all-done.1.in_ref, bf16[64,768]{1,0:T(8,128)(2,1)S(1)} %pad_maximum_fusion.c0, bf16[64,768]{1,0:T(8,128)(2,1)S(1)} %collective-permute-done.3.c1, ...), custom_call_target="tpu_custom_call" | custom-call | flops 1048576 | bytes 2097152 | tf_op jit(solution)/shard_map/pallas_call | solution.py:275
  60.0 6.0 %all-to-all-start.2 = ((s16[32,64,128]{2,1,0:T(8,128)(2,1)}), s16[32,64,128]{2,1,0:T(8,128)(2,1)S(1)}, u32[]{:S(2)}, u32[]{:S(2)}) async-start(s16[32,64,128]{2,1,0:T(8,128)(2,1)} %get-tuple-element.29), calls=%async_computation.2 | async-start | bytes 1048576 | tf_op jit(solution)/shard_map/all_to_all | solution.py:319
  66.0 1.3 %collective-permute-start.6 = (bf16[256,768]{1,0:T(8,128)(2,1)S(1)}, bf16[256,768]{1,0:T(8,128)(2,1)S(1)}, u32[]{:S(2)}, u32[]{:S(2)}) collective-permute-start(bf16[256,768]{1,0:T(8,128)(2,1)S(1)} %get-tuple-element.37.refs_0_), channel_id=1, source_target_pairs={{0,8},{8,16},{16,24},{24,0},{2,10},{10,18},{18,26},{26,2},{4,12},{... | collective-permute-start | bytes 1179656 | tf_op jit(solution)/shard_map/ppermute | solution.py:331
  67.3 1.4 %collective-permute-start.7 = (bf16[256,768]{1,0:T(8,128)(2,1)S(1)}, bf16[256,768]{1,0:T(8,128)(2,1)S(1)}, u32[]{:S(2)}, u32[]{:S(2)}) collective-permute-start(bf16[256,768]{1,0:T(8,128)(2,1)S(1)} %get-tuple-element.37.refs_0_), channel_id=1, source_target_pairs={{0,24},{8,0},{16,8},{24,16},{2,26},{10,2},{18,10},{26,18},{4,28},{... | collective-permute-start | bytes 1179656 | tf_op jit(solution)/shard_map/ppermute | solution.py:331
  68.8 1.5 %collective-permute-start.8 = (bf16[256,768]{1,0:T(8,128)(2,1)S(1)}, bf16[256,768]{1,0:T(8,128)(2,1)}, u32[]{:S(2)}, u32[]{:S(2)}) collective-permute-start(bf16[256,768]{1,0:T(8,128)(2,1)S(1)} %get-tuple-element.37.refs_0_), channel_id=1, source_target_pairs={{0,16},{8,24},{16,0},{24,8},{2,18},{10,26},{18,2},{26,10},{4,20},{... | collective-permute-start | bytes 1179656 | tf_op jit(solution)/shard_map/ppermute | solution.py:331
  70.3 5.7 %collective-permute-done.6.refs_1_ = bf16[256,768]{1,0:T(8,128)(2,1)S(1)} collective-permute-done((bf16[256,768]{1,0:T(8,128)(2,1)S(1)}, bf16[256,768]{1,0:T(8,128)(2,1)S(1)}, u32[]{:S(2)}, u32[]{:S(2)}) %collective-permute-start.6) | collective-permute-done | bytes 393248 | tf_op jit(solution)/shard_map/ppermute | solution.py:331
  76.0 4.2 %collective-permute-done.7.refs_2_ = bf16[256,768]{1,0:T(8,128)(2,1)S(1)} collective-permute-done((bf16[256,768]{1,0:T(8,128)(2,1)S(1)}, bf16[256,768]{1,0:T(8,128)(2,1)S(1)}, u32[]{:S(2)}, u32[]{:S(2)}) %collective-permute-start.7) | collective-permute-done | bytes 393248 | tf_op jit(solution)/shard_map/ppermute | solution.py:331
  80.9 0.9 collective-permute-done.8.refs_3_
  82.3 2.0 %shard_map.62 = (s16[32,208,128]{2,1,0:T(8,128)(2,1)}, f32[32,768]{1,0:T(8,128)S(1)}) custom-call(s32[5]{0:T(128)S(1)} %stack.23.place, s16[32,64,128]{2,1,0:T(8,128)(2,1)S(1)} %all-to-all-done.2.in_ref), custom_call_target="tpu_custom_call" | custom-call | flops 1048576 | bytes 3145728 | tf_op jit(solution)/shard_map/pallas_call | solution.py:275
  84.3 3.7 %all-to-all-start.3 = ((s16[4,1664,128]{2,1,0:T(8,128)(2,1)}), s16[4,1664,128]{2,1,0:T(8,128)(2,1)S(1)}, u32[]{:S(2)}, u32[]{:S(2)}) async-start(s16[4,1664,128]{2,1,0:T(8,128)(2,1)} %bitcast.10), calls=%async_computation.3 | async-start | bytes 3407872 | tf_op jit(solution)/shard_map/all_to_all | solution.py:313
  88.0 2.5 %collective-permute-start.10 = (bf16[256,768]{1,0:T(8,128)(2,1)}, bf16[256,768]{1,0:T(8,128)(2,1)S(1)}, u32[]{:S(2)}, u32[]{:S(2)}) collective-permute-start(bf16[256,768]{1,0:T(8,128)(2,1)} %copy-done.6), channel_id=1, source_target_pairs={{0,32},{32,0},{1,33},{33,1},{2,34},{34,2},{3,35},{35,3},{4,36},{36... | collective-permute-start | bytes 1179656 | tf_op jit(solution)/shard_map/ppermute | solution.py:288
  93.9 1.0 copy-done.5
  94.9 1.0 copy-done.7
  95.9 1.0 copy-done.9
  96.9 5.2 %shard_map.63 = (f32[1,1024]{1,0:T(1,128)}, bf16[768,1024]{1,0:T(8,128)(2,1)S(1)}) custom-call(f32[1,1024]{1,0:T(1,128)S(1)} %bitcast.20, bf16[1024,768]{1,0:T(8,128)(2,1)S(1)} %copy-done.2, bf16[256,768]{1,0:T(8,128)(2,1)S(1)} %copy-done.5, bf16[256,768]{1,0:T(8,128)(2,1)S(1)} %copy-done.7, bf16[256,768]{1,0:T(8,128)(2,1)S(1)} %copy-done.9, ...), custom_call_target="tpu_custom_call" | custom-call | flops 3221225472 | bytes 5242880 | tf_op jit(solution)/shard_map/pallas_call | solution.py:275
  102.1 1.2 %copy-done.12 = bf16[768,1024]{1,0:T(8,128)(2,1)} copy-done((bf16[768,1024]{1,0:T(8,128)(2,1)}, bf16[768,1024]{1,0:T(8,128)(2,1)S(1)}, u32[]{:S(2)}) %copy-start.12) | copy-done | bytes 1572888
  103.9 1.0 collective-permute-start.14
  104.9 1.4 %copy-done.13 = bf16[768,1024]{1,0:T(8,128)(2,1)S(1)} copy-done((bf16[768,1024]{1,0:T(8,128)(2,1)S(1)}, bf16[768,1024]{1,0:T(8,128)(2,1)}, u32[]{:S(2)}) %copy-start.13) | copy-done | bytes 1572888
  106.3 3.7 %shard_map.64.least_ref = f32[8,1024]{1,0:T(8,128)S(1)} custom-call(bf16[768,1024]{1,0:T(8,128)(2,1)S(1)} %copy-done.13, s16[32,208,128]{2,1,0:T(8,128)(2,1)S(1)} %bitcast.16, f32[8,1024]{1,0:T(8,128)S(1)} %broadcast_in_dim.3.least_ref), custom_call_target="tpu_custom_call" | custom-call | flops 3221225472 | bytes 3145728 | tf_op jit(solution)/shard_map/pallas_call | solution.py:275
  110.1 4.9 %shard_map.65 = (f32[1,1024]{1,0:T(1,128)}, f32[64,768]{1,0:T(8,128)}) custom-call(s32[5]{0:T(128)S(1)} %stack.23.place, bf16[768,1024]{1,0:T(8,128)(2,1)S(1)} %copy-done.13, s16[32,208,128]{2,1,0:T(8,128)(2,1)S(1)} %collective-permute-done.14.piece, f32[8,1024]{1,0:T(8,128)S(1)} %shard_map.64.least_ref, f32[1,1024]{1,0:T(1,128)S(1)} %bitcast.21, ...), custom_call_target="tpu_custom_call" | custom-call | flops 3221225472 | bytes 3145728 | tf_op jit(solution)/shard_map/pallas_call | solution.py:275
  (46 shorter events, 7.3 us)
Async XLA Ops:
  0.6 3.3 %copy-start = (bf16[64,768]{1,0:T(8,128)(2,1)S(1)}, bf16[64,768]{1,0:T(8,128)(2,1)}, u32[]{:S(2)}) copy-start(bf16[64,768]{1,0:T(8,128)(2,1)} %param.4) | copy-start | bytes 294916
  0.6 8.9 %collective-permute-start.1 = (bf16[1024,768]{1,0:T(8,128)(2,1)}, bf16[1024,768]{1,0:T(8,128)(2,1)S(1)}, u32[]{:S(2)}, u32[]{:S(2)}) collective-permute-start(bf16[1024,768]{1,0:T(8,128)(2,1)} %rows_ref.1), channel_id=1, source_target_pairs={{0,32},{32,0},{1,33},{33,1},{2,34},{34,2},{3,35},{35,3},{4,36},{36... | collective-permute-start | bytes 4718600 | tf_op jit(solution)/shard_map/ppermute | solution.py:288
  4.0 5.6 %collective-permute-start.2 = (bf16[32,768]{1,0:T(8,128)(2,1)S(1)}, bf16[32,768]{1,0:T(8,128)(2,1)S(1)}, u32[]{:S(2)}, u32[]{:S(2)}) collective-permute-start(bf16[32,768]{1,0:T(8,128)(2,1)S(1)} %constant_dynamic-slice_fusion), channel_id=1, source_target_pairs={{0,1},{1,0},{2,3},{3,2},{4,5},{5,4},{6,7},{7,6},{8,9},{9,8},{10,11... | collective-permute-start | bytes 147464 | tf_op jit(solution)/shard_map/ppermute | solution.py:288
  4.0 5.6 %collective-permute-start = (s32[1,1024]{1,0:T(1,128)}, s32[1,1024]{1,0:T(1,128)S(1)}, u32[]{:S(2)}, u32[]{:S(2)}) collective-permute-start(s32[1,1024]{1,0:T(1,128)} %bitcast.17), channel_id=1, source_target_pairs={{0,32},{32,0},{1,33},{33,1},{2,34},{34,2},{3,35},{35,3},{4,36},{36... | collective-permute-start | bytes 12296 | tf_op jit(solution)/shard_map/ppermute | solution.py:288
  5.0 1.4 %copy-start.1 = (bf16[1024,768]{1,0:T(8,128)(2,1)S(1)}, bf16[1024,768]{1,0:T(8,128)(2,1)}, u32[]{:S(2)}) copy-start(bf16[1024,768]{1,0:T(8,128)(2,1)} %rows_ref.1) | copy-start | bytes 4718596
  6.5 0.7 copy-start.3
  32.3 26.1 %all-to-all-start.1 = ((s16[32,64,128]{2,1,0:T(8,128)(2,1)}), s16[32,64,128]{2,1,0:T(8,128)(2,1)S(1)}, u32[]{:S(2)}, u32[]{:S(2)}) async-start(s16[32,64,128]{2,1,0:T(8,128)(2,1)} %shard_map.60), calls=%async_computation.1 | async-start | bytes 1048576 | tf_op jit(solution)/shard_map/all_to_all | solution.py:319
  42.3 4.8 %collective-permute-start.3 = (bf16[64,768]{1,0:T(8,128)(2,1)S(1)}, bf16[64,768]{1,0:T(8,128)(2,1)S(1)}, u32[]{:S(2)}, u32[]{:S(2)}) collective-permute-start(bf16[64,768]{1,0:T(8,128)(2,1)S(1)} %pad_maximum_fusion.c0), channel_id=1, source_target_pairs={{0,2},{8,10},{16,18},{24,26},{2,4},{10,12},{18,20},{26,28},{4,6},{... | collective-permute-start | bytes 294920 | tf_op jit(solution)/shard_map/ppermute | solution.py:331
  42.6 5.2 %collective-permute-start.4 = (bf16[64,768]{1,0:T(8,128)(2,1)S(1)}, bf16[64,768]{1,0:T(8,128)(2,1)S(1)}, u32[]{:S(2)}, u32[]{:S(2)}) collective-permute-start(bf16[64,768]{1,0:T(8,128)(2,1)S(1)} %pad_maximum_fusion.c0), channel_id=1, source_target_pairs={{0,6},{8,14},{16,22},{24,30},{2,0},{10,8},{18,16},{26,24},{4,2},{1... | collective-permute-start | bytes 294920 | tf_op jit(solution)/shard_map/ppermute | solution.py:331
  45.0 5.0 %collective-permute-start.5 = (bf16[64,768]{1,0:T(8,128)(2,1)S(1)}, bf16[64,768]{1,0:T(8,128)(2,1)S(1)}, u32[]{:S(2)}, u32[]{:S(2)}) collective-permute-start(bf16[64,768]{1,0:T(8,128)(2,1)S(1)} %pad_maximum_fusion.c0), channel_id=1, source_target_pairs={{0,4},{8,12},{16,20},{24,28},{2,6},{10,14},{18,22},{26,30},{4,0},{... | collective-permute-start | bytes 294920 | tf_op jit(solution)/shard_map/ppermute | solution.py:331
  60.0 24.3 %copy-start.4 = (bf16[256,768]{1,0:T(8,128)(2,1)}, bf16[256,768]{1,0:T(8,128)(2,1)S(1)}, u32[]{:S(2)}) copy-start(bf16[256,768]{1,0:T(8,128)(2,1)S(1)} %get-tuple-element.37.refs_0_) | copy-start | bytes 1179652
  60.0 22.3 %all-to-all-start.2 = ((s16[32,64,128]{2,1,0:T(8,128)(2,1)}), s16[32,64,128]{2,1,0:T(8,128)(2,1)S(1)}, u32[]{:S(2)}, u32[]{:S(2)}) async-start(s16[32,64,128]{2,1,0:T(8,128)(2,1)} %get-tuple-element.29), calls=%async_computation.2 | async-start | bytes 1048576 | tf_op jit(solution)/shard_map/all_to_all | solution.py:319
  66.0 9.9 %collective-permute-start.6 = (bf16[256,768]{1,0:T(8,128)(2,1)S(1)}, bf16[256,768]{1,0:T(8,128)(2,1)S(1)}, u32[]{:S(2)}, u32[]{:S(2)}) collective-permute-start(bf16[256,768]{1,0:T(8,128)(2,1)S(1)} %get-tuple-element.37.refs_0_), channel_id=1, source_target_pairs={{0,8},{8,16},{16,24},{24,0},{2,10},{10,18},{18,26},{26,2},{4,12},{... | collective-permute-start | bytes 1179656 | tf_op jit(solution)/shard_map/ppermute | solution.py:331
  67.3 12.8 %collective-permute-start.7 = (bf16[256,768]{1,0:T(8,128)(2,1)S(1)}, bf16[256,768]{1,0:T(8,128)(2,1)S(1)}, u32[]{:S(2)}, u32[]{:S(2)}) collective-permute-start(bf16[256,768]{1,0:T(8,128)(2,1)S(1)} %get-tuple-element.37.refs_0_), channel_id=1, source_target_pairs={{0,24},{8,0},{16,8},{24,16},{2,26},{10,2},{18,10},{26,18},{4,28},{... | collective-permute-start | bytes 1179656 | tf_op jit(solution)/shard_map/ppermute | solution.py:331
  68.8 13.0 %collective-permute-start.8 = (bf16[256,768]{1,0:T(8,128)(2,1)S(1)}, bf16[256,768]{1,0:T(8,128)(2,1)}, u32[]{:S(2)}, u32[]{:S(2)}) collective-permute-start(bf16[256,768]{1,0:T(8,128)(2,1)S(1)} %get-tuple-element.37.refs_0_), channel_id=1, source_target_pairs={{0,16},{8,24},{16,0},{24,8},{2,18},{10,26},{18,2},{26,10},{4,20},{... | collective-permute-start | bytes 1179656 | tf_op jit(solution)/shard_map/ppermute | solution.py:331
  76.0 4.2 %copy-start.6 = (bf16[256,768]{1,0:T(8,128)(2,1)}, bf16[256,768]{1,0:T(8,128)(2,1)S(1)}, u32[]{:S(2)}) copy-start(bf16[256,768]{1,0:T(8,128)(2,1)S(1)} %collective-permute-done.6.refs_1_) | copy-start | bytes 1179652
  80.2 0.8 copy-start.8
  84.3 6.7 %copy-start.2 = (bf16[1024,768]{1,0:T(8,128)(2,1)S(1)}, bf16[1024,768]{1,0:T(8,128)(2,1)}, u32[]{:S(2)}) copy-start(bf16[1024,768]{1,0:T(8,128)(2,1)} %rows_ref.1) | copy-start | bytes 4718596
  84.3 19.7 %all-to-all-start.3 = ((s16[4,1664,128]{2,1,0:T(8,128)(2,1)}), s16[4,1664,128]{2,1,0:T(8,128)(2,1)S(1)}, u32[]{:S(2)}, u32[]{:S(2)}) async-start(s16[4,1664,128]{2,1,0:T(8,128)(2,1)} %bitcast.10), calls=%async_computation.3 | async-start | bytes 3407872 | tf_op jit(solution)/shard_map/all_to_all | solution.py:313
  88.0 4.1 %collective-permute-start.10 = (bf16[256,768]{1,0:T(8,128)(2,1)}, bf16[256,768]{1,0:T(8,128)(2,1)S(1)}, u32[]{:S(2)}, u32[]{:S(2)}) collective-permute-start(bf16[256,768]{1,0:T(8,128)(2,1)} %copy-done.6), channel_id=1, source_target_pairs={{0,32},{32,0},{1,33},{33,1},{2,34},{34,2},{3,35},{35,3},{4,36},{36... | collective-permute-start | bytes 1179656 | tf_op jit(solution)/shard_map/ppermute | solution.py:288
  90.5 2.1 %collective-permute-start.11 = (bf16[256,768]{1,0:T(8,128)(2,1)}, bf16[256,768]{1,0:T(8,128)(2,1)S(1)}, u32[]{:S(2)}, u32[]{:S(2)}) collective-permute-start(bf16[256,768]{1,0:T(8,128)(2,1)} %copy-done.8), channel_id=1, source_target_pairs={{0,32},{32,0},{1,33},{33,1},{2,34},{34,2},{3,35},{35,3},{4,36},{36... | collective-permute-start | bytes 1179656 | tf_op jit(solution)/shard_map/ppermute | solution.py:288
  90.5 2.7 %collective-permute-start.12 = (bf16[256,768]{1,0:T(8,128)(2,1)}, bf16[256,768]{1,0:T(8,128)(2,1)S(1)}, u32[]{:S(2)}, u32[]{:S(2)}) collective-permute-start(bf16[256,768]{1,0:T(8,128)(2,1)} %collective-permute-done.8.refs_3_), channel_id=1, source_target_pairs={{0,32},{32,0},{1,33},{33,1},{2,34},{34,2},{3,35},{35,3},{4,36},{36... | collective-permute-start | bytes 1179656 | tf_op jit(solution)/shard_map/ppermute | solution.py:288
  91.0 2.9 %collective-permute-start.9 = (bf16[256,768]{1,0:T(8,128)(2,1)}, bf16[256,768]{1,0:T(8,128)(2,1)S(1)}, u32[]{:S(2)}, u32[]{:S(2)}) collective-permute-start(bf16[256,768]{1,0:T(8,128)(2,1)} %copy-done.4), channel_id=1, source_target_pairs={{0,32},{32,0},{1,33},{33,1},{2,34},{34,2},{3,35},{35,3},{4,36},{36... | collective-permute-start | bytes 1179656 | tf_op jit(solution)/shard_map/ppermute | solution.py:288
  91.4 11.9 %collective-permute-start.13 = (f32[32,768]{1,0:T(8,128)S(1)}, f32[32,768]{1,0:T(8,128)S(1)}, u32[]{:S(2)}, u32[]{:S(2)}) collective-permute-start(f32[32,768]{1,0:T(8,128)S(1)} %get-tuple-element.32.own), channel_id=1, source_target_pairs={{0,32},{32,0},{1,33},{33,1},{2,34},{34,2},{3,35},{35,3},{4,36},{36... | collective-permute-start | bytes 294920 | tf_op jit(solution)/shard_map/ppermute | solution.py:288
  93.9 1.0 copy-start.5
  94.9 1.0 copy-start.7
  95.9 1.0 copy-start.9
  102.1 1.2 %copy-start.12 = (bf16[768,1024]{1,0:T(8,128)(2,1)}, bf16[768,1024]{1,0:T(8,128)(2,1)S(1)}, u32[]{:S(2)}) copy-start(bf16[768,1024]{1,0:T(8,128)(2,1)S(1)} %get-tuple-element.44.turned_ref) | copy-start | bytes 4718596
  103.3 0.6 copy-start.10
  103.9 6.1 %collective-permute-start.14 = (s16[32,208,128]{2,1,0:T(8,128)(2,1)S(1)}, s16[32,208,128]{2,1,0:T(8,128)(2,1)S(1)}, u32[]{:S(2)}, u32[]{:S(2)}) collective-permute-start(s16[32,208,128]{2,1,0:T(8,128)(2,1)S(1)} %bitcast.15), channel_id=1, source_target_pairs={{0,32},{32,0},{1,33},{33,1},{2,34},{34,2},{3,35},{35,3},{4,36},{36... | collective-permute-start | bytes 5111816 | tf_op jit(solution)/shard_map/ppermute | solution.py:288
  104.9 1.4 %copy-start.13 = (bf16[768,1024]{1,0:T(8,128)(2,1)S(1)}, bf16[768,1024]{1,0:T(8,128)(2,1)}, u32[]{:S(2)}) copy-start(bf16[768,1024]{1,0:T(8,128)(2,1)} %copy-done.12) | copy-start | bytes 4718596
  106.3 3.7 %copy-start.11 = (f32[32,768]{1,0:T(8,128)S(1)}, f32[32,768]{1,0:T(8,128)}, u32[]{:S(2)}) copy-start(f32[32,768]{1,0:T(8,128)} %copy-done.10) | copy-start | bytes 294916

commit v3 on v1

--- a/solution.py
+++ b/solution.py
@@ -59,10 +59,14 @@
 
 def is_named(t, place, labels):
     first, second, half = (place[i] for i in range(3))
-    j = lax.broadcasted_iota(jnp.int32, (TILE, 1), 0)
-    c = j // HALF
-    shard = (c // 2) * first + t * second + c % 2
-    k = shard * (2 * HALF) + half + j % HALF
+    within = lax.broadcasted_iota(jnp.int32, (HALF, 1), 0) + half
+    k = jnp.concatenate(
+        [
+            within + ((c // 2) * first + t * second + c % 2) * (2 * HALF)
+            for c in range(EACH)
+        ],
+        0,
+    )
     return jnp.where(k == labels, 1.0, 0.0)
 
 
@@ -162,9 +166,18 @@
     return jnp.minimum(least, jnp.min(value.reshape(n // 8, 8, value.shape[1]), 0))
 
 
-def old_kernel(norms_ref, rows_ref, *refs):
-    *centers, out_ref, turned_ref = refs
+def turn_kernel(rows_ref, turned_ref, norms_ref):
     turned_ref[...] = (rows_ref[...] * jnp.bfloat16(-2.0)).T
+    total = jnp.zeros((8, turned_ref.shape[1]), jnp.float32)
+    for i in range(D // 16):
+        wide = turned_ref[i * 16 : (i + 1) * 16, :].astype(jnp.float32)
+        wide = wide * wide
+        total = total + (wide[:8] + wide[8:])
+    norms_ref[...] = jnp.sum(total, 0, keepdims=True) * 0.25
+
+
+def old_kernel(norms_ref, turned_ref, *refs):
+    *centers, out_ref = refs
     turned = turned_ref[...]
     least = jnp.full((8, turned.shape[1]), jnp.inf, jnp.float32)
     for ref in centers:
@@ -175,20 +188,19 @@
     out_ref[...] = norms_ref[...] + jnp.min(least, 0, keepdims=True)
 
 
-def new_kernel(turned_ref, norms_ref, least_ref, *refs):
-    *pieces, out_ref = refs
+def new_min(turned_ref, piece, least_ref):
     turned = turned_ref[...]
     least = least_ref[...]
-    for ref, t in [(ref, t) for ref in pieces for t in range(CHUNKS // EACH)]:
+    for t in range(CHUNKS // EACH):
         high, low, scale, norm = [], [], [], []
         for c in range(t * EACH, (t + 1) * EACH):
             wide = jnp.concatenate(
-                [ref[c, block(b), :].astype(jnp.float32) for b in range(COLS)], 1
+                [piece[c, block(b), :].astype(jnp.float32) for b in range(COLS)], 1
             )
             top = wide.astype(jnp.bfloat16)
             high.append(top)
             low.append((wide - top.astype(jnp.float32)).astype(jnp.bfloat16))
-            foot = ref[c, BODY:CODED, :].astype(jnp.float32)
+            foot = piece[c, BODY:CODED, :].astype(jnp.float32)
             s = scale_of(to_column(foot[1:2, :]))
             scale.append(s)
             norm.append(jnp.sum(wide * wide, 1, keepdims=True) * (s * s))
@@ -197,10 +209,21 @@
         ) + jnp.dot(jnp.concatenate(low, 0), turned, preferred_element_type=jnp.float32)
         value = product * jnp.concatenate(scale, 0) + jnp.concatenate(norm, 0)
         least = nearest(value, least)
-    if out_ref.shape == least.shape:
-        out_ref[...] = least
-    else:
-        out_ref[...] = norms_ref[...] + jnp.min(least, 0, keepdims=True)
+    return least
+
+
+def new_own_kernel(turned_ref, piece, least_ref, out_ref):
+    out_ref[...] = new_min(turned_ref, piece, least_ref)
+
+
+def new_other_kernel(
+    place, turned_ref, piece, least_ref, norms_ref, own, other, out_ref, refined_ref
+):
+    least = new_min(turned_ref, piece, least_ref)
+    out_ref[...] = norms_ref[...] + jnp.min(least, 0, keepdims=True)
+    half = place[2]
+    refined_ref[pl.ds(pl.multiple_of(half, HALF), HALF), :] = own[...]
+    refined_ref[pl.ds(pl.multiple_of(HALF - half, HALF), HALF), :] = other[...]
 
 
 def call(kernel, out_shape, *args, flops=0, moved=0, smem=0):
@@ -305,9 +328,6 @@
     current = jnp.concatenate([mine, swap(mine, "zl")])
     (other_rows, current) = lax.optimization_barrier((other_rows, current))
 
-    wide = embeddings.astype(f32)
-    norms = jnp.sum(wide * wide, 1).reshape(1, n)
-
     sums = call(
         own_sums_kernel,
         shape((4 * TILE, D), f32),
@@ -327,11 +347,18 @@
         exchange_four(sums),
         flops=1 << 22, moved=3 << 20,
     )
-    (current,) = after(sums, (current,))
+    current, rows = after(sums, (current, embeddings))
+    turned, norms = call(
+        turn_kernel,
+        (shape((D, n), bf16), shape((1, n), f32)),
+        rows,
+        flops=4 * n * D, moved=4 << 20,
+    )
+    sums, turned = lax.optimization_barrier((exchange_eight(sums), turned))
     group, current = call(
         second_sums_kernel,
         (coded(1), shape((8 * HALF, D), bf16)),
-        exchange_eight(sums), *around(current, 0),
+        sums, *around(current, 0),
         flops=1 << 20, moved=1 << 20,
     )
     (current,) = after(group, (current,))
@@ -347,37 +374,31 @@
 
     current = list(after(refined, current))
     current_other = [swap(part, "core") for part in current]
-    old_min, turned = call(
+    old_min = call(
         old_kernel,
-        (shape((1, n), f32), shape((D, n), bf16)),
-        norms, embeddings, *current, *current_other,
+        shape((1, n), f32),
+        norms, turned, *current, *current_other,
         flops=2 * 2048 * n * D, moved=5 << 20,
     )
-
     refined_other = swap(refined, "core")
-    refined_centers = jnp.concatenate(
-        [
-            jnp.where(first, refined, refined_other),
-            jnp.where(first, refined_other, refined),
-        ]
-    )
-
-    new, turned, refined_centers = lax.optimization_barrier(
-        (new, turned, refined_centers)
-    )
+    new, old_min, refined_other = lax.optimization_barrier((new, old_min, refined_other))
     new = exchange_four(
         jnp.broadcast_to(new[None], (4, *new.shape)).reshape(CHUNKS, CODED, 128)
     )
     new_other = swap(new, "core")
-    least = jnp.full((8, n), jnp.inf, f32)
-    for piece, result in ((new, 8), (new_other, 1)):
-        least = call(
-            new_kernel,
-            shape((result, n), f32),
-            turned, norms, least, piece,
-            flops=4 * 1024 * n * D, moved=3 << 20,
-        )
-    return old_min.reshape(n), refined_centers, least.reshape(n)
+    least = call(
+        new_own_kernel,
+        shape((8, n), f32),
+        turned, new, jnp.full((8, n), jnp.inf, f32),
+        flops=4 * 1024 * n * D, moved=3 << 20,
+    )
+    new_min, refined_centers = call(
+        new_other_kernel,
+        (shape((1, n), f32), shape((2 * HALF, D), f32)),
+        place, turned, new_other, least, norms, refined, refined_other,
+        flops=4 * 1024 * n * D, moved=3 << 20, smem=1,
+    )
+    return old_min.reshape(n), refined_centers, new_min.reshape(n)
 
 
 def solution(mesh):

time: 110 us -> 108 us (0.982)
  waiting for transfers between devices: 10.4 us -> 9.25 us
    ppermute x6, waiting for transfers between devices: 7.26 us -> 0.95 us  [around(): parts.append(lax.ppermute(part, ('core', 'y', 'x'), pairs))]
    all_to_all x2, waiting for transfers between devices: 1.23 us -> 4.48 us  [exchange_eight(): lax.all_to_all(value, ('core', 'y', 'x', 'zl'), 0, 0, axis_index_groups=e...]
    ppermute x9, waiting for transfers between devices: 0.02 us -> 2.03 us  [swap(): return lax.ppermute(value, axis, [(0, 1), (1, 0)])]
    all_to_all x2, starting transfers between devices: 8.07 us -> 9.78 us  [exchange_eight(): lax.all_to_all(value, ('core', 'y', 'x', 'zl'), 0, 0, axis_index_groups=e...]
    ppermute x9, starting transfers between devices: 12.7 us -> 11.1 us  [swap(): return lax.ppermute(value, axis, [(0, 1), (1, 0)])]
    pallas_call x8 -> x9, Pallas kernels: 22.3 us -> 22 us  [call(): pl.pallas_call(kernel, out_shape=out_shape, in_specs=specs, out_specs=tup...]
    unnamed x12 -> x14, local copies, waits for them, and re-layouts: 3.3 us -> 3.3 us
  transfers between devices with their start and end apart: 20 -> 20, of which waited for: 5 -> 7; matrix products, arithmetic and copies ran while one was open for 1% -> 0% of each run, Pallas kernels for 11% -> 10%
where the time goes in v3:
time: 108 us
  starting transfers between devices  35.8 us (33%)
  blocking collectives  35.1 us (32%)
  Pallas kernels  22 us (20%)
  waiting for transfers between devices  9.25 us (9%)
  local copies, waits for them, and re-layouts  4.54 us (4%)
    all_to_all x2, blocking collectives, exchange_four(): lax.all_to_all(value.reshape(4, -1, 128), ('core', 'y', 'x'), 0, 0, axis_...  35.1 us
    pallas_call x9, Pallas kernels, call(): pl.pallas_call(kernel, out_shape=out_shape, in_specs=specs, out_specs=tup...  22 us
    ppermute x9, starting transfers between devices, swap(): return lax.ppermute(value, axis, [(0, 1), (1, 0)])  11.1 us
    ppermute x3, starting transfers between devices, around_z(): lax.ppermute(part, 'zh', [(i, (i + k) % 4) for i in range(4)])  10 us
    all_to_all x2, starting transfers between devices, exchange_eight(): lax.all_to_all(value, ('core', 'y', 'x', 'zl'), 0, 0, axis_index_groups=e...  9.78 us
    ppermute x6, starting transfers between devices, around(): parts.append(lax.ppermute(part, ('core', 'y', 'x'), pairs))  4.91 us
    all_to_all x2, waiting for transfers between devices, exchange_eight(): lax.all_to_all(value, ('core', 'y', 'x', 'zl'), 0, 0, axis_index_groups=e...  4.48 us
    unnamed x14, local copies, waits for them, and re-layouts  3.3 us
  transfers between devices with their start and end apart: 20, of which 7 were waited for; matrix products, arithmetic and copies ran while one was open for 0% of the time, Pallas kernels for 10%

profile of v3, /device:TPU:1, one launch (start us, length us, event | category | flops | bytes accessed | tf_op | source)
XLA Modules:
  0.0 107.6 jit_solution(10631557394591025856)
XLA Ops:
  0.6 3.3 %collective-permute-start.1 = (bf16[1024,768]{1,0:T(8,128)(2,1)}, bf16[1024,768]{1,0:T(8,128)(2,1)S(1)}, u32[]{:S(2)}, u32[]{:S(2)}) collective-permute-start(bf16[1024,768]{1,0:T(8,128)(2,1)} %rows_ref), channel_id=1, source_target_pairs={{0,32},{32,0},{1,33},{33,1},{2,34},{34,2},{3,35},{35,3},{4,36},{36... | collective-permute-start | bytes 4718600 | tf_op jit(solution)/shard_map/ppermute | solution.py:249
  4.0 1.0 collective-permute-start
  5.0 1.4 %copy-done.1 = bf16[1024,768]{1,0:T(8,128)(2,1)S(1)} copy-done((bf16[1024,768]{1,0:T(8,128)(2,1)S(1)}, bf16[1024,768]{1,0:T(8,128)(2,1)}, u32[]{:S(2)}) %copy-start.1) | copy-done | bytes 1572888
  6.4 0.7 copy-done.3
  7.1 2.4 %shard_map.58.own_sums = f32[1024,768]{1,0:T(8,128)S(1)} custom-call(s32[3]{0:T(128)S(1)} %pad_add_fusion.place, s32[1,1024]{1,0:T(1,128)S(1)} %bitcast.15, bf16[1024,768]{1,0:T(8,128)(2,1)S(1)} %copy-done.1), custom_call_target="tpu_custom_call" | custom-call | flops 1610612736 | bytes 5242880 | tf_op jit(solution)/shard_map/pallas_call | solution.py:236
  9.6 3.8 %shard_map.59 = s16[32,208,128]{2,1,0:T(8,128)(2,1)S(1)} custom-call(s32[3]{0:T(128)S(1)} %pad_add_fusion.place, s32[1,1024]{1,0:T(1,128)S(1)} %bitcast.16, s32[1,1024]{1,0:T(1,128)S(1)} %collective-permute-done.labels, f32[1024,768]{1,0:T(8,128)S(1)} %shard_map.58.own_sums, bf16[1024,768]{1,0:T(8,128)(2,1)S(1)} %collective-permute-done.1.rows), custom_call_target="tpu_custom_call" | custom-call | flops 1610612736 | bytes 6291456 | tf_op jit(solution)/shard_map/pallas_call | solution.py:236
  13.3 17.4 %all_to_all.20 = s16[4,1664,128]{2,1,0:T(8,128)(2,1)S(1)} all-to-all(s16[4,1664,128]{2,1,0:T(8,128)(2,1)S(1)} %bitcast.10), channel_id=1, replica_groups={{0,2,4,6},{8,10,12,14},{16,18,20,22},{24,26,28,30},{32,40,48,56},{34,42..., dimensions={0} | all-to-all | bytes 3407872 | tf_op jit(solution)/shard_map/all_to_all | solution.py:281
  30.7 1.6 %shard_map.60 = s16[8,208,128]{2,1,0:T(8,128)(2,1)} custom-call(s16[32,208,128]{2,1,0:T(8,128)(2,1)S(1)} %bitcast.11), custom_call_target="tpu_custom_call" | custom-call | flops 4194304 | bytes 3145728 | tf_op jit(solution)/shard_map/pallas_call | solution.py:236
  32.3 3.9 %all-to-all-start.1 = ((s16[8,208,128]{2,1,0:T(8,128)(2,1)}), s16[8,208,128]{2,1,0:T(8,128)(2,1)S(1)}, u32[]{:S(2)}, u32[]{:S(2)}) async-start(s16[8,208,128]{2,1,0:T(8,128)(2,1)} %shard_map.60), calls=%async_computation.1 | async-start | bytes 851968 | tf_op jit(solution)/shard_map/all_to_all | solution.py:287
  36.5 2.4 %collective-permute-start.4 = (bf16[64,768]{1,0:T(8,128)(2,1)S(1)}, bf16[64,768]{1,0:T(8,128)(2,1)S(1)}, u32[]{:S(2)}, u32[]{:S(2)}) collective-permute-start(bf16[64,768]{1,0:T(8,128)(2,1)S(1)} %pad_maximum_fusion.c0), channel_id=1, source_target_pairs={{0,6},{8,14},{16,22},{24,30},{2,0},{10,8},{18,16},{26,24},{4,2},{1... | collective-permute-start | bytes 294920 | tf_op jit(solution)/shard_map/ppermute | solution.py:301
  38.9 0.6 shard_map.61
  39.5 1.2 %copy-done.4 = bf16[768,1024]{1,0:T(8,128)(2,1)} copy-done((bf16[768,1024]{1,0:T(8,128)(2,1)}, bf16[768,1024]{1,0:T(8,128)(2,1)S(1)}, u32[]{:S(2)}) %copy-start.4) | copy-done | bytes 1572888
  40.7 4.5 %all-to-all-done.1.in_ref = s16[8,208,128]{2,1,0:T(8,128)(2,1)S(1)} async-done(((s16[8,208,128]{2,1,0:T(8,128)(2,1)}), s16[8,208,128]{2,1,0:T(8,128)(2,1)S(1)}, u32[]{:S(2)}, u32[]{:S(2)}) %all-to-all-start.1) | async-done | bytes 426016 | tf_op jit(solution)/shard_map/all_to_all | solution.py:287
  45.2 0.9 collective-permute-done.5.c3
  46.4 1.0 collective-permute-start.10
  47.4 1.1 %collective-permute-start.11 = (bf16[256,768]{1,0:T(8,128)(2,1)S(1)}, bf16[256,768]{1,0:T(8,128)(2,1)S(1)}, u32[]{:S(2)}, u32[]{:S(2)}) collective-permute-start(bf16[256,768]{1,0:T(8,128)(2,1)S(1)} %get-tuple-element.53.refs_0_), channel_id=1, source_target_pairs={{0,16},{8,24},{16,0},{24,8},{2,18},{10,26},{18,2},{26,10},{4,20},{... | collective-permute-start | bytes 1179656 | tf_op jit(solution)/shard_map/ppermute | solution.py:301
  48.6 3.0 %collective-permute-start.6 = (s16[1,208,128]{2,1,0:T(8,128)(2,1)S(1)}, s16[1,208,128]{2,1,0:T(8,128)(2,1)S(1)}, u32[]{:S(2)}, u32[]{:S(2)}) collective-permute-start(s16[1,208,128]{2,1,0:T(8,128)(2,1)S(1)} %get-tuple-element.41.own), channel_id=1, source_target_pairs={{0,64},{64,128},{128,192},{192,0},{1,65},{65,129},{129,193},{193,1... | collective-permute-start | bytes 159752 | tf_op jit(solution)/shard_map/ppermute | solution.py:254
  51.6 4.7 %collective-permute-start.7 = (s16[1,208,128]{2,1,0:T(8,128)(2,1)S(1)}, s16[1,208,128]{2,1,0:T(8,128)(2,1)S(1)}, u32[]{:S(2)}, u32[]{:S(2)}) collective-permute-start(s16[1,208,128]{2,1,0:T(8,128)(2,1)S(1)} %get-tuple-element.41.own), channel_id=1, source_target_pairs={{0,128},{64,192},{128,0},{192,64},{1,129},{65,193},{129,1},{193,65... | collective-permute-start | bytes 159752 | tf_op jit(solution)/shard_map/ppermute | solution.py:254
  56.3 2.4 %collective-permute-start.8 = (s16[1,208,128]{2,1,0:T(8,128)(2,1)S(1)}, s16[1,208,128]{2,1,0:T(8,128)(2,1)S(1)}, u32[]{:S(2)}, u32[]{:S(2)}) collective-permute-start(s16[1,208,128]{2,1,0:T(8,128)(2,1)S(1)} %get-tuple-element.41.own), channel_id=1, source_target_pairs={{0,192},{64,0},{128,64},{192,128},{1,193},{65,1},{129,65},{193,129... | collective-permute-start | bytes 159752 | tf_op jit(solution)/shard_map/ppermute | solution.py:254
  58.6 1.8 %collective-permute-done.8.three = s16[1,208,128]{2,1,0:T(8,128)(2,1)S(1)} collective-permute-done((s16[1,208,128]{2,1,0:T(8,128)(2,1)S(1)}, s16[1,208,128]{2,1,0:T(8,128)(2,1)S(1)}, u32[]{:S(2)}, u32[]{:S(2)}) %collective-permute-start.8) | collective-permute-done | bytes 53280 | tf_op jit(solution)/shard_map/ppermute | solution.py:254
  60.4 1.0 shard_map.63
  61.5 5.9 %all-to-all-start.2 = ((s16[8,208,128]{2,1,0:T(8,128)(2,1)}), s16[8,208,128]{2,1,0:T(8,128)(2,1)}, u32[]{:S(2)}, u32[]{:S(2)}) async-start(s16[8,208,128]{2,1,0:T(8,128)(2,1)} %get-tuple-element.45), calls=%async_computation.2 | async-start | bytes 851968 | tf_op jit(solution)/shard_map/all_to_all | solution.py:287
  67.4 5.4 %collective-permute-start.12 = (bf16[256,768]{1,0:T(8,128)(2,1)S(1)}, bf16[256,768]{1,0:T(8,128)(2,1)S(1)}, u32[]{:S(2)}, u32[]{:S(2)}) collective-permute-start(bf16[256,768]{1,0:T(8,128)(2,1)S(1)} %get-tuple-element.53.refs_0_), channel_id=1, source_target_pairs={{0,32},{32,0},{1,33},{33,1},{2,34},{34,2},{3,35},{35,3},{4,36},{36... | collective-permute-start | bytes 1179656 | tf_op jit(solution)/shard_map/ppermute | solution.py:249
  73.4 0.4 collective-permute-start.16
  74.1 0.6 collective-permute-done.13.refs_5_
  74.7 0.6 collective-permute-done.14.refs_6_
  75.3 0.6 collective-permute-done.15.refs_7_
  75.8 4.1 %shard_map.64 = f32[1,1024]{1,0:T(1,128)} custom-call(f32[1,1024]{1,0:T(1,128)S(1)} %get-tuple-element.46.norms_ref, bf16[768,1024]{1,0:T(8,128)(2,1)S(1)} %copy-done.5, bf16[256,768]{1,0:T(8,128)(2,1)S(1)} %get-tuple-element.53.refs_0_, bf16[256,768]{1,0:T(8,128)(2,1)S(1)} %collective-permute-done.9.refs_1_, ...), custom_call_target="tpu_custom_call" | custom-call | flops 3221225472 | bytes 5242880 | tf_op jit(solution)/shard_map/pallas_call | solution.py:236
  79.9 1.2 %broadcast_in_dim.12 = s16[4,1664,128]{2,1,0:T(8,128)(2,1)S(1)} broadcast(s16[1664,128]{1,0:T(8,128)(2,1)} %bitcast.7), dimensions={1,2} | broadcast | bytes 2129920 | tf_op jit(solution)/shard_map/broadcast_in_dim | solution.py:386
  81.1 17.7 %all_to_all.21 = s16[4,1664,128]{2,1,0:T(8,128)(2,1)S(1)} all-to-all(s16[4,1664,128]{2,1,0:T(8,128)(2,1)S(1)} %broadcast_in_dim.12), channel_id=1, replica_groups={{0,2,4,6},{8,10,12,14},{16,18,20,22},{24,26,28,30},{32,40,48,56},{34,42..., dimensions={0} | all-to-all | bytes 3407872 | tf_op jit(solution)/shard_map/all_to_all | solution.py:281
  99.3 3.5 %shard_map.65.least_ref = f32[8,1024]{1,0:T(8,128)S(1)} custom-call(bf16[768,1024]{1,0:T(8,128)(2,1)S(1)} %copy-done.6, s16[32,208,128]{2,1,0:T(8,128)(2,1)S(1)} %bitcast.13, f32[8,1024]{1,0:T(8,128)S(1)} %broadcast_in_dim.13.least_ref), custom_call_target="tpu_custom_call" | custom-call | flops 3221225472 | bytes 3145728 | tf_op jit(solution)/shard_map/pallas_call | solution.py:236
  102.8 4.7 %shard_map.66 = (f32[1,1024]{1,0:T(1,128)}, f32[64,768]{1,0:T(8,128)}) custom-call(s32[3]{0:T(128)S(1)} %pad_add_fusion.place, bf16[768,1024]{1,0:T(8,128)(2,1)S(1)} %copy-done.6, s16[32,208,128]{2,1,0:T(8,128)(2,1)S(1)} %collective-permute-done.17.piece, f32[8,1024]{1,0:T(8,128)S(1)} %shard_map.65.least_ref, f32[1,1024]{1,0:T(1,128)S(1)} %get-tuple-element.46.norms_ref, ...), custom_call_target="tpu_custom_call" | custom-call | flops 3221225472 | bytes 3145728 | tf_op jit(solution)/shard_map/pallas_call | solution.py:236
  (38 shorter events, 2.1 us)
Async XLA Ops:
  0.6 3.3 %copy-start = (bf16[64,768]{1,0:T(8,128)(2,1)S(1)}, bf16[64,768]{1,0:T(8,128)(2,1)}, u32[]{:S(2)}) copy-start(bf16[64,768]{1,0:T(8,128)(2,1)} %param.4) | copy-start | bytes 294916
  0.6 8.9 %collective-permute-start.1 = (bf16[1024,768]{1,0:T(8,128)(2,1)}, bf16[1024,768]{1,0:T(8,128)(2,1)S(1)}, u32[]{:S(2)}, u32[]{:S(2)}) collective-permute-start(bf16[1024,768]{1,0:T(8,128)(2,1)} %rows_ref), channel_id=1, source_target_pairs={{0,32},{32,0},{1,33},{33,1},{2,34},{34,2},{3,35},{35,3},{4,36},{36... | collective-permute-start | bytes 4718600 | tf_op jit(solution)/shard_map/ppermute | solution.py:249
  4.0 5.5 %collective-permute-start.2 = (bf16[32,768]{1,0:T(8,128)(2,1)S(1)}, bf16[32,768]{1,0:T(8,128)(2,1)S(1)}, u32[]{:S(2)}, u32[]{:S(2)}) collective-permute-start(bf16[32,768]{1,0:T(8,128)(2,1)S(1)} %constant_dynamic-slice_fusion), channel_id=1, source_target_pairs={{0,1},{1,0},{2,3},{3,2},{4,5},{5,4},{6,7},{7,6},{8,9},{9,8},{10,11... | collective-permute-start | bytes 147464 | tf_op jit(solution)/shard_map/ppermute | solution.py:249
  4.0 5.6 %collective-permute-start = (s32[1,1024]{1,0:T(1,128)}, s32[1,1024]{1,0:T(1,128)S(1)}, u32[]{:S(2)}, u32[]{:S(2)}) collective-permute-start(s32[1,1024]{1,0:T(1,128)} %bitcast.14), channel_id=1, source_target_pairs={{0,32},{32,0},{1,33},{33,1},{2,34},{34,2},{3,35},{35,3},{4,36},{36... | collective-permute-start | bytes 12296 | tf_op jit(solution)/shard_map/ppermute | solution.py:249
  5.0 1.4 %copy-start.1 = (bf16[1024,768]{1,0:T(8,128)(2,1)S(1)}, bf16[1024,768]{1,0:T(8,128)(2,1)}, u32[]{:S(2)}) copy-start(bf16[1024,768]{1,0:T(8,128)(2,1)} %rows_ref) | copy-start | bytes 4718596
  6.4 0.7 copy-start.3
  30.7 8.1 %copy-start.2 = (bf16[1024,768]{1,0:T(8,128)(2,1)S(1)}, bf16[1024,768]{1,0:T(8,128)(2,1)}, u32[]{:S(2)}) copy-start(bf16[1024,768]{1,0:T(8,128)(2,1)} %rows_ref) | copy-start | bytes 4718596
  32.3 12.8 %all-to-all-start.1 = ((s16[8,208,128]{2,1,0:T(8,128)(2,1)}), s16[8,208,128]{2,1,0:T(8,128)(2,1)S(1)}, u32[]{:S(2)}, u32[]{:S(2)}) async-start(s16[8,208,128]{2,1,0:T(8,128)(2,1)} %shard_map.60), calls=%async_computation.1 | async-start | bytes 851968 | tf_op jit(solution)/shard_map/all_to_all | solution.py:287
  36.2 9.0 %collective-permute-start.3 = (bf16[64,768]{1,0:T(8,128)(2,1)S(1)}, bf16[64,768]{1,0:T(8,128)(2,1)S(1)}, u32[]{:S(2)}, u32[]{:S(2)}) collective-permute-start(bf16[64,768]{1,0:T(8,128)(2,1)S(1)} %pad_maximum_fusion.c0), channel_id=1, source_target_pairs={{0,2},{8,10},{16,18},{24,26},{2,4},{10,12},{18,20},{26,28},{4,6},{... | collective-permute-start | bytes 294920 | tf_op jit(solution)/shard_map/ppermute | solution.py:301
  36.5 8.7 %collective-permute-start.4 = (bf16[64,768]{1,0:T(8,128)(2,1)S(1)}, bf16[64,768]{1,0:T(8,128)(2,1)S(1)}, u32[]{:S(2)}, u32[]{:S(2)}) collective-permute-start(bf16[64,768]{1,0:T(8,128)(2,1)S(1)} %pad_maximum_fusion.c0), channel_id=1, source_target_pairs={{0,6},{8,14},{16,22},{24,30},{2,0},{10,8},{18,16},{26,24},{4,2},{1... | collective-permute-start | bytes 294920 | tf_op jit(solution)/shard_map/ppermute | solution.py:301
  38.9 7.2 %collective-permute-start.5 = (bf16[64,768]{1,0:T(8,128)(2,1)S(1)}, bf16[64,768]{1,0:T(8,128)(2,1)S(1)}, u32[]{:S(2)}, u32[]{:S(2)}) collective-permute-start(bf16[64,768]{1,0:T(8,128)(2,1)S(1)} %pad_maximum_fusion.c0), channel_id=1, source_target_pairs={{0,4},{8,12},{16,20},{24,28},{2,6},{10,14},{18,22},{26,30},{4,0},{... | collective-permute-start | bytes 294920 | tf_op jit(solution)/shard_map/ppermute | solution.py:301
  39.5 1.2 %copy-start.4 = (bf16[768,1024]{1,0:T(8,128)(2,1)}, bf16[768,1024]{1,0:T(8,128)(2,1)S(1)}, u32[]{:S(2)}) copy-start(bf16[768,1024]{1,0:T(8,128)(2,1)S(1)} %get-tuple-element.47.turned_ref) | copy-start | bytes 4718596
  45.2 30.7 %copy-start.5 = (bf16[768,1024]{1,0:T(8,128)(2,1)S(1)}, bf16[768,1024]{1,0:T(8,128)(2,1)}, u32[]{:S(2)}) copy-start(bf16[768,1024]{1,0:T(8,128)(2,1)} %copy-done.4) | copy-start | bytes 4718596
  46.4 14.1 %collective-permute-start.10 = (bf16[256,768]{1,0:T(8,128)(2,1)S(1)}, bf16[256,768]{1,0:T(8,128)(2,1)S(1)}, u32[]{:S(2)}, u32[]{:S(2)}) collective-permute-start(bf16[256,768]{1,0:T(8,128)(2,1)S(1)} %get-tuple-element.53.refs_0_), channel_id=1, source_target_pairs={{0,24},{8,0},{16,8},{24,16},{2,26},{10,2},{18,10},{26,18},{4,28},{... | collective-permute-start | bytes 1179656 | tf_op jit(solution)/shard_map/ppermute | solution.py:301
  47.4 13.0 %collective-permute-start.11 = (bf16[256,768]{1,0:T(8,128)(2,1)S(1)}, bf16[256,768]{1,0:T(8,128)(2,1)S(1)}, u32[]{:S(2)}, u32[]{:S(2)}) collective-permute-start(bf16[256,768]{1,0:T(8,128)(2,1)S(1)} %get-tuple-element.53.refs_0_), channel_id=1, source_target_pairs={{0,16},{8,24},{16,0},{24,8},{2,18},{10,26},{18,2},{26,10},{4,20},{... | collective-permute-start | bytes 1179656 | tf_op jit(solution)/shard_map/ppermute | solution.py:301
  48.6 11.9 %collective-permute-start.9 = (bf16[256,768]{1,0:T(8,128)(2,1)S(1)}, bf16[256,768]{1,0:T(8,128)(2,1)S(1)}, u32[]{:S(2)}, u32[]{:S(2)}) collective-permute-start(bf16[256,768]{1,0:T(8,128)(2,1)S(1)} %get-tuple-element.53.refs_0_), channel_id=1, source_target_pairs={{0,8},{8,16},{16,24},{24,0},{2,10},{10,18},{18,26},{26,2},{4,12},{... | collective-permute-start | bytes 1179656 | tf_op jit(solution)/shard_map/ppermute | solution.py:301
  48.6 7.6 %collective-permute-start.6 = (s16[1,208,128]{2,1,0:T(8,128)(2,1)S(1)}, s16[1,208,128]{2,1,0:T(8,128)(2,1)S(1)}, u32[]{:S(2)}, u32[]{:S(2)}) collective-permute-start(s16[1,208,128]{2,1,0:T(8,128)(2,1)S(1)} %get-tuple-element.41.own), channel_id=1, source_target_pairs={{0,64},{64,128},{128,192},{192,0},{1,65},{65,129},{129,193},{193,1... | collective-permute-start | bytes 159752 | tf_op jit(solution)/shard_map/ppermute | solution.py:254
  51.6 7.1 %collective-permute-start.7 = (s16[1,208,128]{2,1,0:T(8,128)(2,1)S(1)}, s16[1,208,128]{2,1,0:T(8,128)(2,1)S(1)}, u32[]{:S(2)}, u32[]{:S(2)}) collective-permute-start(s16[1,208,128]{2,1,0:T(8,128)(2,1)S(1)} %get-tuple-element.41.own), channel_id=1, source_target_pairs={{0,128},{64,192},{128,0},{192,64},{1,129},{65,193},{129,1},{193,65... | collective-permute-start | bytes 159752 | tf_op jit(solution)/shard_map/ppermute | solution.py:254
  56.3 4.2 %collective-permute-start.8 = (s16[1,208,128]{2,1,0:T(8,128)(2,1)S(1)}, s16[1,208,128]{2,1,0:T(8,128)(2,1)S(1)}, u32[]{:S(2)}, u32[]{:S(2)}) collective-permute-start(s16[1,208,128]{2,1,0:T(8,128)(2,1)S(1)} %get-tuple-element.41.own), channel_id=1, source_target_pairs={{0,192},{64,0},{128,64},{192,128},{1,193},{65,1},{129,65},{193,129... | collective-permute-start | bytes 159752 | tf_op jit(solution)/shard_map/ppermute | solution.py:254
  61.5 18.4 %all-to-all-start.2 = ((s16[8,208,128]{2,1,0:T(8,128)(2,1)}), s16[8,208,128]{2,1,0:T(8,128)(2,1)}, u32[]{:S(2)}, u32[]{:S(2)}) async-start(s16[8,208,128]{2,1,0:T(8,128)(2,1)} %get-tuple-element.45), calls=%async_computation.2 | async-start | bytes 851968 | tf_op jit(solution)/shard_map/all_to_all | solution.py:287
  67.4 6.8 %collective-permute-start.12 = (bf16[256,768]{1,0:T(8,128)(2,1)S(1)}, bf16[256,768]{1,0:T(8,128)(2,1)S(1)}, u32[]{:S(2)}, u32[]{:S(2)}) collective-permute-start(bf16[256,768]{1,0:T(8,128)(2,1)S(1)} %get-tuple-element.53.refs_0_), channel_id=1, source_target_pairs={{0,32},{32,0},{1,33},{33,1},{2,34},{34,2},{3,35},{35,3},{4,36},{36... | collective-permute-start | bytes 1179656 | tf_op jit(solution)/shard_map/ppermute | solution.py:249
  72.8 1.9 %collective-permute-start.13 = (bf16[256,768]{1,0:T(8,128)(2,1)S(1)}, bf16[256,768]{1,0:T(8,128)(2,1)S(1)}, u32[]{:S(2)}, u32[]{:S(2)}) collective-permute-start(bf16[256,768]{1,0:T(8,128)(2,1)S(1)} %collective-permute-done.9.refs_1_), channel_id=1, source_target_pairs={{0,32},{32,0},{1,33},{33,1},{2,34},{34,2},{3,35},{35,3},{4,36},{36... | collective-permute-start | bytes 1179656 | tf_op jit(solution)/shard_map/ppermute | solution.py:249
  72.9 2.4 %collective-permute-start.14 = (bf16[256,768]{1,0:T(8,128)(2,1)S(1)}, bf16[256,768]{1,0:T(8,128)(2,1)S(1)}, u32[]{:S(2)}, u32[]{:S(2)}) collective-permute-start(bf16[256,768]{1,0:T(8,128)(2,1)S(1)} %collective-permute-done.10.refs_2_), channel_id=1, source_target_pairs={{0,32},{32,0},{1,33},{33,1},{2,34},{34,2},{3,35},{35,3},{4,36},{36... | collective-permute-start | bytes 1179656 | tf_op jit(solution)/shard_map/ppermute | solution.py:249
  73.3 2.5 %collective-permute-start.15 = (bf16[256,768]{1,0:T(8,128)(2,1)S(1)}, bf16[256,768]{1,0:T(8,128)(2,1)S(1)}, u32[]{:S(2)}, u32[]{:S(2)}) collective-permute-start(bf16[256,768]{1,0:T(8,128)(2,1)S(1)} %collective-permute-done.11.refs_3_), channel_id=1, source_target_pairs={{0,32},{32,0},{1,33},{33,1},{2,34},{34,2},{3,35},{35,3},{4,36},{36... | collective-permute-start | bytes 1179656 | tf_op jit(solution)/shard_map/ppermute | solution.py:249
  73.4 6.5 %collective-permute-start.16 = (f32[32,768]{1,0:T(8,128)S(1)}, f32[32,768]{1,0:T(8,128)S(1)}, u32[]{:S(2)}, u32[]{:S(2)}) collective-permute-start(f32[32,768]{1,0:T(8,128)S(1)} %get-tuple-element.48.own), channel_id=1, source_target_pairs={{0,32},{32,0},{1,33},{33,1},{2,34},{34,2},{3,35},{35,3},{4,36},{36... | collective-permute-start | bytes 294920 | tf_op jit(solution)/shard_map/ppermute | solution.py:249
  81.1 18.1 %copy-start.6 = (bf16[768,1024]{1,0:T(8,128)(2,1)S(1)}, bf16[768,1024]{1,0:T(8,128)(2,1)}, u32[]{:S(2)}) copy-start(bf16[768,1024]{1,0:T(8,128)(2,1)} %copy-done.4) | copy-start | bytes 4718596
  98.9 4.0 %collective-permute-start.17 = (s16[32,208,128]{2,1,0:T(8,128)(2,1)S(1)}, s16[32,208,128]{2,1,0:T(8,128)(2,1)S(1)}, u32[]{:S(2)}, u32[]{:S(2)}) collective-permute-start(s16[32,208,128]{2,1,0:T(8,128)(2,1)S(1)} %bitcast.12), channel_id=1, source_target_pairs={{0,32},{32,0},{1,33},{33,1},{2,34},{34,2},{3,35},{35,3},{4,36},{36... | collective-permute-start | bytes 5111816 | tf_op jit(solution)/shard_map/ppermute | solution.py:249

commit v4 on v3

--- a/solution.py
+++ b/solution.py
@@ -176,16 +176,31 @@
     norms_ref[...] = jnp.sum(total, 0, keepdims=True) * 0.25
 
 
-def old_kernel(norms_ref, turned_ref, *refs):
-    *centers, out_ref = refs
+def old_least(turned_ref, centers, least):
     turned = turned_ref[...]
-    least = jnp.full((8, turned.shape[1]), jnp.inf, jnp.float32)
     for ref in centers:
         wide = ref[...].astype(jnp.float32)
         norm = jnp.sum(wide * wide, 1, keepdims=True)
         product = jnp.dot(ref[...], turned, preferred_element_type=jnp.float32)
         least = nearest(product + norm, least)
+    return least
+
+
+def old_own_kernel(turned_ref, *refs):
+    *centers, out_ref = refs
+    least = jnp.full(out_ref.shape, jnp.inf, jnp.float32)
+    out_ref[...] = old_least(turned_ref, centers, least)
+
+
+def old_other_kernel(norms_ref, turned_ref, least_ref, *refs):
+    *centers, out_ref = refs
+    least = old_least(turned_ref, centers, least_ref[...])
     out_ref[...] = norms_ref[...] + jnp.min(least, 0, keepdims=True)
+
+
+def spread_kernel(in_ref, out_ref):
+    for k in range(4):
+        out_ref[k * EACH : (k + 1) * EACH] = in_ref[...]
 
 
 def new_min(turned_ref, piece, least_ref):
@@ -374,16 +389,22 @@
 
     current = list(after(refined, current))
     current_other = [swap(part, "core") for part in current]
+    least = call(
+        old_own_kernel,
+        shape((8, n), f32),
+        turned, *current,
+        flops=2 * 1024 * n * D, moved=3 << 20,
+    )
     old_min = call(
-        old_kernel,
+        old_other_kernel,
         shape((1, n), f32),
-        norms, turned, *current, *current_other,
-        flops=2 * 2048 * n * D, moved=5 << 20,
+        norms, turned, least, *current_other,
+        flops=2 * 1024 * n * D, moved=3 << 20,
     )
     refined_other = swap(refined, "core")
     new, old_min, refined_other = lax.optimization_barrier((new, old_min, refined_other))
     new = exchange_four(
-        jnp.broadcast_to(new[None], (4, *new.shape)).reshape(CHUNKS, CODED, 128)
+        call(spread_kernel, coded(CHUNKS), new, flops=1 << 10, moved=2 << 20)
     )
     new_other = swap(new, "core")
     least = call(

time: 108 us -> 107 us (level)
  waiting for transfers between devices: 9.25 us -> 7.37 us
  Pallas kernels: 22 us -> 23.6 us
  local copies, waits for them, and re-layouts: 4.54 us -> 3.31 us
    ppermute x9, waiting for transfers between devices: 2.03 us -> 0.02 us  [swap(): return lax.ppermute(value, axis, [(0, 1), (1, 0)])]
    pallas_call x9 -> x11, Pallas kernels: 22 us -> 23.6 us  [call(): pl.pallas_call(kernel, out_shape=out_shape, in_specs=specs, out_specs=tup...]
    broadcast_in_dim x1 -> x0, local copies, waits for them, and re-layouts: 1.23 us -> none  [on_device(): jnp.broadcast_to(new[None], (4, *new.shape)).reshape(CHUNKS, CODED, 128)]
  transfers between devices with their start and end apart: 20 -> 20, of which waited for: 7 -> 3; matrix products, arithmetic and copies ran while one was open for 0% -> 0% of each run, Pallas kernels for 10% -> 11%
where the time goes in v4:
time: 107 us
  starting transfers between devices  36.4 us (34%)
  blocking collectives  35.1 us (33%)
  Pallas kernels  23.6 us (22%)
  waiting for transfers between devices  7.37 us (7%)
  local copies, waits for them, and re-layouts  3.31 us (3%)
    all_to_all x2, blocking collectives, exchange_four(): lax.all_to_all(value.reshape(4, -1, 128), ('core', 'y', 'x'), 0, 0, axis_...  35.1 us
    pallas_call x11, Pallas kernels, call(): pl.pallas_call(kernel, out_shape=out_shape, in_specs=specs, out_specs=tup...  23.6 us
    ppermute x9, starting transfers between devices, swap(): return lax.ppermute(value, axis, [(0, 1), (1, 0)])  11.7 us
    ppermute x3, starting transfers between devices, around_z(): lax.ppermute(part, 'zh', [(i, (i + k) % 4) for i in range(4)])  10 us
    all_to_all x2, starting transfers between devices, exchange_eight(): lax.all_to_all(value, ('core', 'y', 'x', 'zl'), 0, 0, axis_index_groups=e...  9.76 us
    ppermute x6, starting transfers between devices, around(): parts.append(lax.ppermute(part, ('core', 'y', 'x'), pairs))  4.91 us
    all_to_all x2, waiting for transfers between devices, exchange_eight(): lax.all_to_all(value, ('core', 'y', 'x', 'zl'), 0, 0, axis_index_groups=e...  4.48 us
    unnamed x14, local copies, waits for them, and re-layouts  3.3 us
  transfers between devices with their start and end apart: 20, of which 3 were waited for; matrix products, arithmetic and copies ran while one was open for 0% of the time, Pallas kernels for 11%

profile of v4, /device:TPU:1, one launch (start us, length us, event | category | flops | bytes accessed | tf_op | source)
XLA Modules:
  0.0 106.6 jit_solution(17099741931940854004)
XLA Ops:
  0.6 3.3 %collective-permute-start.1 = (bf16[1024,768]{1,0:T(8,128)(2,1)}, bf16[1024,768]{1,0:T(8,128)(2,1)S(1)}, u32[]{:S(2)}, u32[]{:S(2)}) collective-permute-start(bf16[1024,768]{1,0:T(8,128)(2,1)} %rows_ref), channel_id=1, source_target_pairs={{0,32},{32,0},{1,33},{33,1},{2,34},{34,2},{3,35},{35,3},{4,36},{36... | collective-permute-start | bytes 4718600 | tf_op jit(solution)/shard_map/ppermute | solution.py:264
  4.0 1.0 collective-permute-start
  5.0 1.4 %copy-done.1 = bf16[1024,768]{1,0:T(8,128)(2,1)S(1)} copy-done((bf16[1024,768]{1,0:T(8,128)(2,1)S(1)}, bf16[1024,768]{1,0:T(8,128)(2,1)}, u32[]{:S(2)}) %copy-start.1) | copy-done | bytes 1572888
  6.4 0.7 copy-done.3
  7.1 2.4 %shard_map.58.own_sums = f32[1024,768]{1,0:T(8,128)S(1)} custom-call(s32[3]{0:T(128)S(1)} %pad_add_fusion.place, s32[1,1024]{1,0:T(1,128)S(1)} %bitcast.16, bf16[1024,768]{1,0:T(8,128)(2,1)S(1)} %copy-done.1), custom_call_target="tpu_custom_call" | custom-call | flops 1610612736 | bytes 5242880 | tf_op jit(solution)/shard_map/pallas_call | solution.py:251
  9.6 3.8 %shard_map.59 = s16[32,208,128]{2,1,0:T(8,128)(2,1)S(1)} custom-call(s32[3]{0:T(128)S(1)} %pad_add_fusion.place, s32[1,1024]{1,0:T(1,128)S(1)} %bitcast.17, s32[1,1024]{1,0:T(1,128)S(1)} %collective-permute-done.labels, f32[1024,768]{1,0:T(8,128)S(1)} %shard_map.58.own_sums, bf16[1024,768]{1,0:T(8,128)(2,1)S(1)} %collective-permute-done.1.rows), custom_call_target="tpu_custom_call" | custom-call | flops 1610612736 | bytes 6291456 | tf_op jit(solution)/shard_map/pallas_call | solution.py:251
  13.4 17.4 %all_to_all.20 = s16[4,1664,128]{2,1,0:T(8,128)(2,1)S(1)} all-to-all(s16[4,1664,128]{2,1,0:T(8,128)(2,1)S(1)} %bitcast.10), channel_id=1, replica_groups={{0,2,4,6},{8,10,12,14},{16,18,20,22},{24,26,28,30},{32,40,48,56},{34,42..., dimensions={0} | all-to-all | bytes 3407872 | tf_op jit(solution)/shard_map/all_to_all | solution.py:296
  30.8 1.6 %shard_map.60 = s16[8,208,128]{2,1,0:T(8,128)(2,1)} custom-call(s16[32,208,128]{2,1,0:T(8,128)(2,1)S(1)} %bitcast.11), custom_call_target="tpu_custom_call" | custom-call | flops 4194304 | bytes 3145728 | tf_op jit(solution)/shard_map/pallas_call | solution.py:251
  32.4 3.9 %all-to-all-start.1 = ((s16[8,208,128]{2,1,0:T(8,128)(2,1)}), s16[8,208,128]{2,1,0:T(8,128)(2,1)S(1)}, u32[]{:S(2)}, u32[]{:S(2)}) async-start(s16[8,208,128]{2,1,0:T(8,128)(2,1)} %shard_map.60), calls=%async_computation.1 | async-start | bytes 851968 | tf_op jit(solution)/shard_map/all_to_all | solution.py:302
  36.3 0.3 collective-permute-start.3
  36.6 2.4 %collective-permute-start.4 = (bf16[64,768]{1,0:T(8,128)(2,1)S(1)}, bf16[64,768]{1,0:T(8,128)(2,1)S(1)}, u32[]{:S(2)}, u32[]{:S(2)}) collective-permute-start(bf16[64,768]{1,0:T(8,128)(2,1)S(1)} %pad_maximum_fusion.c0), channel_id=1, source_target_pairs={{0,6},{8,14},{16,22},{24,30},{2,0},{10,8},{18,16},{26,24},{4,2},{1... | collective-permute-start | bytes 294920 | tf_op jit(solution)/shard_map/ppermute | solution.py:316
  38.9 0.6 shard_map.61
  39.6 1.2 %copy-done.4 = bf16[768,1024]{1,0:T(8,128)(2,1)} copy-done((bf16[768,1024]{1,0:T(8,128)(2,1)}, bf16[768,1024]{1,0:T(8,128)(2,1)S(1)}, u32[]{:S(2)}) %copy-start.4) | copy-done | bytes 1572888
  40.8 4.5 %all-to-all-done.1.in_ref = s16[8,208,128]{2,1,0:T(8,128)(2,1)S(1)} async-done(((s16[8,208,128]{2,1,0:T(8,128)(2,1)}), s16[8,208,128]{2,1,0:T(8,128)(2,1)S(1)}, u32[]{:S(2)}, u32[]{:S(2)}) %all-to-all-start.1) | async-done | bytes 426016 | tf_op jit(solution)/shard_map/all_to_all | solution.py:302
  45.2 0.9 collective-permute-done.5.c3
  46.5 1.0 collective-permute-start.10
  47.5 1.1 %collective-permute-start.11 = (bf16[256,768]{1,0:T(8,128)(2,1)S(1)}, bf16[256,768]{1,0:T(8,128)(2,1)S(1)}, u32[]{:S(2)}, u32[]{:S(2)}) collective-permute-start(bf16[256,768]{1,0:T(8,128)(2,1)S(1)} %get-tuple-element.53.refs_0_), channel_id=1, source_target_pairs={{0,16},{8,24},{16,0},{24,8},{2,18},{10,26},{18,2},{26,10},{4,20},{... | collective-permute-start | bytes 1179656 | tf_op jit(solution)/shard_map/ppermute | solution.py:316
  48.7 3.0 %collective-permute-start.6 = (s16[1,208,128]{2,1,0:T(8,128)(2,1)S(1)}, s16[1,208,128]{2,1,0:T(8,128)(2,1)S(1)}, u32[]{:S(2)}, u32[]{:S(2)}) collective-permute-start(s16[1,208,128]{2,1,0:T(8,128)(2,1)S(1)} %get-tuple-element.41.own), channel_id=1, source_target_pairs={{0,64},{64,128},{128,192},{192,0},{1,65},{65,129},{129,193},{193,1... | collective-permute-start | bytes 159752 | tf_op jit(solution)/shard_map/ppermute | solution.py:269
  51.7 4.7 %collective-permute-start.7 = (s16[1,208,128]{2,1,0:T(8,128)(2,1)S(1)}, s16[1,208,128]{2,1,0:T(8,128)(2,1)S(1)}, u32[]{:S(2)}, u32[]{:S(2)}) collective-permute-start(s16[1,208,128]{2,1,0:T(8,128)(2,1)S(1)} %get-tuple-element.41.own), channel_id=1, source_target_pairs={{0,128},{64,192},{128,0},{192,64},{1,129},{65,193},{129,1},{193,65... | collective-permute-start | bytes 159752 | tf_op jit(solution)/shard_map/ppermute | solution.py:269
  56.3 2.4 %collective-permute-start.8 = (s16[1,208,128]{2,1,0:T(8,128)(2,1)S(1)}, s16[1,208,128]{2,1,0:T(8,128)(2,1)S(1)}, u32[]{:S(2)}, u32[]{:S(2)}) collective-permute-start(s16[1,208,128]{2,1,0:T(8,128)(2,1)S(1)} %get-tuple-element.41.own), channel_id=1, source_target_pairs={{0,192},{64,0},{128,64},{192,128},{1,193},{65,1},{129,65},{193,129... | collective-permute-start | bytes 159752 | tf_op jit(solution)/shard_map/ppermute | solution.py:269
  58.7 1.9 %collective-permute-done.8.three = s16[1,208,128]{2,1,0:T(8,128)(2,1)S(1)} collective-permute-done((s16[1,208,128]{2,1,0:T(8,128)(2,1)S(1)}, s16[1,208,128]{2,1,0:T(8,128)(2,1)S(1)}, u32[]{:S(2)}, u32[]{:S(2)}) %collective-permute-start.8) | collective-permute-done | bytes 53280 | tf_op jit(solution)/shard_map/ppermute | solution.py:269
  60.6 1.0 shard_map.63
  61.7 5.9 %all-to-all-start.2 = ((s16[8,208,128]{2,1,0:T(8,128)(2,1)}), s16[8,208,128]{2,1,0:T(8,128)(2,1)S(1)}, u32[]{:S(2)}, u32[]{:S(2)}) async-start(s16[8,208,128]{2,1,0:T(8,128)(2,1)} %get-tuple-element.45), calls=%async_computation.2 | async-start | bytes 851968 | tf_op jit(solution)/shard_map/all_to_all | solution.py:302
  67.6 5.3 %collective-permute-start.12 = (bf16[256,768]{1,0:T(8,128)(2,1)S(1)}, bf16[256,768]{1,0:T(8,128)(2,1)S(1)}, u32[]{:S(2)}, u32[]{:S(2)}) collective-permute-start(bf16[256,768]{1,0:T(8,128)(2,1)S(1)} %get-tuple-element.53.refs_0_), channel_id=1, source_target_pairs={{0,32},{32,0},{1,33},{33,1},{2,34},{34,2},{3,35},{35,3},{4,36},{36... | collective-permute-start | bytes 1179656 | tf_op jit(solution)/shard_map/ppermute | solution.py:264
  72.9 0.4 collective-permute-start.14
  73.5 0.4 collective-permute-start.16
  73.9 2.8 %shard_map.64.least_ref = f32[8,1024]{1,0:T(8,128)S(1)} custom-call(bf16[768,1024]{1,0:T(8,128)(2,1)S(1)} %copy-done.5, bf16[256,768]{1,0:T(8,128)(2,1)S(1)} %get-tuple-element.53.refs_0_, bf16[256,768]{1,0:T(8,128)(2,1)} %collective-permute-done.9.refs_1_, bf16[256,768]{1,0:T(8,128)(2,1)S(1)} %collective-permute-done.10.refs_2_, ...), custom_call_target="tpu_custom_call" | custom-call | flops 1610612736 | bytes 3145728 | tf_op jit(solution)/shard_map/pallas_call | solution.py:251
  76.8 2.5 %shard_map.65 = f32[1,1024]{1,0:T(1,128)} custom-call(f32[1,1024]{1,0:T(1,128)S(1)} %get-tuple-element.46.norms_ref, bf16[768,1024]{1,0:T(8,128)(2,1)S(1)} %copy-done.5, f32[8,1024]{1,0:T(8,128)S(1)} %shard_map.64.least_ref, bf16[256,768]{1,0:T(8,128)(2,1)S(1)} %collective-permute-done.12.refs_0_, bf16[256,768]{1,0:T(8,128)(2,1)S(1)} %collective-permute-done.13.refs_1_, ...), custom_call_target="tpu_custom_call" | custom-call | flops 1610612736 | bytes 3145728 | tf_op jit(solution)/shard_map/pallas_call | solution.py:251
  79.5 17.7 %all_to_all.21 = s16[4,1664,128]{2,1,0:T(8,128)(2,1)S(1)} all-to-all(s16[4,1664,128]{2,1,0:T(8,128)(2,1)S(1)} %bitcast.12), channel_id=1, replica_groups={{0,2,4,6},{8,10,12,14},{16,18,20,22},{24,26,28,30},{32,40,48,56},{34,42..., dimensions={0} | all-to-all | bytes 3407872 | tf_op jit(solution)/shard_map/all_to_all | solution.py:296
  97.2 1.1 collective-permute-start.17
  98.2 3.6 %shard_map.67.least_ref = f32[8,1024]{1,0:T(8,128)S(1)} custom-call(bf16[768,1024]{1,0:T(8,128)(2,1)S(1)} %copy-done.6, s16[32,208,128]{2,1,0:T(8,128)(2,1)S(1)} %bitcast.14, f32[8,1024]{1,0:T(8,128)S(1)} %broadcast_in_dim.3.least_ref), custom_call_target="tpu_custom_call" | custom-call | flops 3221225472 | bytes 3145728 | tf_op jit(solution)/shard_map/pallas_call | solution.py:251
  101.8 4.8 %shard_map.68 = (f32[1,1024]{1,0:T(1,128)}, f32[64,768]{1,0:T(8,128)}) custom-call(s32[3]{0:T(128)S(1)} %pad_add_fusion.place, bf16[768,1024]{1,0:T(8,128)(2,1)S(1)} %copy-done.6, s16[32,208,128]{2,1,0:T(8,128)(2,1)S(1)} %collective-permute-done.17.piece, f32[8,1024]{1,0:T(8,128)S(1)} %shard_map.67.least_ref, f32[1,1024]{1,0:T(1,128)S(1)} %get-tuple-element.46.norms_ref, ...), custom_call_target="tpu_custom_call" | custom-call | flops 3221225472 | bytes 3145728 | tf_op jit(solution)/shard_map/pallas_call | solution.py:251
  (39 shorter events, 0.9 us)
Async XLA Ops:
  0.6 3.3 %copy-start = (bf16[64,768]{1,0:T(8,128)(2,1)S(1)}, bf16[64,768]{1,0:T(8,128)(2,1)}, u32[]{:S(2)}) copy-start(bf16[64,768]{1,0:T(8,128)(2,1)} %param.4) | copy-start | bytes 294916
  0.6 8.9 %collective-permute-start.1 = (bf16[1024,768]{1,0:T(8,128)(2,1)}, bf16[1024,768]{1,0:T(8,128)(2,1)S(1)}, u32[]{:S(2)}, u32[]{:S(2)}) collective-permute-start(bf16[1024,768]{1,0:T(8,128)(2,1)} %rows_ref), channel_id=1, source_target_pairs={{0,32},{32,0},{1,33},{33,1},{2,34},{34,2},{3,35},{35,3},{4,36},{36... | collective-permute-start | bytes 4718600 | tf_op jit(solution)/shard_map/ppermute | solution.py:264
  4.0 5.6 %collective-permute-start.2 = (bf16[32,768]{1,0:T(8,128)(2,1)S(1)}, bf16[32,768]{1,0:T(8,128)(2,1)S(1)}, u32[]{:S(2)}, u32[]{:S(2)}) collective-permute-start(bf16[32,768]{1,0:T(8,128)(2,1)S(1)} %constant_dynamic-slice_fusion), channel_id=1, source_target_pairs={{0,1},{1,0},{2,3},{3,2},{4,5},{5,4},{6,7},{7,6},{8,9},{9,8},{10,11... | collective-permute-start | bytes 147464 | tf_op jit(solution)/shard_map/ppermute | solution.py:264
  4.0 5.6 %collective-permute-start = (s32[1,1024]{1,0:T(1,128)}, s32[1,1024]{1,0:T(1,128)S(1)}, u32[]{:S(2)}, u32[]{:S(2)}) collective-permute-start(s32[1,1024]{1,0:T(1,128)} %bitcast.15), channel_id=1, source_target_pairs={{0,32},{32,0},{1,33},{33,1},{2,34},{34,2},{3,35},{35,3},{4,36},{36... | collective-permute-start | bytes 12296 | tf_op jit(solution)/shard_map/ppermute | solution.py:264
  5.0 1.4 %copy-start.1 = (bf16[1024,768]{1,0:T(8,128)(2,1)S(1)}, bf16[1024,768]{1,0:T(8,128)(2,1)}, u32[]{:S(2)}) copy-start(bf16[1024,768]{1,0:T(8,128)(2,1)} %rows_ref) | copy-start | bytes 4718596
  6.4 0.7 copy-start.3
  30.8 8.1 %copy-start.2 = (bf16[1024,768]{1,0:T(8,128)(2,1)S(1)}, bf16[1024,768]{1,0:T(8,128)(2,1)}, u32[]{:S(2)}) copy-start(bf16[1024,768]{1,0:T(8,128)(2,1)} %rows_ref) | copy-start | bytes 4718596
  32.4 12.8 %all-to-all-start.1 = ((s16[8,208,128]{2,1,0:T(8,128)(2,1)}), s16[8,208,128]{2,1,0:T(8,128)(2,1)S(1)}, u32[]{:S(2)}, u32[]{:S(2)}) async-start(s16[8,208,128]{2,1,0:T(8,128)(2,1)} %shard_map.60), calls=%async_computation.1 | async-start | bytes 851968 | tf_op jit(solution)/shard_map/all_to_all | solution.py:302
  36.3 9.0 %collective-permute-start.3 = (bf16[64,768]{1,0:T(8,128)(2,1)S(1)}, bf16[64,768]{1,0:T(8,128)(2,1)S(1)}, u32[]{:S(2)}, u32[]{:S(2)}) collective-permute-start(bf16[64,768]{1,0:T(8,128)(2,1)S(1)} %pad_maximum_fusion.c0), channel_id=1, source_target_pairs={{0,2},{8,10},{16,18},{24,26},{2,4},{10,12},{18,20},{26,28},{4,6},{... | collective-permute-start | bytes 294920 | tf_op jit(solution)/shard_map/ppermute | solution.py:316
  36.6 8.7 %collective-permute-start.4 = (bf16[64,768]{1,0:T(8,128)(2,1)S(1)}, bf16[64,768]{1,0:T(8,128)(2,1)S(1)}, u32[]{:S(2)}, u32[]{:S(2)}) collective-permute-start(bf16[64,768]{1,0:T(8,128)(2,1)S(1)} %pad_maximum_fusion.c0), channel_id=1, source_target_pairs={{0,6},{8,14},{16,22},{24,30},{2,0},{10,8},{18,16},{26,24},{4,2},{1... | collective-permute-start | bytes 294920 | tf_op jit(solution)/shard_map/ppermute | solution.py:316
  38.9 7.2 %collective-permute-start.5 = (bf16[64,768]{1,0:T(8,128)(2,1)S(1)}, bf16[64,768]{1,0:T(8,128)(2,1)S(1)}, u32[]{:S(2)}, u32[]{:S(2)}) collective-permute-start(bf16[64,768]{1,0:T(8,128)(2,1)S(1)} %pad_maximum_fusion.c0), channel_id=1, source_target_pairs={{0,4},{8,12},{16,20},{24,28},{2,6},{10,14},{18,22},{26,30},{4,0},{... | collective-permute-start | bytes 294920 | tf_op jit(solution)/shard_map/ppermute | solution.py:316
  39.6 1.2 %copy-start.4 = (bf16[768,1024]{1,0:T(8,128)(2,1)}, bf16[768,1024]{1,0:T(8,128)(2,1)S(1)}, u32[]{:S(2)}) copy-start(bf16[768,1024]{1,0:T(8,128)(2,1)S(1)} %get-tuple-element.47.turned_ref) | copy-start | bytes 4718596
  45.2 28.6 %copy-start.5 = (bf16[768,1024]{1,0:T(8,128)(2,1)S(1)}, bf16[768,1024]{1,0:T(8,128)(2,1)}, u32[]{:S(2)}) copy-start(bf16[768,1024]{1,0:T(8,128)(2,1)} %copy-done.4) | copy-start | bytes 4718596
  46.5 14.2 %collective-permute-start.10 = (bf16[256,768]{1,0:T(8,128)(2,1)S(1)}, bf16[256,768]{1,0:T(8,128)(2,1)S(1)}, u32[]{:S(2)}, u32[]{:S(2)}) collective-permute-start(bf16[256,768]{1,0:T(8,128)(2,1)S(1)} %get-tuple-element.53.refs_0_), channel_id=1, source_target_pairs={{0,24},{8,0},{16,8},{24,16},{2,26},{10,2},{18,10},{26,18},{4,28},{... | collective-permute-start | bytes 1179656 | tf_op jit(solution)/shard_map/ppermute | solution.py:316
  47.5 13.1 %collective-permute-start.11 = (bf16[256,768]{1,0:T(8,128)(2,1)S(1)}, bf16[256,768]{1,0:T(8,128)(2,1)S(1)}, u32[]{:S(2)}, u32[]{:S(2)}) collective-permute-start(bf16[256,768]{1,0:T(8,128)(2,1)S(1)} %get-tuple-element.53.refs_0_), channel_id=1, source_target_pairs={{0,16},{8,24},{16,0},{24,8},{2,18},{10,26},{18,2},{26,10},{4,20},{... | collective-permute-start | bytes 1179656 | tf_op jit(solution)/shard_map/ppermute | solution.py:316
  48.6 12.0 %collective-permute-start.9 = (bf16[256,768]{1,0:T(8,128)(2,1)S(1)}, bf16[256,768]{1,0:T(8,128)(2,1)}, u32[]{:S(2)}, u32[]{:S(2)}) collective-permute-start(bf16[256,768]{1,0:T(8,128)(2,1)S(1)} %get-tuple-element.53.refs_0_), channel_id=1, source_target_pairs={{0,8},{8,16},{16,24},{24,0},{2,10},{10,18},{18,26},{26,2},{4,12},{... | collective-permute-start | bytes 1179656 | tf_op jit(solution)/shard_map/ppermute | solution.py:316
  48.7 7.6 %collective-permute-start.6 = (s16[1,208,128]{2,1,0:T(8,128)(2,1)S(1)}, s16[1,208,128]{2,1,0:T(8,128)(2,1)S(1)}, u32[]{:S(2)}, u32[]{:S(2)}) collective-permute-start(s16[1,208,128]{2,1,0:T(8,128)(2,1)S(1)} %get-tuple-element.41.own), channel_id=1, source_target_pairs={{0,64},{64,128},{128,192},{192,0},{1,65},{65,129},{129,193},{193,1... | collective-permute-start | bytes 159752 | tf_op jit(solution)/shard_map/ppermute | solution.py:269
  51.7 7.0 %collective-permute-start.7 = (s16[1,208,128]{2,1,0:T(8,128)(2,1)S(1)}, s16[1,208,128]{2,1,0:T(8,128)(2,1)S(1)}, u32[]{:S(2)}, u32[]{:S(2)}) collective-permute-start(s16[1,208,128]{2,1,0:T(8,128)(2,1)S(1)} %get-tuple-element.41.own), channel_id=1, source_target_pairs={{0,128},{64,192},{128,0},{192,64},{1,129},{65,193},{129,1},{193,65... | collective-permute-start | bytes 159752 | tf_op jit(solution)/shard_map/ppermute | solution.py:269
  56.3 4.3 %collective-permute-start.8 = (s16[1,208,128]{2,1,0:T(8,128)(2,1)S(1)}, s16[1,208,128]{2,1,0:T(8,128)(2,1)S(1)}, u32[]{:S(2)}, u32[]{:S(2)}) collective-permute-start(s16[1,208,128]{2,1,0:T(8,128)(2,1)S(1)} %get-tuple-element.41.own), channel_id=1, source_target_pairs={{0,192},{64,0},{128,64},{192,128},{1,193},{65,1},{129,65},{193,129... | collective-permute-start | bytes 159752 | tf_op jit(solution)/shard_map/ppermute | solution.py:269
  61.7 17.6 %all-to-all-start.2 = ((s16[8,208,128]{2,1,0:T(8,128)(2,1)}), s16[8,208,128]{2,1,0:T(8,128)(2,1)S(1)}, u32[]{:S(2)}, u32[]{:S(2)}) async-start(s16[8,208,128]{2,1,0:T(8,128)(2,1)} %get-tuple-element.45), calls=%async_computation.2 | async-start | bytes 851968 | tf_op jit(solution)/shard_map/all_to_all | solution.py:302
  67.6 9.2 %collective-permute-start.12 = (bf16[256,768]{1,0:T(8,128)(2,1)S(1)}, bf16[256,768]{1,0:T(8,128)(2,1)S(1)}, u32[]{:S(2)}, u32[]{:S(2)}) collective-permute-start(bf16[256,768]{1,0:T(8,128)(2,1)S(1)} %get-tuple-element.53.refs_0_), channel_id=1, source_target_pairs={{0,32},{32,0},{1,33},{33,1},{2,34},{34,2},{3,35},{35,3},{4,36},{36... | collective-permute-start | bytes 1179656 | tf_op jit(solution)/shard_map/ppermute | solution.py:264
  72.9 3.9 %collective-permute-start.13 = (bf16[256,768]{1,0:T(8,128)(2,1)}, bf16[256,768]{1,0:T(8,128)(2,1)S(1)}, u32[]{:S(2)}, u32[]{:S(2)}) collective-permute-start(bf16[256,768]{1,0:T(8,128)(2,1)} %collective-permute-done.9.refs_1_), channel_id=1, source_target_pairs={{0,32},{32,0},{1,33},{33,1},{2,34},{34,2},{3,35},{35,3},{4,36},{36... | collective-permute-start | bytes 1179656 | tf_op jit(solution)/shard_map/ppermute | solution.py:264
  72.9 3.8 %collective-permute-start.14 = (bf16[256,768]{1,0:T(8,128)(2,1)S(1)}, bf16[256,768]{1,0:T(8,128)(2,1)S(1)}, u32[]{:S(2)}, u32[]{:S(2)}) collective-permute-start(bf16[256,768]{1,0:T(8,128)(2,1)S(1)} %collective-permute-done.10.refs_2_), channel_id=1, source_target_pairs={{0,32},{32,0},{1,33},{33,1},{2,34},{34,2},{3,35},{35,3},{4,36},{36... | collective-permute-start | bytes 1179656 | tf_op jit(solution)/shard_map/ppermute | solution.py:264
  73.4 3.4 %collective-permute-start.15 = (bf16[256,768]{1,0:T(8,128)(2,1)S(1)}, bf16[256,768]{1,0:T(8,128)(2,1)S(1)}, u32[]{:S(2)}, u32[]{:S(2)}) collective-permute-start(bf16[256,768]{1,0:T(8,128)(2,1)S(1)} %collective-permute-done.11.refs_3_), channel_id=1, source_target_pairs={{0,32},{32,0},{1,33},{33,1},{2,34},{34,2},{3,35},{35,3},{4,36},{36... | collective-permute-start | bytes 1179656 | tf_op jit(solution)/shard_map/ppermute | solution.py:264
  73.5 5.8 %collective-permute-start.16 = (f32[32,768]{1,0:T(8,128)S(1)}, f32[32,768]{1,0:T(8,128)S(1)}, u32[]{:S(2)}, u32[]{:S(2)}) collective-permute-start(f32[32,768]{1,0:T(8,128)S(1)} %get-tuple-element.48.own), channel_id=1, source_target_pairs={{0,32},{32,0},{1,33},{33,1},{2,34},{34,2},{3,35},{35,3},{4,36},{36... | collective-permute-start | bytes 294920 | tf_op jit(solution)/shard_map/ppermute | solution.py:264
  79.5 18.8 %copy-start.6 = (bf16[768,1024]{1,0:T(8,128)(2,1)S(1)}, bf16[768,1024]{1,0:T(8,128)(2,1)}, u32[]{:S(2)}) copy-start(bf16[768,1024]{1,0:T(8,128)(2,1)} %copy-done.4) | copy-start | bytes 4718596
  97.2 4.7 %collective-permute-start.17 = (s16[32,208,128]{2,1,0:T(8,128)(2,1)S(1)}, s16[32,208,128]{2,1,0:T(8,128)(2,1)S(1)}, u32[]{:S(2)}, u32[]{:S(2)}) collective-permute-start(s16[32,208,128]{2,1,0:T(8,128)(2,1)S(1)} %bitcast.13), channel_id=1, source_target_pairs={{0,32},{32,0},{1,33},{33,1},{2,34},{34,2},{3,35},{35,3},{4,36},{36... | collective-permute-start | bytes 5111816 | tf_op jit(solution)/shard_map/ppermute | solution.py:264

commit v5 on v4

--- a/solution.py
+++ b/solution.py
@@ -192,23 +192,20 @@
     out_ref[...] = old_least(turned_ref, centers, least)
 
 
-def old_other_kernel(norms_ref, turned_ref, least_ref, *refs):
-    *centers, out_ref = refs
+def old_other_kernel(place, norms_ref, turned_ref, least_ref, own, other, *refs):
+    *centers, out_ref, refined_ref = refs
     least = old_least(turned_ref, centers, least_ref[...])
     out_ref[...] = norms_ref[...] + jnp.min(least, 0, keepdims=True)
-
-
-def spread_kernel(in_ref, out_ref):
-    for k in range(4):
-        out_ref[k * EACH : (k + 1) * EACH] = in_ref[...]
-
-
-def new_min(turned_ref, piece, least_ref):
+    half = place[2]
+    refined_ref[pl.ds(pl.multiple_of(half, HALF), HALF), :] = own[...]
+    refined_ref[pl.ds(pl.multiple_of(HALF - half, HALF), HALF), :] = other[...]
+
+
+def new_least(turned_ref, pieces, least):
     turned = turned_ref[...]
-    least = least_ref[...]
-    for t in range(CHUNKS // EACH):
+    for piece in pieces:
         high, low, scale, norm = [], [], [], []
-        for c in range(t * EACH, (t + 1) * EACH):
+        for c in range(EACH):
             wide = jnp.concatenate(
                 [piece[c, block(b), :].astype(jnp.float32) for b in range(COLS)], 1
             )
@@ -227,18 +224,14 @@
     return least
 
 
-def new_own_kernel(turned_ref, piece, least_ref, out_ref):
-    out_ref[...] = new_min(turned_ref, piece, least_ref)
-
-
-def new_other_kernel(
-    place, turned_ref, piece, least_ref, norms_ref, own, other, out_ref, refined_ref
-):
-    least = new_min(turned_ref, piece, least_ref)
+def new_kernel(turned_ref, least_ref, *refs):
+    *pieces, out_ref = refs
+    out_ref[...] = new_least(turned_ref, pieces, least_ref[...])
+
+
+def last_kernel(turned_ref, least_ref, norms_ref, piece, out_ref):
+    least = new_least(turned_ref, [piece], least_ref[...])
     out_ref[...] = norms_ref[...] + jnp.min(least, 0, keepdims=True)
-    half = place[2]
-    refined_ref[pl.ds(pl.multiple_of(half, HALF), HALF), :] = own[...]
-    refined_ref[pl.ds(pl.multiple_of(HALF - half, HALF), HALF), :] = other[...]
 
 
 def call(kernel, out_shape, *args, flops=0, moved=0, smem=0):
@@ -395,29 +388,36 @@
         turned, *current,
         flops=2 * 1024 * n * D, moved=3 << 20,
     )
-    old_min = call(
+    old_min, refined_centers = call(
         old_other_kernel,
+        (shape((1, n), f32), shape((2 * HALF, D), f32)),
+        place, norms, turned, least, refined, swap(refined, "core"), *current_other,
+        flops=2 * 1024 * n * D, moved=3 << 20, smem=1,
+    )
+    new, old_min = lax.optimization_barrier((new, old_min))
+    new = around(new, 0)
+
+    def take(least, *pieces):
+        return call(
+            new_kernel,
+            shape((8, n), f32),
+            turned, least, *pieces,
+            flops=4 * TILE * n * D * len(pieces), moved=len(pieces) << 19,
+        )
+
+    least = jnp.full((8, n), jnp.inf, f32)
+    least = take(least, new[0], swap(new[0], "core"))
+    least, new[1], new[2] = lax.optimization_barrier((least, new[1], new[2]))
+    swapped = [swap(new[1], "core"), swap(new[2], "core")]
+    least = take(least, new[1], new[2])
+    least, new[3] = lax.optimization_barrier((least, new[3]))
+    last = swap(new[3], "core")
+    least = take(least, *swapped, new[3])
+    new_min = call(
+        last_kernel,
         shape((1, n), f32),
-        norms, turned, least, *current_other,
-        flops=2 * 1024 * n * D, moved=3 << 20,
-    )
-    refined_other = swap(refined, "core")
-    new, old_min, refined_other = lax.optimization_barrier((new, old_min, refined_other))
-    new = exchange_four(
-        call(spread_kernel, coded(CHUNKS), new, flops=1 << 10, moved=2 << 20)
-    )
-    new_other = swap(new, "core")
-    least = call(
-        new_own_kernel,
-        shape((8, n), f32),
-        turned, new, jnp.full((8, n), jnp.inf, f32),
-        flops=4 * 1024 * n * D, moved=3 << 20,
-    )
-    new_min, refined_centers = call(
-        new_other_kernel,
-        (shape((1, n), f32), shape((2 * HALF, D), f32)),
-        place, turned, new_other, least, norms, refined, refined_other,
-        flops=4 * 1024 * n * D, moved=3 << 20, smem=1,
+        turned, least, norms, last,
+        flops=4 * TILE * n * D, moved=1 << 19,
     )
     return old_min.reshape(n), refined_centers, new_min.reshape(n)
 

time: 107 us -> 102 us (0.953)
  blocking collectives: 35.1 us -> 17.4 us
  waiting for transfers between devices: 7.37 us -> 14.2 us
  starting transfers between devices: 36.4 us -> 42.3 us
    all_to_all x2 -> x1, blocking collectives: 35.1 us -> 17.4 us  [exchange_four(): lax.all_to_all(value.reshape(4, -1, 128), ('core', 'y', 'x'), 0, 0, axis_...]
    ppermute x6 -> x9, waiting for transfers between devices: 0.95 us -> 7.79 us  [around(): parts.append(lax.ppermute(part, ('core', 'y', 'x'), pairs))]
    ppermute x6 -> x9, starting transfers between devices: 4.91 us -> 8.49 us  [around(): parts.append(lax.ppermute(part, ('core', 'y', 'x'), pairs))]
    ppermute x9 -> x12, starting transfers between devices: 11.7 us -> 14 us  [swap(): return lax.ppermute(value, axis, [(0, 1), (1, 0)])]
    pallas_call x11 -> x12, Pallas kernels: 23.6 us -> 23.7 us  [call(): pl.pallas_call(kernel, out_shape=out_shape, in_specs=specs, out_specs=tup...]
    unnamed x14 -> x12, local copies, waits for them, and re-layouts: 3.3 us -> 3.29 us
  transfers between devices with their start and end apart: 20 -> 26, of which waited for: 3 -> 5; matrix products, arithmetic and copies ran while one was open for 0% -> 0% of each run, Pallas kernels for 11% -> 15%
where the time goes in v5:
time: 102 us
  starting transfers between devices  42.3 us (41%)
  Pallas kernels  23.7 us (23%)
  blocking collectives  17.4 us (17%)
  waiting for transfers between devices  14.2 us (14%)
  local copies, waits for them, and re-layouts  3.3 us (3%)
    pallas_call x12, Pallas kernels, call(): pl.pallas_call(kernel, out_shape=out_shape, in_specs=specs, out_specs=tup...  23.7 us
    all_to_all x1, blocking collectives, exchange_four(): lax.all_to_all(value.reshape(4, -1, 128), ('core', 'y', 'x'), 0, 0, axis_...  17.4 us
    ppermute x12, starting transfers between devices, swap(): return lax.ppermute(value, axis, [(0, 1), (1, 0)])  14 us
    ppermute x3, starting transfers between devices, around_z(): lax.ppermute(part, 'zh', [(i, (i + k) % 4) for i in range(4)])  10 us
    all_to_all x2, starting transfers between devices, exchange_eight(): lax.all_to_all(value, ('core', 'y', 'x', 'zl'), 0, 0, axis_index_groups=e...  9.77 us
    ppermute x9, starting transfers between devices, around(): parts.append(lax.ppermute(part, ('core', 'y', 'x'), pairs))  8.49 us
    ppermute x9, waiting for transfers between devices, around(): parts.append(lax.ppermute(part, ('core', 'y', 'x'), pairs))  7.79 us
    all_to_all x2, waiting for transfers between devices, exchange_eight(): lax.all_to_all(value, ('core', 'y', 'x', 'zl'), 0, 0, axis_index_groups=e...  4.49 us
  transfers between devices with their start and end apart: 26, of which 5 were waited for; matrix products, arithmetic and copies ran while one was open for 0% of the time, Pallas kernels for 15%

profile of v5, /device:TPU:1, one launch (start us, length us, event | category | flops | bytes accessed | tf_op | source)
XLA Modules:
  0.0 101.8 jit_solution(13029092590877940568)
XLA Ops:
  0.6 3.3 %collective-permute-start.1 = (bf16[1024,768]{1,0:T(8,128)(2,1)}, bf16[1024,768]{1,0:T(8,128)(2,1)S(1)}, u32[]{:S(2)}, u32[]{:S(2)}) collective-permute-start(bf16[1024,768]{1,0:T(8,128)(2,1)} %rows_ref), channel_id=1, source_target_pairs={{0,32},{32,0},{1,33},{33,1},{2,34},{34,2},{3,35},{35,3},{4,36},{36... | collective-permute-start | bytes 4718600 | tf_op jit(solution)/shard_map/ppermute | solution.py:257
  4.0 1.0 collective-permute-start
  5.0 1.4 %copy-done.1 = bf16[1024,768]{1,0:T(8,128)(2,1)S(1)} copy-done((bf16[1024,768]{1,0:T(8,128)(2,1)S(1)}, bf16[1024,768]{1,0:T(8,128)(2,1)}, u32[]{:S(2)}) %copy-start.1) | copy-done | bytes 1572888
  7.1 2.4 %shard_map.58.own_sums = f32[1024,768]{1,0:T(8,128)S(1)} custom-call(s32[3]{0:T(128)S(1)} %pad_add_fusion.place, s32[1,1024]{1,0:T(1,128)S(1)} %bitcast.11, bf16[1024,768]{1,0:T(8,128)(2,1)S(1)} %copy-done.1), custom_call_target="tpu_custom_call" | custom-call | flops 1610612736 | bytes 5242880 | tf_op jit(solution)/shard_map/pallas_call | solution.py:244
  9.6 3.8 %shard_map.59 = s16[32,208,128]{2,1,0:T(8,128)(2,1)S(1)} custom-call(s32[3]{0:T(128)S(1)} %pad_add_fusion.place, s32[1,1024]{1,0:T(1,128)S(1)} %bitcast.12, s32[1,1024]{1,0:T(1,128)S(1)} %collective-permute-done.labels, f32[1024,768]{1,0:T(8,128)S(1)} %shard_map.58.own_sums, bf16[1024,768]{1,0:T(8,128)(2,1)S(1)} %collective-permute-done.1.rows), custom_call_target="tpu_custom_call" | custom-call | flops 1610612736 | bytes 6291456 | tf_op jit(solution)/shard_map/pallas_call | solution.py:244
  13.4 17.4 %all_to_all.15 = s16[4,1664,128]{2,1,0:T(8,128)(2,1)S(1)} all-to-all(s16[4,1664,128]{2,1,0:T(8,128)(2,1)S(1)} %bitcast.8), channel_id=1, replica_groups={{0,2,4,6},{8,10,12,14},{16,18,20,22},{24,26,28,30},{32,40,48,56},{34,42..., dimensions={0} | all-to-all | bytes 3407872 | tf_op jit(solution)/shard_map/all_to_all | solution.py:289
  30.8 1.6 %shard_map.60 = s16[8,208,128]{2,1,0:T(8,128)(2,1)} custom-call(s16[32,208,128]{2,1,0:T(8,128)(2,1)S(1)} %bitcast.9), custom_call_target="tpu_custom_call" | custom-call | flops 4194304 | bytes 3145728 | tf_op jit(solution)/shard_map/pallas_call | solution.py:244
  32.4 3.9 %all-to-all-start.1 = ((s16[8,208,128]{2,1,0:T(8,128)(2,1)}), s16[8,208,128]{2,1,0:T(8,128)(2,1)S(1)}, u32[]{:S(2)}, u32[]{:S(2)}) async-start(s16[8,208,128]{2,1,0:T(8,128)(2,1)} %shard_map.60), calls=%async_computation.1 | async-start | bytes 851968 | tf_op jit(solution)/shard_map/all_to_all | solution.py:295
  36.5 2.4 %collective-permute-start.4 = (bf16[64,768]{1,0:T(8,128)(2,1)S(1)}, bf16[64,768]{1,0:T(8,128)(2,1)S(1)}, u32[]{:S(2)}, u32[]{:S(2)}) collective-permute-start(bf16[64,768]{1,0:T(8,128)(2,1)S(1)} %pad_maximum_fusion.c0), channel_id=1, source_target_pairs={{0,6},{8,14},{16,22},{24,30},{2,0},{10,8},{18,16},{26,24},{4,2},{1... | collective-permute-start | bytes 294920 | tf_op jit(solution)/shard_map/ppermute | solution.py:309
  39.6 1.2 %copy-done.4 = bf16[768,1024]{1,0:T(8,128)(2,1)} copy-done((bf16[768,1024]{1,0:T(8,128)(2,1)}, bf16[768,1024]{1,0:T(8,128)(2,1)S(1)}, u32[]{:S(2)}) %copy-start.4) | copy-done | bytes 1572888
  40.7 4.5 %all-to-all-done.1.in_ref = s16[8,208,128]{2,1,0:T(8,128)(2,1)S(1)} async-done(((s16[8,208,128]{2,1,0:T(8,128)(2,1)}), s16[8,208,128]{2,1,0:T(8,128)(2,1)S(1)}, u32[]{:S(2)}, u32[]{:S(2)}) %all-to-all-start.1) | async-done | bytes 426016 | tf_op jit(solution)/shard_map/all_to_all | solution.py:295
  45.2 0.9 collective-permute-done.5.c3
  46.4 1.0 %collective-permute-start.10 = (bf16[256,768]{1,0:T(8,128)(2,1)S(1)}, bf16[256,768]{1,0:T(8,128)(2,1)S(1)}, u32[]{:S(2)}, u32[]{:S(2)}) collective-permute-start(bf16[256,768]{1,0:T(8,128)(2,1)S(1)} %get-tuple-element.57.refs_0_), channel_id=1, source_target_pairs={{0,24},{8,0},{16,8},{24,16},{2,26},{10,2},{18,10},{26,18},{4,28},{... | collective-permute-start | bytes 1179656 | tf_op jit(solution)/shard_map/ppermute | solution.py:309
  47.5 1.1 %collective-permute-start.11 = (bf16[256,768]{1,0:T(8,128)(2,1)S(1)}, bf16[256,768]{1,0:T(8,128)(2,1)S(1)}, u32[]{:S(2)}, u32[]{:S(2)}) collective-permute-start(bf16[256,768]{1,0:T(8,128)(2,1)S(1)} %get-tuple-element.57.refs_0_), channel_id=1, source_target_pairs={{0,16},{8,24},{16,0},{24,8},{2,18},{10,26},{18,2},{26,10},{4,20},{... | collective-permute-start | bytes 1179656 | tf_op jit(solution)/shard_map/ppermute | solution.py:309
  48.7 3.0 %collective-permute-start.6 = (s16[1,208,128]{2,1,0:T(8,128)(2,1)S(1)}, s16[1,208,128]{2,1,0:T(8,128)(2,1)S(1)}, u32[]{:S(2)}, u32[]{:S(2)}) collective-permute-start(s16[1,208,128]{2,1,0:T(8,128)(2,1)S(1)} %get-tuple-element.45.own), channel_id=1, source_target_pairs={{0,64},{64,128},{128,192},{192,0},{1,65},{65,129},{129,193},{193,1... | collective-permute-start | bytes 159752 | tf_op jit(solution)/shard_map/ppermute | solution.py:262
  51.7 4.7 %collective-permute-start.7 = (s16[1,208,128]{2,1,0:T(8,128)(2,1)S(1)}, s16[1,208,128]{2,1,0:T(8,128)(2,1)S(1)}, u32[]{:S(2)}, u32[]{:S(2)}) collective-permute-start(s16[1,208,128]{2,1,0:T(8,128)(2,1)S(1)} %get-tuple-element.45.own), channel_id=1, source_target_pairs={{0,128},{64,192},{128,0},{192,64},{1,129},{65,193},{129,1},{193,65... | collective-permute-start | bytes 159752 | tf_op jit(solution)/shard_map/ppermute | solution.py:262
  56.3 2.4 %collective-permute-start.8 = (s16[1,208,128]{2,1,0:T(8,128)(2,1)S(1)}, s16[1,208,128]{2,1,0:T(8,128)(2,1)S(1)}, u32[]{:S(2)}, u32[]{:S(2)}) collective-permute-start(s16[1,208,128]{2,1,0:T(8,128)(2,1)S(1)} %get-tuple-element.45.own), channel_id=1, source_target_pairs={{0,192},{64,0},{128,64},{192,128},{1,193},{65,1},{129,65},{193,129... | collective-permute-start | bytes 159752 | tf_op jit(solution)/shard_map/ppermute | solution.py:262
  58.7 1.9 %collective-permute-done.8.three = s16[1,208,128]{2,1,0:T(8,128)(2,1)S(1)} collective-permute-done((s16[1,208,128]{2,1,0:T(8,128)(2,1)S(1)}, s16[1,208,128]{2,1,0:T(8,128)(2,1)S(1)}, u32[]{:S(2)}, u32[]{:S(2)}) %collective-permute-start.8) | collective-permute-done | bytes 53280 | tf_op jit(solution)/shard_map/ppermute | solution.py:262
  60.6 1.0 shard_map.63
  61.6 5.9 %all-to-all-start.2 = ((s16[8,208,128]{2,1,0:T(8,128)(2,1)}), s16[8,208,128]{2,1,0:T(8,128)(2,1)S(1)}, u32[]{:S(2)}, u32[]{:S(2)}) async-start(s16[8,208,128]{2,1,0:T(8,128)(2,1)} %get-tuple-element.49), calls=%async_computation.2 | async-start | bytes 851968 | tf_op jit(solution)/shard_map/all_to_all | solution.py:295
  67.5 5.3 %collective-permute-start.13 = (bf16[256,768]{1,0:T(8,128)(2,1)S(1)}, bf16[256,768]{1,0:T(8,128)(2,1)S(1)}, u32[]{:S(2)}, u32[]{:S(2)}) collective-permute-start(bf16[256,768]{1,0:T(8,128)(2,1)S(1)} %get-tuple-element.57.refs_0_), channel_id=1, source_target_pairs={{0,32},{32,0},{1,33},{33,1},{2,34},{34,2},{3,35},{35,3},{4,36},{36... | collective-permute-start | bytes 1179656 | tf_op jit(solution)/shard_map/ppermute | solution.py:257
  73.9 2.8 %shard_map.64.least_ref = f32[8,1024]{1,0:T(8,128)S(1)} custom-call(bf16[768,1024]{1,0:T(8,128)(2,1)S(1)} %copy-done.5, bf16[256,768]{1,0:T(8,128)(2,1)S(1)} %get-tuple-element.57.refs_0_, bf16[256,768]{1,0:T(8,128)(2,1)} %collective-permute-done.9.refs_1_, bf16[256,768]{1,0:T(8,128)(2,1)S(1)} %collective-permute-done.10.refs_2_, ...), custom_call_target="tpu_custom_call" | custom-call | flops 1610612736 | bytes 3145728 | tf_op jit(solution)/shard_map/pallas_call | solution.py:244
  76.8 3.0 %shard_map.65 = (f32[1,1024]{1,0:T(1,128)}, f32[64,768]{1,0:T(8,128)}) custom-call(s32[3]{0:T(128)S(1)} %pad_add_fusion.place, f32[1,1024]{1,0:T(1,128)S(1)} %get-tuple-element.50.norms_ref, bf16[768,1024]{1,0:T(8,128)(2,1)S(1)} %copy-done.5, f32[8,1024]{1,0:T(8,128)S(1)} %shard_map.64.least_ref, f32[32,768]{1,0:T(8,128)S(1)} %get-tuple-element.52.own, ...), custom_call_target="tpu_custom_call" | custom-call | flops 1610612736 | bytes 3145728 | tf_op jit(solution)/shard_map/pallas_call | solution.py:244
  79.8 1.2 %collective-permute-start.17 = (s16[8,208,128]{2,1,0:T(8,128)(2,1)S(1)}, s16[8,208,128]{2,1,0:T(8,128)(2,1)S(1)}, u32[]{:S(2)}, u32[]{:S(2)}) collective-permute-start(s16[8,208,128]{2,1,0:T(8,128)(2,1)S(1)} %all-to-all-done.2.refs_0_), channel_id=1, source_target_pairs={{0,32},{32,0},{1,33},{33,1},{2,34},{34,2},{3,35},{35,3},{4,36},{36... | collective-permute-start | bytes 1277960 | tf_op jit(solution)/shard_map/ppermute | solution.py:257
  81.6 2.1 %collective-permute-start.19 = (s16[8,208,128]{2,1,0:T(8,128)(2,1)S(1)}, s16[8,208,128]{2,1,0:T(8,128)(2,1)S(1)}, u32[]{:S(2)}, u32[]{:S(2)}) collective-permute-start(s16[8,208,128]{2,1,0:T(8,128)(2,1)S(1)} %all-to-all-done.2.refs_0_), channel_id=1, source_target_pairs={{0,6},{8,14},{16,22},{24,30},{2,0},{10,8},{18,16},{26,24},{4,2},{1... | collective-permute-start | bytes 1277960 | tf_op jit(solution)/shard_map/ppermute | solution.py:309
  84.6 1.9 %shard_map.66.least_ref = f32[8,1024]{1,0:T(8,128)S(1)} custom-call(bf16[768,1024]{1,0:T(8,128)(2,1)S(1)} %copy-done.5, f32[8,1024]{1,0:T(8,128)S(1)} %broadcast_in_dim.3.least_ref, s16[8,208,128]{2,1,0:T(8,128)(2,1)S(1)} %all-to-all-done.2.refs_0_, s16[8,208,128]{2,1,0:T(8,128)(2,1)S(1)} %collective-permute-done.17.refs_1_), custom_call_target="tpu_custom_call" | custom-call | flops 1610612736 | bytes 1048576 | tf_op jit(solution)/shard_map/pallas_call | solution.py:244
  86.5 3.0 %collective-permute-done.18.refs_0_ = s16[8,208,128]{2,1,0:T(8,128)(2,1)S(1)} collective-permute-done((s16[8,208,128]{2,1,0:T(8,128)(2,1)S(1)}, s16[8,208,128]{2,1,0:T(8,128)(2,1)S(1)}, u32[]{:S(2)}, u32[]{:S(2)}) %collective-permute-start.18) | collective-permute-done | bytes 426016 | tf_op jit(solution)/shard_map/ppermute | solution.py:309
  89.5 3.8 %collective-permute-done.19.refs_1_ = s16[8,208,128]{2,1,0:T(8,128)(2,1)S(1)} collective-permute-done((s16[8,208,128]{2,1,0:T(8,128)(2,1)S(1)}, s16[8,208,128]{2,1,0:T(8,128)(2,1)S(1)}, u32[]{:S(2)}, u32[]{:S(2)}) %collective-permute-start.19) | collective-permute-done | bytes 426016 | tf_op jit(solution)/shard_map/ppermute | solution.py:309
  93.3 1.6 %collective-permute-start.21 = (s16[8,208,128]{2,1,0:T(8,128)(2,1)S(1)}, s16[8,208,128]{2,1,0:T(8,128)(2,1)S(1)}, u32[]{:S(2)}, u32[]{:S(2)}) collective-permute-start(s16[8,208,128]{2,1,0:T(8,128)(2,1)S(1)} %collective-permute-done.18.refs_0_), channel_id=1, source_target_pairs={{0,32},{32,0},{1,33},{33,1},{2,34},{34,2},{3,35},{35,3},{4,36},{36... | collective-permute-start | bytes 1277960 | tf_op jit(solution)/shard_map/ppermute | solution.py:257
  94.9 1.9 %shard_map.67.least_ref = f32[8,1024]{1,0:T(8,128)S(1)} custom-call(bf16[768,1024]{1,0:T(8,128)(2,1)S(1)} %copy-done.5, f32[8,1024]{1,0:T(8,128)S(1)} %shard_map.66.least_ref, s16[8,208,128]{2,1,0:T(8,128)(2,1)S(1)} %collective-permute-done.18.refs_0_, s16[8,208,128]{2,1,0:T(8,128)(2,1)S(1)} %collective-permute-done.19.refs_1_), custom_call_target="tpu_custom_call" | custom-call | flops 1610612736 | bytes 1048576 | tf_op jit(solution)/shard_map/pallas_call | solution.py:244
  97.4 2.7 %shard_map.68.least_ref = f32[8,1024]{1,0:T(8,128)S(1)} custom-call(bf16[768,1024]{1,0:T(8,128)(2,1)S(1)} %copy-done.5, f32[8,1024]{1,0:T(8,128)S(1)} %shard_map.67.least_ref, s16[8,208,128]{2,1,0:T(8,128)(2,1)S(1)} %collective-permute-done.21.refs_0_, s16[8,208,128]{2,1,0:T(8,128)(2,1)S(1)} %collective-permute-done.22.refs_1_, ...), custom_call_target="tpu_custom_call" | custom-call | flops 2415919104 | bytes 1572864 | tf_op jit(solution)/shard_map/pallas_call | solution.py:244
  100.1 1.7 %shard_map.69 = f32[1,1024]{1,0:T(1,128)} custom-call(bf16[768,1024]{1,0:T(8,128)(2,1)S(1)} %copy-done.5, f32[8,1024]{1,0:T(8,128)S(1)} %shard_map.68.least_ref, f32[1,1024]{1,0:T(1,128)S(1)} %get-tuple-element.50.norms_ref, s16[8,208,128]{2,1,0:T(8,128)(2,1)S(1)} %collective-permute-done.23.piece), custom_call_target="tpu_custom_call" | custom-call | flops 805306368 | bytes 524288 | tf_op jit(solution)/shard_map/pallas_call | solution.py:244
  (49 shorter events, 5.2 us)
Async XLA Ops:
  0.6 3.3 %copy-start = (bf16[64,768]{1,0:T(8,128)(2,1)S(1)}, bf16[64,768]{1,0:T(8,128)(2,1)}, u32[]{:S(2)}) copy-start(bf16[64,768]{1,0:T(8,128)(2,1)} %param.4) | copy-start | bytes 294916
  0.6 8.9 %collective-permute-start.1 = (bf16[1024,768]{1,0:T(8,128)(2,1)}, bf16[1024,768]{1,0:T(8,128)(2,1)S(1)}, u32[]{:S(2)}, u32[]{:S(2)}) collective-permute-start(bf16[1024,768]{1,0:T(8,128)(2,1)} %rows_ref), channel_id=1, source_target_pairs={{0,32},{32,0},{1,33},{33,1},{2,34},{34,2},{3,35},{35,3},{4,36},{36... | collective-permute-start | bytes 4718600 | tf_op jit(solution)/shard_map/ppermute | solution.py:257
  4.0 5.6 %collective-permute-start.2 = (bf16[32,768]{1,0:T(8,128)(2,1)S(1)}, bf16[32,768]{1,0:T(8,128)(2,1)S(1)}, u32[]{:S(2)}, u32[]{:S(2)}) collective-permute-start(bf16[32,768]{1,0:T(8,128)(2,1)S(1)} %constant_dynamic-slice_fusion), channel_id=1, source_target_pairs={{0,1},{1,0},{2,3},{3,2},{4,5},{5,4},{6,7},{7,6},{8,9},{9,8},{10,11... | collective-permute-start | bytes 147464 | tf_op jit(solution)/shard_map/ppermute | solution.py:257
  4.0 5.6 %collective-permute-start = (s32[1,1024]{1,0:T(1,128)}, s32[1,1024]{1,0:T(1,128)S(1)}, u32[]{:S(2)}, u32[]{:S(2)}) collective-permute-start(s32[1,1024]{1,0:T(1,128)} %bitcast.10), channel_id=1, source_target_pairs={{0,32},{32,0},{1,33},{33,1},{2,34},{34,2},{3,35},{35,3},{4,36},{36... | collective-permute-start | bytes 12296 | tf_op jit(solution)/shard_map/ppermute | solution.py:257
  5.0 1.4 %copy-start.1 = (bf16[1024,768]{1,0:T(8,128)(2,1)S(1)}, bf16[1024,768]{1,0:T(8,128)(2,1)}, u32[]{:S(2)}) copy-start(bf16[1024,768]{1,0:T(8,128)(2,1)} %rows_ref) | copy-start | bytes 4718596
  6.4 0.7 copy-start.3
  30.8 8.1 %copy-start.2 = (bf16[1024,768]{1,0:T(8,128)(2,1)S(1)}, bf16[1024,768]{1,0:T(8,128)(2,1)}, u32[]{:S(2)}) copy-start(bf16[1024,768]{1,0:T(8,128)(2,1)} %rows_ref) | copy-start | bytes 4718596
  32.4 12.8 %all-to-all-start.1 = ((s16[8,208,128]{2,1,0:T(8,128)(2,1)}), s16[8,208,128]{2,1,0:T(8,128)(2,1)S(1)}, u32[]{:S(2)}, u32[]{:S(2)}) async-start(s16[8,208,128]{2,1,0:T(8,128)(2,1)} %shard_map.60), calls=%async_computation.1 | async-start | bytes 851968 | tf_op jit(solution)/shard_map/all_to_all | solution.py:295
  36.2 9.0 %collective-permute-start.3 = (bf16[64,768]{1,0:T(8,128)(2,1)S(1)}, bf16[64,768]{1,0:T(8,128)(2,1)S(1)}, u32[]{:S(2)}, u32[]{:S(2)}) collective-permute-start(bf16[64,768]{1,0:T(8,128)(2,1)S(1)} %pad_maximum_fusion.c0), channel_id=1, source_target_pairs={{0,2},{8,10},{16,18},{24,26},{2,4},{10,12},{18,20},{26,28},{4,6},{... | collective-permute-start | bytes 294920 | tf_op jit(solution)/shard_map/ppermute | solution.py:309
  36.5 8.7 %collective-permute-start.4 = (bf16[64,768]{1,0:T(8,128)(2,1)S(1)}, bf16[64,768]{1,0:T(8,128)(2,1)S(1)}, u32[]{:S(2)}, u32[]{:S(2)}) collective-permute-start(bf16[64,768]{1,0:T(8,128)(2,1)S(1)} %pad_maximum_fusion.c0), channel_id=1, source_target_pairs={{0,6},{8,14},{16,22},{24,30},{2,0},{10,8},{18,16},{26,24},{4,2},{1... | collective-permute-start | bytes 294920 | tf_op jit(solution)/shard_map/ppermute | solution.py:309
  38.9 7.2 %collective-permute-start.5 = (bf16[64,768]{1,0:T(8,128)(2,1)S(1)}, bf16[64,768]{1,0:T(8,128)(2,1)S(1)}, u32[]{:S(2)}, u32[]{:S(2)}) collective-permute-start(bf16[64,768]{1,0:T(8,128)(2,1)S(1)} %pad_maximum_fusion.c0), channel_id=1, source_target_pairs={{0,4},{8,12},{16,20},{24,28},{2,6},{10,14},{18,22},{26,30},{4,0},{... | collective-permute-start | bytes 294920 | tf_op jit(solution)/shard_map/ppermute | solution.py:309
  39.5 1.2 %copy-start.4 = (bf16[768,1024]{1,0:T(8,128)(2,1)}, bf16[768,1024]{1,0:T(8,128)(2,1)S(1)}, u32[]{:S(2)}) copy-start(bf16[768,1024]{1,0:T(8,128)(2,1)S(1)} %get-tuple-element.51.turned_ref) | copy-start | bytes 4718596
  45.2 28.6 %copy-start.5 = (bf16[768,1024]{1,0:T(8,128)(2,1)S(1)}, bf16[768,1024]{1,0:T(8,128)(2,1)}, u32[]{:S(2)}) copy-start(bf16[768,1024]{1,0:T(8,128)(2,1)} %copy-done.4) | copy-start | bytes 4718596
  46.4 14.2 %collective-permute-start.10 = (bf16[256,768]{1,0:T(8,128)(2,1)S(1)}, bf16[256,768]{1,0:T(8,128)(2,1)S(1)}, u32[]{:S(2)}, u32[]{:S(2)}) collective-permute-start(bf16[256,768]{1,0:T(8,128)(2,1)S(1)} %get-tuple-element.57.refs_0_), channel_id=1, source_target_pairs={{0,24},{8,0},{16,8},{24,16},{2,26},{10,2},{18,10},{26,18},{4,28},{... | collective-permute-start | bytes 1179656 | tf_op jit(solution)/shard_map/ppermute | solution.py:309
  47.5 13.1 %collective-permute-start.11 = (bf16[256,768]{1,0:T(8,128)(2,1)S(1)}, bf16[256,768]{1,0:T(8,128)(2,1)S(1)}, u32[]{:S(2)}, u32[]{:S(2)}) collective-permute-start(bf16[256,768]{1,0:T(8,128)(2,1)S(1)} %get-tuple-element.57.refs_0_), channel_id=1, source_target_pairs={{0,16},{8,24},{16,0},{24,8},{2,18},{10,26},{18,2},{26,10},{4,20},{... | collective-permute-start | bytes 1179656 | tf_op jit(solution)/shard_map/ppermute | solution.py:309
  48.6 12.0 %collective-permute-start.9 = (bf16[256,768]{1,0:T(8,128)(2,1)S(1)}, bf16[256,768]{1,0:T(8,128)(2,1)}, u32[]{:S(2)}, u32[]{:S(2)}) collective-permute-start(bf16[256,768]{1,0:T(8,128)(2,1)S(1)} %get-tuple-element.57.refs_0_), channel_id=1, source_target_pairs={{0,8},{8,16},{16,24},{24,0},{2,10},{10,18},{18,26},{26,2},{4,12},{... | collective-permute-start | bytes 1179656 | tf_op jit(solution)/shard_map/ppermute | solution.py:309
  48.7 7.6 %collective-permute-start.6 = (s16[1,208,128]{2,1,0:T(8,128)(2,1)S(1)}, s16[1,208,128]{2,1,0:T(8,128)(2,1)S(1)}, u32[]{:S(2)}, u32[]{:S(2)}) collective-permute-start(s16[1,208,128]{2,1,0:T(8,128)(2,1)S(1)} %get-tuple-element.45.own), channel_id=1, source_target_pairs={{0,64},{64,128},{128,192},{192,0},{1,65},{65,129},{129,193},{193,1... | collective-permute-start | bytes 159752 | tf_op jit(solution)/shard_map/ppermute | solution.py:262
  51.7 7.0 %collective-permute-start.7 = (s16[1,208,128]{2,1,0:T(8,128)(2,1)S(1)}, s16[1,208,128]{2,1,0:T(8,128)(2,1)S(1)}, u32[]{:S(2)}, u32[]{:S(2)}) collective-permute-start(s16[1,208,128]{2,1,0:T(8,128)(2,1)S(1)} %get-tuple-element.45.own), channel_id=1, source_target_pairs={{0,128},{64,192},{128,0},{192,64},{1,129},{65,193},{129,1},{193,65... | collective-permute-start | bytes 159752 | tf_op jit(solution)/shard_map/ppermute | solution.py:262
  56.3 4.3 %collective-permute-start.8 = (s16[1,208,128]{2,1,0:T(8,128)(2,1)S(1)}, s16[1,208,128]{2,1,0:T(8,128)(2,1)S(1)}, u32[]{:S(2)}, u32[]{:S(2)}) collective-permute-start(s16[1,208,128]{2,1,0:T(8,128)(2,1)S(1)} %get-tuple-element.45.own), channel_id=1, source_target_pairs={{0,192},{64,0},{128,64},{192,128},{1,193},{65,1},{129,65},{193,129... | collective-permute-start | bytes 159752 | tf_op jit(solution)/shard_map/ppermute | solution.py:262
  61.6 18.2 %all-to-all-start.2 = ((s16[8,208,128]{2,1,0:T(8,128)(2,1)}), s16[8,208,128]{2,1,0:T(8,128)(2,1)S(1)}, u32[]{:S(2)}, u32[]{:S(2)}) async-start(s16[8,208,128]{2,1,0:T(8,128)(2,1)} %get-tuple-element.49), calls=%async_computation.2 | async-start | bytes 851968 | tf_op jit(solution)/shard_map/all_to_all | solution.py:295
  67.5 9.2 %collective-permute-start.13 = (bf16[256,768]{1,0:T(8,128)(2,1)S(1)}, bf16[256,768]{1,0:T(8,128)(2,1)S(1)}, u32[]{:S(2)}, u32[]{:S(2)}) collective-permute-start(bf16[256,768]{1,0:T(8,128)(2,1)S(1)} %get-tuple-element.57.refs_0_), channel_id=1, source_target_pairs={{0,32},{32,0},{1,33},{33,1},{2,34},{34,2},{3,35},{35,3},{4,36},{36... | collective-permute-start | bytes 1179656 | tf_op jit(solution)/shard_map/ppermute | solution.py:257
  72.8 3.9 %collective-permute-start.14 = (bf16[256,768]{1,0:T(8,128)(2,1)}, bf16[256,768]{1,0:T(8,128)(2,1)S(1)}, u32[]{:S(2)}, u32[]{:S(2)}) collective-permute-start(bf16[256,768]{1,0:T(8,128)(2,1)} %collective-permute-done.9.refs_1_), channel_id=1, source_target_pairs={{0,32},{32,0},{1,33},{33,1},{2,34},{34,2},{3,35},{35,3},{4,36},{36... | collective-permute-start | bytes 1179656 | tf_op jit(solution)/shard_map/ppermute | solution.py:257
  72.9 3.8 %collective-permute-start.15 = (bf16[256,768]{1,0:T(8,128)(2,1)S(1)}, bf16[256,768]{1,0:T(8,128)(2,1)S(1)}, u32[]{:S(2)}, u32[]{:S(2)}) collective-permute-start(bf16[256,768]{1,0:T(8,128)(2,1)S(1)} %collective-permute-done.10.refs_2_), channel_id=1, source_target_pairs={{0,32},{32,0},{1,33},{33,1},{2,34},{34,2},{3,35},{35,3},{4,36},{36... | collective-permute-start | bytes 1179656 | tf_op jit(solution)/shard_map/ppermute | solution.py:257
  73.4 3.4 %collective-permute-start.16 = (bf16[256,768]{1,0:T(8,128)(2,1)S(1)}, bf16[256,768]{1,0:T(8,128)(2,1)S(1)}, u32[]{:S(2)}, u32[]{:S(2)}) collective-permute-start(bf16[256,768]{1,0:T(8,128)(2,1)S(1)} %collective-permute-done.11.refs_3_), channel_id=1, source_target_pairs={{0,32},{32,0},{1,33},{33,1},{2,34},{34,2},{3,35},{35,3},{4,36},{36... | collective-permute-start | bytes 1179656 | tf_op jit(solution)/shard_map/ppermute | solution.py:257
  73.4 3.3 %collective-permute-start.12 = (f32[32,768]{1,0:T(8,128)S(1)}, f32[32,768]{1,0:T(8,128)S(1)}, u32[]{:S(2)}, u32[]{:S(2)}) collective-permute-start(f32[32,768]{1,0:T(8,128)S(1)} %get-tuple-element.52.own), channel_id=1, source_target_pairs={{0,32},{32,0},{1,33},{33,1},{2,34},{34,2},{3,35},{35,3},{4,36},{36... | collective-permute-start | bytes 294920 | tf_op jit(solution)/shard_map/ppermute | solution.py:257
  79.8 4.8 %collective-permute-start.17 = (s16[8,208,128]{2,1,0:T(8,128)(2,1)S(1)}, s16[8,208,128]{2,1,0:T(8,128)(2,1)S(1)}, u32[]{:S(2)}, u32[]{:S(2)}) collective-permute-start(s16[8,208,128]{2,1,0:T(8,128)(2,1)S(1)} %all-to-all-done.2.refs_0_), channel_id=1, source_target_pairs={{0,32},{32,0},{1,33},{33,1},{2,34},{34,2},{3,35},{35,3},{4,36},{36... | collective-permute-start | bytes 1277960 | tf_op jit(solution)/shard_map/ppermute | solution.py:257
  81.0 8.5 %collective-permute-start.18 = (s16[8,208,128]{2,1,0:T(8,128)(2,1)S(1)}, s16[8,208,128]{2,1,0:T(8,128)(2,1)S(1)}, u32[]{:S(2)}, u32[]{:S(2)}) collective-permute-start(s16[8,208,128]{2,1,0:T(8,128)(2,1)S(1)} %all-to-all-done.2.refs_0_), channel_id=1, source_target_pairs={{0,2},{8,10},{16,18},{24,26},{2,4},{10,12},{18,20},{26,28},{4,6},{... | collective-permute-start | bytes 1277960 | tf_op jit(solution)/shard_map/ppermute | solution.py:309
  81.6 11.7 %collective-permute-start.19 = (s16[8,208,128]{2,1,0:T(8,128)(2,1)S(1)}, s16[8,208,128]{2,1,0:T(8,128)(2,1)S(1)}, u32[]{:S(2)}, u32[]{:S(2)}) collective-permute-start(s16[8,208,128]{2,1,0:T(8,128)(2,1)S(1)} %all-to-all-done.2.refs_0_), channel_id=1, source_target_pairs={{0,6},{8,14},{16,22},{24,30},{2,0},{10,8},{18,16},{26,24},{4,2},{1... | collective-permute-start | bytes 1277960 | tf_op jit(solution)/shard_map/ppermute | solution.py:309
  83.7 13.1 %collective-permute-start.20 = (s16[8,208,128]{2,1,0:T(8,128)(2,1)S(1)}, s16[8,208,128]{2,1,0:T(8,128)(2,1)S(1)}, u32[]{:S(2)}, u32[]{:S(2)}) collective-permute-start(s16[8,208,128]{2,1,0:T(8,128)(2,1)S(1)} %all-to-all-done.2.refs_0_), channel_id=1, source_target_pairs={{0,4},{8,12},{16,20},{24,28},{2,6},{10,14},{18,22},{26,30},{4,0},{... | collective-permute-start | bytes 1277960 | tf_op jit(solution)/shard_map/ppermute | solution.py:309
  93.3 4.1 %collective-permute-start.21 = (s16[8,208,128]{2,1,0:T(8,128)(2,1)S(1)}, s16[8,208,128]{2,1,0:T(8,128)(2,1)S(1)}, u32[]{:S(2)}, u32[]{:S(2)}) collective-permute-start(s16[8,208,128]{2,1,0:T(8,128)(2,1)S(1)} %collective-permute-done.18.refs_0_), channel_id=1, source_target_pairs={{0,32},{32,0},{1,33},{33,1},{2,34},{34,2},{3,35},{35,3},{4,36},{36... | collective-permute-start | bytes 1277960 | tf_op jit(solution)/shard_map/ppermute | solution.py:257
  94.9 2.5 %collective-permute-start.22 = (s16[8,208,128]{2,1,0:T(8,128)(2,1)S(1)}, s16[8,208,128]{2,1,0:T(8,128)(2,1)S(1)}, u32[]{:S(2)}, u32[]{:S(2)}) collective-permute-start(s16[8,208,128]{2,1,0:T(8,128)(2,1)S(1)} %collective-permute-done.19.refs_1_), channel_id=1, source_target_pairs={{0,32},{32,0},{1,33},{33,1},{2,34},{34,2},{3,35},{35,3},{4,36},{36... | collective-permute-start | bytes 1277960 | tf_op jit(solution)/shard_map/ppermute | solution.py:257
  96.8 3.3 %collective-permute-start.23 = (s16[8,208,128]{2,1,0:T(8,128)(2,1)S(1)}, s16[8,208,128]{2,1,0:T(8,128)(2,1)S(1)}, u32[]{:S(2)}, u32[]{:S(2)}) collective-permute-start(s16[8,208,128]{2,1,0:T(8,128)(2,1)S(1)} %collective-permute-done.20.refs_2_), channel_id=1, source_target_pairs={{0,32},{32,0},{1,33},{33,1},{2,34},{34,2},{3,35},{35,3},{4,36},{36... | collective-permute-start | bytes 1277960 | tf_op jit(solution)/shard_map/ppermute | solution.py:257

commit v6 on v5

--- a/solution.py
+++ b/solution.py
@@ -388,13 +388,13 @@
         turned, *current,
         flops=2 * 1024 * n * D, moved=3 << 20,
     )
+    new, least = lax.optimization_barrier((new, least))
     old_min, refined_centers = call(
         old_other_kernel,
         (shape((1, n), f32), shape((2 * HALF, D), f32)),
         place, norms, turned, least, refined, swap(refined, "core"), *current_other,
         flops=2 * 1024 * n * D, moved=3 << 20, smem=1,
     )
-    new, old_min = lax.optimization_barrier((new, old_min))
     new = around(new, 0)
 
     def take(least, *pieces):
@@ -407,7 +407,9 @@
 
     least = jnp.full((8, n), jnp.inf, f32)
     least = take(least, new[0], swap(new[0], "core"))
-    least, new[1], new[2] = lax.optimization_barrier((least, new[1], new[2]))
+    least, old_min, new[1], new[2] = lax.optimization_barrier(
+        (least, old_min, new[1], new[2])
+    )
     swapped = [swap(new[1], "core"), swap(new[2], "core")]
     least = take(least, new[1], new[2])
     least, new[3] = lax.optimization_barrier((least, new[3]))

time: 102 us -> 102 us (level)
  waiting for transfers between devices: 14.2 us -> 12 us
  starting transfers between devices: 42.3 us -> 43.8 us
    ppermute x12, starting transfers between devices: 14 us -> 16.4 us  [swap(): return lax.ppermute(value, axis, [(0, 1), (1, 0)])]
    ppermute x9, waiting for transfers between devices: 7.79 us -> 5.59 us  [around(): parts.append(lax.ppermute(part, ('core', 'y', 'x'), pairs))]
  transfers between devices with their start and end apart: 26 -> 26, of which waited for: 5 -> 4; matrix products, arithmetic and copies ran while one was open for 0% -> 0% of each run, Pallas kernels for 15% -> 16%
where the time goes in v6:
time: 102 us
  starting transfers between devices  43.8 us (43%)
  Pallas kernels  24.5 us (24%)
  blocking collectives  17.4 us (17%)
  waiting for transfers between devices  12 us (12%)
  local copies, waits for them, and re-layouts  3.3 us (3%)
    pallas_call x12, Pallas kernels, call(): pl.pallas_call(kernel, out_shape=out_shape, in_specs=specs, out_specs=tup...  24.5 us
    all_to_all x1, blocking collectives, exchange_four(): lax.all_to_all(value.reshape(4, -1, 128), ('core', 'y', 'x'), 0, 0, axis_...  17.4 us
    ppermute x12, starting transfers between devices, swap(): return lax.ppermute(value, axis, [(0, 1), (1, 0)])  16.4 us
    ppermute x3, starting transfers between devices, around_z(): lax.ppermute(part, 'zh', [(i, (i + k) % 4) for i in range(4)])  10 us
    all_to_all x2, starting transfers between devices, exchange_eight(): lax.all_to_all(value, ('core', 'y', 'x', 'zl'), 0, 0, axis_index_groups=e...  9.76 us
    ppermute x9, starting transfers between devices, around(): parts.append(lax.ppermute(part, ('core', 'y', 'x'), pairs))  7.58 us
    ppermute x9, waiting for transfers between devices, around(): parts.append(lax.ppermute(part, ('core', 'y', 'x'), pairs))  5.59 us
    all_to_all x2, waiting for transfers between devices, exchange_eight(): lax.all_to_all(value, ('core', 'y', 'x', 'zl'), 0, 0, axis_index_groups=e...  4.49 us
  transfers between devices with their start and end apart: 26, of which 4 were waited for; matrix products, arithmetic and copies ran while one was open for 0% of the time, Pallas kernels for 16%

profile of v6, /device:TPU:1, one launch (start us, length us, event | category | flops | bytes accessed | tf_op | source)
XLA Modules:
  0.0 101.9 jit_solution(7071262291908106017)
XLA Ops:
  0.6 3.3 %collective-permute-start.1 = (bf16[1024,768]{1,0:T(8,128)(2,1)}, bf16[1024,768]{1,0:T(8,128)(2,1)S(1)}, u32[]{:S(2)}, u32[]{:S(2)}) collective-permute-start(bf16[1024,768]{1,0:T(8,128)(2,1)} %rows_ref), channel_id=1, source_target_pairs={{0,32},{32,0},{1,33},{33,1},{2,34},{34,2},{3,35},{35,3},{4,36},{36... | collective-permute-start | bytes 4718600 | tf_op jit(solution)/shard_map/ppermute | solution.py:257
  4.0 1.0 collective-permute-start
  5.0 1.4 %copy-done.1 = bf16[1024,768]{1,0:T(8,128)(2,1)S(1)} copy-done((bf16[1024,768]{1,0:T(8,128)(2,1)S(1)}, bf16[1024,768]{1,0:T(8,128)(2,1)}, u32[]{:S(2)}) %copy-start.1) | copy-done | bytes 1572888
  6.4 0.7 copy-done.3
  7.1 2.4 %shard_map.58.own_sums = f32[1024,768]{1,0:T(8,128)S(1)} custom-call(s32[3]{0:T(128)S(1)} %pad_add_fusion.place, s32[1,1024]{1,0:T(1,128)S(1)} %bitcast.11, bf16[1024,768]{1,0:T(8,128)(2,1)S(1)} %copy-done.1), custom_call_target="tpu_custom_call" | custom-call | flops 1610612736 | bytes 5242880 | tf_op jit(solution)/shard_map/pallas_call | solution.py:244
  9.6 3.8 %shard_map.59 = s16[32,208,128]{2,1,0:T(8,128)(2,1)S(1)} custom-call(s32[3]{0:T(128)S(1)} %pad_add_fusion.place, s32[1,1024]{1,0:T(1,128)S(1)} %bitcast.12, s32[1,1024]{1,0:T(1,128)S(1)} %collective-permute-done.labels, f32[1024,768]{1,0:T(8,128)S(1)} %shard_map.58.own_sums, bf16[1024,768]{1,0:T(8,128)(2,1)S(1)} %collective-permute-done.1.rows), custom_call_target="tpu_custom_call" | custom-call | flops 1610612736 | bytes 6291456 | tf_op jit(solution)/shard_map/pallas_call | solution.py:244
  13.5 17.4 %all_to_all.15 = s16[4,1664,128]{2,1,0:T(8,128)(2,1)S(1)} all-to-all(s16[4,1664,128]{2,1,0:T(8,128)(2,1)S(1)} %bitcast.8), channel_id=1, replica_groups={{0,2,4,6},{8,10,12,14},{16,18,20,22},{24,26,28,30},{32,40,48,56},{34,42..., dimensions={0} | all-to-all | bytes 3407872 | tf_op jit(solution)/shard_map/all_to_all | solution.py:289
  30.8 1.6 %shard_map.60 = s16[8,208,128]{2,1,0:T(8,128)(2,1)} custom-call(s16[32,208,128]{2,1,0:T(8,128)(2,1)S(1)} %bitcast.9), custom_call_target="tpu_custom_call" | custom-call | flops 4194304 | bytes 3145728 | tf_op jit(solution)/shard_map/pallas_call | solution.py:244
  32.4 3.9 %all-to-all-start.1 = ((s16[8,208,128]{2,1,0:T(8,128)(2,1)}), s16[8,208,128]{2,1,0:T(8,128)(2,1)S(1)}, u32[]{:S(2)}, u32[]{:S(2)}) async-start(s16[8,208,128]{2,1,0:T(8,128)(2,1)} %shard_map.60), calls=%async_computation.1 | async-start | bytes 851968 | tf_op jit(solution)/shard_map/all_to_all | solution.py:295
  36.6 2.4 %collective-permute-start.4 = (bf16[64,768]{1,0:T(8,128)(2,1)S(1)}, bf16[64,768]{1,0:T(8,128)(2,1)S(1)}, u32[]{:S(2)}, u32[]{:S(2)}) collective-permute-start(bf16[64,768]{1,0:T(8,128)(2,1)S(1)} %pad_maximum_fusion.c0), channel_id=1, source_target_pairs={{0,6},{8,14},{16,22},{24,30},{2,0},{10,8},{18,16},{26,24},{4,2},{1... | collective-permute-start | bytes 294920 | tf_op jit(solution)/shard_map/ppermute | solution.py:309
  39.6 1.2 %copy-done.4 = bf16[768,1024]{1,0:T(8,128)(2,1)} copy-done((bf16[768,1024]{1,0:T(8,128)(2,1)}, bf16[768,1024]{1,0:T(8,128)(2,1)S(1)}, u32[]{:S(2)}) %copy-start.4) | copy-done | bytes 1572888
  40.8 4.5 %all-to-all-done.1.in_ref = s16[8,208,128]{2,1,0:T(8,128)(2,1)S(1)} async-done(((s16[8,208,128]{2,1,0:T(8,128)(2,1)}), s16[8,208,128]{2,1,0:T(8,128)(2,1)S(1)}, u32[]{:S(2)}, u32[]{:S(2)}) %all-to-all-start.1) | async-done | bytes 426016 | tf_op jit(solution)/shard_map/all_to_all | solution.py:295
  45.2 0.9 collective-permute-done.5.c3
  46.5 1.0 %collective-permute-start.10 = (bf16[256,768]{1,0:T(8,128)(2,1)S(1)}, bf16[256,768]{1,0:T(8,128)(2,1)S(1)}, u32[]{:S(2)}, u32[]{:S(2)}) collective-permute-start(bf16[256,768]{1,0:T(8,128)(2,1)S(1)} %get-tuple-element.57.refs_0_), channel_id=1, source_target_pairs={{0,24},{8,0},{16,8},{24,16},{2,26},{10,2},{18,10},{26,18},{4,28},{... | collective-permute-start | bytes 1179656 | tf_op jit(solution)/shard_map/ppermute | solution.py:309
  47.5 1.1 %collective-permute-start.11 = (bf16[256,768]{1,0:T(8,128)(2,1)S(1)}, bf16[256,768]{1,0:T(8,128)(2,1)S(1)}, u32[]{:S(2)}, u32[]{:S(2)}) collective-permute-start(bf16[256,768]{1,0:T(8,128)(2,1)S(1)} %get-tuple-element.57.refs_0_), channel_id=1, source_target_pairs={{0,16},{8,24},{16,0},{24,8},{2,18},{10,26},{18,2},{26,10},{4,20},{... | collective-permute-start | bytes 1179656 | tf_op jit(solution)/shard_map/ppermute | solution.py:309
  48.7 3.0 %collective-permute-start.6 = (s16[1,208,128]{2,1,0:T(8,128)(2,1)S(1)}, s16[1,208,128]{2,1,0:T(8,128)(2,1)S(1)}, u32[]{:S(2)}, u32[]{:S(2)}) collective-permute-start(s16[1,208,128]{2,1,0:T(8,128)(2,1)S(1)} %get-tuple-element.47.own), channel_id=1, source_target_pairs={{0,64},{64,128},{128,192},{192,0},{1,65},{65,129},{129,193},{193,1... | collective-permute-start | bytes 159752 | tf_op jit(solution)/shard_map/ppermute | solution.py:262
  51.7 4.7 %collective-permute-start.7 = (s16[1,208,128]{2,1,0:T(8,128)(2,1)S(1)}, s16[1,208,128]{2,1,0:T(8,128)(2,1)S(1)}, u32[]{:S(2)}, u32[]{:S(2)}) collective-permute-start(s16[1,208,128]{2,1,0:T(8,128)(2,1)S(1)} %get-tuple-element.47.own), channel_id=1, source_target_pairs={{0,128},{64,192},{128,0},{192,64},{1,129},{65,193},{129,1},{193,65... | collective-permute-start | bytes 159752 | tf_op jit(solution)/shard_map/ppermute | solution.py:262
  56.3 2.4 %collective-permute-start.8 = (s16[1,208,128]{2,1,0:T(8,128)(2,1)S(1)}, s16[1,208,128]{2,1,0:T(8,128)(2,1)S(1)}, u32[]{:S(2)}, u32[]{:S(2)}) collective-permute-start(s16[1,208,128]{2,1,0:T(8,128)(2,1)S(1)} %get-tuple-element.47.own), channel_id=1, source_target_pairs={{0,192},{64,0},{128,64},{192,128},{1,193},{65,1},{129,65},{193,129... | collective-permute-start | bytes 159752 | tf_op jit(solution)/shard_map/ppermute | solution.py:262
  58.7 1.9 %collective-permute-done.8.three = s16[1,208,128]{2,1,0:T(8,128)(2,1)S(1)} collective-permute-done((s16[1,208,128]{2,1,0:T(8,128)(2,1)S(1)}, s16[1,208,128]{2,1,0:T(8,128)(2,1)S(1)}, u32[]{:S(2)}, u32[]{:S(2)}) %collective-permute-start.8) | collective-permute-done | bytes 53280 | tf_op jit(solution)/shard_map/ppermute | solution.py:262
  60.6 1.0 shard_map.63
  61.7 5.9 %all-to-all-start.2 = ((s16[8,208,128]{2,1,0:T(8,128)(2,1)}), s16[8,208,128]{2,1,0:T(8,128)(2,1)S(1)}, u32[]{:S(2)}, u32[]{:S(2)}) async-start(s16[8,208,128]{2,1,0:T(8,128)(2,1)} %get-tuple-element.51), calls=%async_computation.2 | async-start | bytes 851968 | tf_op jit(solution)/shard_map/all_to_all | solution.py:295
  67.6 5.3 %collective-permute-start.14 = (bf16[256,768]{1,0:T(8,128)(2,1)S(1)}, bf16[256,768]{1,0:T(8,128)(2,1)}, u32[]{:S(2)}, u32[]{:S(2)}) collective-permute-start(bf16[256,768]{1,0:T(8,128)(2,1)S(1)} %get-tuple-element.57.refs_0_), channel_id=1, source_target_pairs={{0,32},{32,0},{1,33},{33,1},{2,34},{34,2},{3,35},{35,3},{4,36},{36... | collective-permute-start | bytes 1179656 | tf_op jit(solution)/shard_map/ppermute | solution.py:257
  73.9 2.8 %shard_map.64.least_ref = f32[8,1024]{1,0:T(8,128)S(1)} custom-call(bf16[768,1024]{1,0:T(8,128)(2,1)S(1)} %copy-done.5, bf16[256,768]{1,0:T(8,128)(2,1)S(1)} %get-tuple-element.57.refs_0_, bf16[256,768]{1,0:T(8,128)(2,1)} %collective-permute-done.9.refs_1_, bf16[256,768]{1,0:T(8,128)(2,1)S(1)} %collective-permute-done.10.refs_2_, ...), custom_call_target="tpu_custom_call" | custom-call | flops 1610612736 | bytes 3145728 | tf_op jit(solution)/shard_map/pallas_call | solution.py:244
  76.8 4.3 %collective-permute-start.12 = (s16[8,208,128]{2,1,0:T(8,128)(2,1)S(1)}, s16[8,208,128]{2,1,0:T(8,128)(2,1)S(1)}, u32[]{:S(2)}, u32[]{:S(2)}) collective-permute-start(s16[8,208,128]{2,1,0:T(8,128)(2,1)S(1)} %all-to-all-done.2.refs_0_), channel_id=1, source_target_pairs={{0,32},{32,0},{1,33},{33,1},{2,34},{34,2},{3,35},{35,3},{4,36},{36... | collective-permute-start | bytes 1277960 | tf_op jit(solution)/shard_map/ppermute | solution.py:257
  81.0 2.7 %collective-permute-start.19 = (s16[8,208,128]{2,1,0:T(8,128)(2,1)S(1)}, s16[8,208,128]{2,1,0:T(8,128)(2,1)S(1)}, u32[]{:S(2)}, u32[]{:S(2)}) collective-permute-start(s16[8,208,128]{2,1,0:T(8,128)(2,1)S(1)} %all-to-all-done.2.refs_0_), channel_id=1, source_target_pairs={{0,6},{8,14},{16,22},{24,30},{2,0},{10,8},{18,16},{26,24},{4,2},{1... | collective-permute-start | bytes 1277960 | tf_op jit(solution)/shard_map/ppermute | solution.py:309
  83.7 3.8 %shard_map.66 = (f32[1,1024]{1,0:T(1,128)}, f32[64,768]{1,0:T(8,128)}) custom-call(s32[3]{0:T(128)S(1)} %pad_add_fusion.place, f32[1,1024]{1,0:T(1,128)S(1)} %get-tuple-element.62.norms_ref, bf16[768,1024]{1,0:T(8,128)(2,1)S(1)} %copy-done.5, f32[8,1024]{1,0:T(8,128)S(1)} %shard_map.64.least_ref, f32[32,768]{1,0:T(8,128)S(1)} %get-tuple-element.52.own, ...), custom_call_target="tpu_custom_call" | custom-call | flops 1610612736 | bytes 3145728 | tf_op jit(solution)/shard_map/pallas_call | solution.py:244
  87.6 1.9 %shard_map.65.least_ref = f32[8,1024]{1,0:T(8,128)S(1)} custom-call(bf16[768,1024]{1,0:T(8,128)(2,1)S(1)} %copy-done.5, f32[8,1024]{1,0:T(8,128)S(1)} %broadcast_in_dim.3.least_ref, s16[8,208,128]{2,1,0:T(8,128)(2,1)S(1)} %all-to-all-done.2.refs_0_, s16[8,208,128]{2,1,0:T(8,128)(2,1)S(1)} %collective-permute-done.12.refs_1_), custom_call_target="tpu_custom_call" | custom-call | flops 1610612736 | bytes 1048576 | tf_op jit(solution)/shard_map/pallas_call | solution.py:244
  89.5 4.6 %collective-permute-done.18.refs_0_ = s16[8,208,128]{2,1,0:T(8,128)(2,1)S(1)} collective-permute-done((s16[8,208,128]{2,1,0:T(8,128)(2,1)S(1)}, s16[8,208,128]{2,1,0:T(8,128)(2,1)S(1)}, u32[]{:S(2)}, u32[]{:S(2)}) %collective-permute-start.18) | collective-permute-done | bytes 426016 | tf_op jit(solution)/shard_map/ppermute | solution.py:309
  94.1 0.9 collective-permute-start.21
  95.0 1.9 %shard_map.67.least_ref = f32[8,1024]{1,0:T(8,128)S(1)} custom-call(bf16[768,1024]{1,0:T(8,128)(2,1)S(1)} %copy-done.5, f32[8,1024]{1,0:T(8,128)S(1)} %shard_map.65.least_ref, s16[8,208,128]{2,1,0:T(8,128)(2,1)S(1)} %collective-permute-done.18.refs_0_, s16[8,208,128]{2,1,0:T(8,128)(2,1)S(1)} %collective-permute-done.19.refs_1_), custom_call_target="tpu_custom_call" | custom-call | flops 1610612736 | bytes 1048576 | tf_op jit(solution)/shard_map/pallas_call | solution.py:244
  97.5 2.7 %shard_map.68.least_ref = f32[8,1024]{1,0:T(8,128)S(1)} custom-call(bf16[768,1024]{1,0:T(8,128)(2,1)S(1)} %copy-done.5, f32[8,1024]{1,0:T(8,128)S(1)} %shard_map.67.least_ref, s16[8,208,128]{2,1,0:T(8,128)(2,1)S(1)} %collective-permute-done.21.refs_0_, s16[8,208,128]{2,1,0:T(8,128)(2,1)S(1)} %collective-permute-done.22.refs_1_, ...), custom_call_target="tpu_custom_call" | custom-call | flops 2415919104 | bytes 1572864 | tf_op jit(solution)/shard_map/pallas_call | solution.py:244
  100.3 1.7 %shard_map.69 = f32[1,1024]{1,0:T(1,128)} custom-call(bf16[768,1024]{1,0:T(8,128)(2,1)S(1)} %copy-done.5, f32[8,1024]{1,0:T(8,128)S(1)} %shard_map.68.least_ref, f32[1,1024]{1,0:T(1,128)S(1)} %get-tuple-element.62.norms_ref, s16[8,208,128]{2,1,0:T(8,128)(2,1)S(1)} %collective-permute-done.23.piece), custom_call_target="tpu_custom_call" | custom-call | flops 805306368 | bytes 524288 | tf_op jit(solution)/shard_map/pallas_call | solution.py:244
  (49 shorter events, 3.1 us)
Async XLA Ops:
  0.6 3.3 %copy-start = (bf16[64,768]{1,0:T(8,128)(2,1)S(1)}, bf16[64,768]{1,0:T(8,128)(2,1)}, u32[]{:S(2)}) copy-start(bf16[64,768]{1,0:T(8,128)(2,1)} %param.4) | copy-start | bytes 294916
  0.6 8.9 %collective-permute-start.1 = (bf16[1024,768]{1,0:T(8,128)(2,1)}, bf16[1024,768]{1,0:T(8,128)(2,1)S(1)}, u32[]{:S(2)}, u32[]{:S(2)}) collective-permute-start(bf16[1024,768]{1,0:T(8,128)(2,1)} %rows_ref), channel_id=1, source_target_pairs={{0,32},{32,0},{1,33},{33,1},{2,34},{34,2},{3,35},{35,3},{4,36},{36... | collective-permute-start | bytes 4718600 | tf_op jit(solution)/shard_map/ppermute | solution.py:257
  4.0 5.6 %collective-permute-start.2 = (bf16[32,768]{1,0:T(8,128)(2,1)S(1)}, bf16[32,768]{1,0:T(8,128)(2,1)S(1)}, u32[]{:S(2)}, u32[]{:S(2)}) collective-permute-start(bf16[32,768]{1,0:T(8,128)(2,1)S(1)} %constant_dynamic-slice_fusion), channel_id=1, source_target_pairs={{0,1},{1,0},{2,3},{3,2},{4,5},{5,4},{6,7},{7,6},{8,9},{9,8},{10,11... | collective-permute-start | bytes 147464 | tf_op jit(solution)/shard_map/ppermute | solution.py:257
  4.0 5.6 %collective-permute-start = (s32[1,1024]{1,0:T(1,128)}, s32[1,1024]{1,0:T(1,128)S(1)}, u32[]{:S(2)}, u32[]{:S(2)}) collective-permute-start(s32[1,1024]{1,0:T(1,128)} %bitcast.10), channel_id=1, source_target_pairs={{0,32},{32,0},{1,33},{33,1},{2,34},{34,2},{3,35},{35,3},{4,36},{36... | collective-permute-start | bytes 12296 | tf_op jit(solution)/shard_map/ppermute | solution.py:257
  5.0 1.4 %copy-start.1 = (bf16[1024,768]{1,0:T(8,128)(2,1)S(1)}, bf16[1024,768]{1,0:T(8,128)(2,1)}, u32[]{:S(2)}) copy-start(bf16[1024,768]{1,0:T(8,128)(2,1)} %rows_ref) | copy-start | bytes 4718596
  6.4 0.7 copy-start.3
  30.8 8.1 %copy-start.2 = (bf16[1024,768]{1,0:T(8,128)(2,1)S(1)}, bf16[1024,768]{1,0:T(8,128)(2,1)}, u32[]{:S(2)}) copy-start(bf16[1024,768]{1,0:T(8,128)(2,1)} %rows_ref) | copy-start | bytes 4718596
  32.4 12.8 %all-to-all-start.1 = ((s16[8,208,128]{2,1,0:T(8,128)(2,1)}), s16[8,208,128]{2,1,0:T(8,128)(2,1)S(1)}, u32[]{:S(2)}, u32[]{:S(2)}) async-start(s16[8,208,128]{2,1,0:T(8,128)(2,1)} %shard_map.60), calls=%async_computation.1 | async-start | bytes 851968 | tf_op jit(solution)/shard_map/all_to_all | solution.py:295
  36.3 9.0 %collective-permute-start.3 = (bf16[64,768]{1,0:T(8,128)(2,1)S(1)}, bf16[64,768]{1,0:T(8,128)(2,1)S(1)}, u32[]{:S(2)}, u32[]{:S(2)}) collective-permute-start(bf16[64,768]{1,0:T(8,128)(2,1)S(1)} %pad_maximum_fusion.c0), channel_id=1, source_target_pairs={{0,2},{8,10},{16,18},{24,26},{2,4},{10,12},{18,20},{26,28},{4,6},{... | collective-permute-start | bytes 294920 | tf_op jit(solution)/shard_map/ppermute | solution.py:309
  36.6 8.7 %collective-permute-start.4 = (bf16[64,768]{1,0:T(8,128)(2,1)S(1)}, bf16[64,768]{1,0:T(8,128)(2,1)S(1)}, u32[]{:S(2)}, u32[]{:S(2)}) collective-permute-start(bf16[64,768]{1,0:T(8,128)(2,1)S(1)} %pad_maximum_fusion.c0), channel_id=1, source_target_pairs={{0,6},{8,14},{16,22},{24,30},{2,0},{10,8},{18,16},{26,24},{4,2},{1... | collective-permute-start | bytes 294920 | tf_op jit(solution)/shard_map/ppermute | solution.py:309
  38.9 7.2 %collective-permute-start.5 = (bf16[64,768]{1,0:T(8,128)(2,1)S(1)}, bf16[64,768]{1,0:T(8,128)(2,1)S(1)}, u32[]{:S(2)}, u32[]{:S(2)}) collective-permute-start(bf16[64,768]{1,0:T(8,128)(2,1)S(1)} %pad_maximum_fusion.c0), channel_id=1, source_target_pairs={{0,4},{8,12},{16,20},{24,28},{2,6},{10,14},{18,22},{26,30},{4,0},{... | collective-permute-start | bytes 294920 | tf_op jit(solution)/shard_map/ppermute | solution.py:309
  39.6 1.2 %copy-start.4 = (bf16[768,1024]{1,0:T(8,128)(2,1)}, bf16[768,1024]{1,0:T(8,128)(2,1)S(1)}, u32[]{:S(2)}) copy-start(bf16[768,1024]{1,0:T(8,128)(2,1)S(1)} %get-tuple-element.42.turned_ref) | copy-start | bytes 4718596
  45.2 28.7 %copy-start.5 = (bf16[768,1024]{1,0:T(8,128)(2,1)S(1)}, bf16[768,1024]{1,0:T(8,128)(2,1)}, u32[]{:S(2)}) copy-start(bf16[768,1024]{1,0:T(8,128)(2,1)} %copy-done.4) | copy-start | bytes 4718596
  46.5 14.2 %collective-permute-start.10 = (bf16[256,768]{1,0:T(8,128)(2,1)S(1)}, bf16[256,768]{1,0:T(8,128)(2,1)S(1)}, u32[]{:S(2)}, u32[]{:S(2)}) collective-permute-start(bf16[256,768]{1,0:T(8,128)(2,1)S(1)} %get-tuple-element.57.refs_0_), channel_id=1, source_target_pairs={{0,24},{8,0},{16,8},{24,16},{2,26},{10,2},{18,10},{26,18},{4,28},{... | collective-permute-start | bytes 1179656 | tf_op jit(solution)/shard_map/ppermute | solution.py:309
  47.5 13.1 %collective-permute-start.11 = (bf16[256,768]{1,0:T(8,128)(2,1)S(1)}, bf16[256,768]{1,0:T(8,128)(2,1)S(1)}, u32[]{:S(2)}, u32[]{:S(2)}) collective-permute-start(bf16[256,768]{1,0:T(8,128)(2,1)S(1)} %get-tuple-element.57.refs_0_), channel_id=1, source_target_pairs={{0,16},{8,24},{16,0},{24,8},{2,18},{10,26},{18,2},{26,10},{4,20},{... | collective-permute-start | bytes 1179656 | tf_op jit(solution)/shard_map/ppermute | solution.py:309
  48.6 12.0 %collective-permute-start.9 = (bf16[256,768]{1,0:T(8,128)(2,1)S(1)}, bf16[256,768]{1,0:T(8,128)(2,1)}, u32[]{:S(2)}, u32[]{:S(2)}) collective-permute-start(bf16[256,768]{1,0:T(8,128)(2,1)S(1)} %get-tuple-element.57.refs_0_), channel_id=1, source_target_pairs={{0,8},{8,16},{16,24},{24,0},{2,10},{10,18},{18,26},{26,2},{4,12},{... | collective-permute-start | bytes 1179656 | tf_op jit(solution)/shard_map/ppermute | solution.py:309
  48.7 7.7 %collective-permute-start.6 = (s16[1,208,128]{2,1,0:T(8,128)(2,1)S(1)}, s16[1,208,128]{2,1,0:T(8,128)(2,1)S(1)}, u32[]{:S(2)}, u32[]{:S(2)}) collective-permute-start(s16[1,208,128]{2,1,0:T(8,128)(2,1)S(1)} %get-tuple-element.47.own), channel_id=1, source_target_pairs={{0,64},{64,128},{128,192},{192,0},{1,65},{65,129},{129,193},{193,1... | collective-permute-start | bytes 159752 | tf_op jit(solution)/shard_map/ppermute | solution.py:262
  51.7 7.1 %collective-permute-start.7 = (s16[1,208,128]{2,1,0:T(8,128)(2,1)S(1)}, s16[1,208,128]{2,1,0:T(8,128)(2,1)S(1)}, u32[]{:S(2)}, u32[]{:S(2)}) collective-permute-start(s16[1,208,128]{2,1,0:T(8,128)(2,1)S(1)} %get-tuple-element.47.own), channel_id=1, source_target_pairs={{0,128},{64,192},{128,0},{192,64},{1,129},{65,193},{129,1},{193,65... | collective-permute-start | bytes 159752 | tf_op jit(solution)/shard_map/ppermute | solution.py:262
  56.3 4.3 %collective-permute-start.8 = (s16[1,208,128]{2,1,0:T(8,128)(2,1)S(1)}, s16[1,208,128]{2,1,0:T(8,128)(2,1)S(1)}, u32[]{:S(2)}, u32[]{:S(2)}) collective-permute-start(s16[1,208,128]{2,1,0:T(8,128)(2,1)S(1)} %get-tuple-element.47.own), channel_id=1, source_target_pairs={{0,192},{64,0},{128,64},{192,128},{1,193},{65,1},{129,65},{193,129... | collective-permute-start | bytes 159752 | tf_op jit(solution)/shard_map/ppermute | solution.py:262
  61.7 15.1 %all-to-all-start.2 = ((s16[8,208,128]{2,1,0:T(8,128)(2,1)}), s16[8,208,128]{2,1,0:T(8,128)(2,1)S(1)}, u32[]{:S(2)}, u32[]{:S(2)}) async-start(s16[8,208,128]{2,1,0:T(8,128)(2,1)} %get-tuple-element.51), calls=%async_computation.2 | async-start | bytes 851968 | tf_op jit(solution)/shard_map/all_to_all | solution.py:295
  67.6 13.5 %collective-permute-start.14 = (bf16[256,768]{1,0:T(8,128)(2,1)S(1)}, bf16[256,768]{1,0:T(8,128)(2,1)}, u32[]{:S(2)}, u32[]{:S(2)}) collective-permute-start(bf16[256,768]{1,0:T(8,128)(2,1)S(1)} %get-tuple-element.57.refs_0_), channel_id=1, source_target_pairs={{0,32},{32,0},{1,33},{33,1},{2,34},{34,2},{3,35},{35,3},{4,36},{36... | collective-permute-start | bytes 1179656 | tf_op jit(solution)/shard_map/ppermute | solution.py:257
  72.9 8.2 %collective-permute-start.15 = (bf16[256,768]{1,0:T(8,128)(2,1)}, bf16[256,768]{1,0:T(8,128)(2,1)}, u32[]{:S(2)}, u32[]{:S(2)}) collective-permute-start(bf16[256,768]{1,0:T(8,128)(2,1)} %collective-permute-done.9.refs_1_), channel_id=1, source_target_pairs={{0,32},{32,0},{1,33},{33,1},{2,34},{34,2},{3,35},{35,3},{4,36},{36... | collective-permute-start | bytes 1179656 | tf_op jit(solution)/shard_map/ppermute | solution.py:257
  73.0 3.8 %collective-permute-start.13 = (f32[32,768]{1,0:T(8,128)S(1)}, f32[32,768]{1,0:T(8,128)S(1)}, u32[]{:S(2)}, u32[]{:S(2)}) collective-permute-start(f32[32,768]{1,0:T(8,128)S(1)} %get-tuple-element.52.own), channel_id=1, source_target_pairs={{0,32},{32,0},{1,33},{33,1},{2,34},{34,2},{3,35},{35,3},{4,36},{36... | collective-permute-start | bytes 294920 | tf_op jit(solution)/shard_map/ppermute | solution.py:257
  73.4 10.3 %collective-permute-start.16 = (bf16[256,768]{1,0:T(8,128)(2,1)S(1)}, bf16[256,768]{1,0:T(8,128)(2,1)}, u32[]{:S(2)}, u32[]{:S(2)}) collective-permute-start(bf16[256,768]{1,0:T(8,128)(2,1)S(1)} %collective-permute-done.10.refs_2_), channel_id=1, source_target_pairs={{0,32},{32,0},{1,33},{33,1},{2,34},{34,2},{3,35},{35,3},{4,36},{36... | collective-permute-start | bytes 1179656 | tf_op jit(solution)/shard_map/ppermute | solution.py:257
  73.5 10.3 %collective-permute-start.17 = (bf16[256,768]{1,0:T(8,128)(2,1)S(1)}, bf16[256,768]{1,0:T(8,128)(2,1)}, u32[]{:S(2)}, u32[]{:S(2)}) collective-permute-start(bf16[256,768]{1,0:T(8,128)(2,1)S(1)} %collective-permute-done.11.refs_3_), channel_id=1, source_target_pairs={{0,32},{32,0},{1,33},{33,1},{2,34},{34,2},{3,35},{35,3},{4,36},{36... | collective-permute-start | bytes 1179656 | tf_op jit(solution)/shard_map/ppermute | solution.py:257
  76.8 10.8 %collective-permute-start.12 = (s16[8,208,128]{2,1,0:T(8,128)(2,1)S(1)}, s16[8,208,128]{2,1,0:T(8,128)(2,1)S(1)}, u32[]{:S(2)}, u32[]{:S(2)}) collective-permute-start(s16[8,208,128]{2,1,0:T(8,128)(2,1)S(1)} %all-to-all-done.2.refs_0_), channel_id=1, source_target_pairs={{0,32},{32,0},{1,33},{33,1},{2,34},{34,2},{3,35},{35,3},{4,36},{36... | collective-permute-start | bytes 1277960 | tf_op jit(solution)/shard_map/ppermute | solution.py:257
  81.0 13.0 %collective-permute-start.18 = (s16[8,208,128]{2,1,0:T(8,128)(2,1)S(1)}, s16[8,208,128]{2,1,0:T(8,128)(2,1)S(1)}, u32[]{:S(2)}, u32[]{:S(2)}) collective-permute-start(s16[8,208,128]{2,1,0:T(8,128)(2,1)S(1)} %all-to-all-done.2.refs_0_), channel_id=1, source_target_pairs={{0,2},{8,10},{16,18},{24,26},{2,4},{10,12},{18,20},{26,28},{4,6},{... | collective-permute-start | bytes 1277960 | tf_op jit(solution)/shard_map/ppermute | solution.py:309
  81.0 13.0 %collective-permute-start.19 = (s16[8,208,128]{2,1,0:T(8,128)(2,1)S(1)}, s16[8,208,128]{2,1,0:T(8,128)(2,1)S(1)}, u32[]{:S(2)}, u32[]{:S(2)}) collective-permute-start(s16[8,208,128]{2,1,0:T(8,128)(2,1)S(1)} %all-to-all-done.2.refs_0_), channel_id=1, source_target_pairs={{0,6},{8,14},{16,22},{24,30},{2,0},{10,8},{18,16},{26,24},{4,2},{1... | collective-permute-start | bytes 1277960 | tf_op jit(solution)/shard_map/ppermute | solution.py:309
  83.7 13.2 %collective-permute-start.20 = (s16[8,208,128]{2,1,0:T(8,128)(2,1)S(1)}, s16[8,208,128]{2,1,0:T(8,128)(2,1)S(1)}, u32[]{:S(2)}, u32[]{:S(2)}) collective-permute-start(s16[8,208,128]{2,1,0:T(8,128)(2,1)S(1)} %all-to-all-done.2.refs_0_), channel_id=1, source_target_pairs={{0,4},{8,12},{16,20},{24,28},{2,6},{10,14},{18,22},{26,30},{4,0},{... | collective-permute-start | bytes 1277960 | tf_op jit(solution)/shard_map/ppermute | solution.py:309
  94.1 3.4 %collective-permute-start.21 = (s16[8,208,128]{2,1,0:T(8,128)(2,1)S(1)}, s16[8,208,128]{2,1,0:T(8,128)(2,1)S(1)}, u32[]{:S(2)}, u32[]{:S(2)}) collective-permute-start(s16[8,208,128]{2,1,0:T(8,128)(2,1)S(1)} %collective-permute-done.18.refs_0_), channel_id=1, source_target_pairs={{0,32},{32,0},{1,33},{33,1},{2,34},{34,2},{3,35},{35,3},{4,36},{36... | collective-permute-start | bytes 1277960 | tf_op jit(solution)/shard_map/ppermute | solution.py:257
  95.0 2.5 %collective-permute-start.22 = (s16[8,208,128]{2,1,0:T(8,128)(2,1)S(1)}, s16[8,208,128]{2,1,0:T(8,128)(2,1)S(1)}, u32[]{:S(2)}, u32[]{:S(2)}) collective-permute-start(s16[8,208,128]{2,1,0:T(8,128)(2,1)S(1)} %collective-permute-done.19.refs_1_), channel_id=1, source_target_pairs={{0,32},{32,0},{1,33},{33,1},{2,34},{34,2},{3,35},{35,3},{4,36},{36... | collective-permute-start | bytes 1277960 | tf_op jit(solution)/shard_map/ppermute | solution.py:257
  96.9 3.3 %collective-permute-start.23 = (s16[8,208,128]{2,1,0:T(8,128)(2,1)S(1)}, s16[8,208,128]{2,1,0:T(8,128)(2,1)S(1)}, u32[]{:S(2)}, u32[]{:S(2)}) collective-permute-start(s16[8,208,128]{2,1,0:T(8,128)(2,1)S(1)} %collective-permute-done.20.refs_2_), channel_id=1, source_target_pairs={{0,32},{32,0},{1,33},{33,1},{2,34},{34,2},{3,35},{35,3},{4,36},{36... | collective-permute-start | bytes 1277960 | tf_op jit(solution)/shard_map/ppermute | solution.py:257

commit v7 on v6

--- a/solution.py
+++ b/solution.py
@@ -297,17 +297,18 @@
     )
 
 
+def send(part, turn, k):
+    pairs = []
+    for core in range(2):
+        for a in range(4):
+            for b in range(4):
+                to = ((a + k) % 4, b) if turn == 0 else (a, (b + k) % 4)
+                pairs.append((spot(core, a, b, 0) // 2, spot(core, *to, 0) // 2))
+    return lax.ppermute(part, ("core", "y", "x"), pairs)
+
+
 def around(part, turn):
-    parts = [part]
-    for k in (1, 3, 2):
-        pairs = []
-        for core in range(2):
-            for a in range(4):
-                for b in range(4):
-                    to = ((a + k) % 4, b) if turn == 0 else (a, (b + k) % 4)
-                    pairs.append((spot(core, a, b, 0) // 2, spot(core, *to, 0) // 2))
-        parts.append(lax.ppermute(part, ("core", "y", "x"), pairs))
-    return parts
+    return [part] + [send(part, turn, k) for k in (1, 3, 2)]
 
 
 def after(first, values):
@@ -395,8 +396,6 @@
         place, norms, turned, least, refined, swap(refined, "core"), *current_other,
         flops=2 * 1024 * n * D, moved=3 << 20, smem=1,
     )
-    new = around(new, 0)
-
     def take(least, *pieces):
         return call(
             new_kernel,
@@ -405,16 +404,18 @@
             flops=4 * TILE * n * D * len(pieces), moved=len(pieces) << 19,
         )
 
+    near = [send(new, 0, 1), send(new, 0, 3)]
+    (far,) = after(old_min, (new,))
+    far = send(far, 0, 2)
     least = jnp.full((8, n), jnp.inf, f32)
-    least = take(least, new[0], swap(new[0], "core"))
-    least, old_min, new[1], new[2] = lax.optimization_barrier(
-        (least, old_min, new[1], new[2])
-    )
-    swapped = [swap(new[1], "core"), swap(new[2], "core")]
-    least = take(least, new[1], new[2])
-    least, new[3] = lax.optimization_barrier((least, new[3]))
-    last = swap(new[3], "core")
-    least = take(least, *swapped, new[3])
+    least = take(least, new, swap(new, "core"))
+    least, old_min, *near = lax.optimization_barrier((least, old_min, *near))
+    swapped = [swap(part, "core") for part in near]
+    least = take(least, *near)
+    least = take(least, *swapped)
+    least, far = lax.optimization_barrier((least, far))
+    last = swap(far, "core")
+    least = take(least, far)
     new_min = call(
         last_kernel,
         shape((1, n), f32),

time: 102 us -> 104 us (1.020)
  starting transfers between devices: 43.8 us -> 45.2 us
    pallas_call x12 -> x13, Pallas kernels: 24.5 us -> 24.7 us  [call(): pl.pallas_call(kernel, out_shape=out_shape, in_specs=specs, out_specs=tup...]
  transfers between devices with their start and end apart: 26 -> 26, of which waited for: 4 -> 6; matrix products, arithmetic and copies ran while one was open for 0% -> 0% of each run, Pallas kernels for 16% -> 16%
where the time goes in v7:
time: 104 us
  starting transfers between devices  45.2 us (43%)
  Pallas kernels  24.7 us (24%)
  blocking collectives  17.4 us (17%)
  waiting for transfers between devices  12.1 us (12%)
  local copies, waits for them, and re-layouts  3.3 us (3%)
    pallas_call x13, Pallas kernels, call(): pl.pallas_call(kernel, out_shape=out_shape, in_specs=specs, out_specs=tup...  24.7 us
    all_to_all x1, blocking collectives, exchange_four(): lax.all_to_all(value.reshape(4, -1, 128), ('core', 'y', 'x'), 0, 0, axis_...  17.4 us
    ppermute x12, starting transfers between devices, swap(): return lax.ppermute(value, axis, [(0, 1), (1, 0)])  17.2 us
    ppermute x3, starting transfers between devices, around_z(): lax.ppermute(part, 'zh', [(i, (i + k) % 4) for i in range(4)])  10 us
    all_to_all x2, starting transfers between devices, exchange_eight(): lax.all_to_all(value, ('core', 'y', 'x', 'zl'), 0, 0, axis_index_groups=e...  9.76 us
    ppermute x9, starting transfers between devices, send(): return lax.ppermute(part, ('core', 'y', 'x'), pairs)  8.23 us
    ppermute x9, waiting for transfers between devices, send(): return lax.ppermute(part, ('core', 'y', 'x'), pairs)  5.38 us
    all_to_all x2, waiting for transfers between devices, exchange_eight(): lax.all_to_all(value, ('core', 'y', 'x', 'zl'), 0, 0, axis_index_groups=e...  4.49 us
  transfers between devices with their start and end apart: 26, of which 6 were waited for; matrix products, arithmetic and copies ran while one was open for 0% of the time, Pallas kernels for 16%

profile of v7, /device:TPU:1, one launch (start us, length us, event | category | flops | bytes accessed | tf_op | source)
XLA Modules:
  0.0 103.7 jit_solution(9909174207358517126)
XLA Ops:
  0.6 3.3 %collective-permute-start.1 = (bf16[1024,768]{1,0:T(8,128)(2,1)}, bf16[1024,768]{1,0:T(8,128)(2,1)S(1)}, u32[]{:S(2)}, u32[]{:S(2)}) collective-permute-start(bf16[1024,768]{1,0:T(8,128)(2,1)} %rows_ref), channel_id=1, source_target_pairs={{0,32},{32,0},{1,33},{33,1},{2,34},{34,2},{3,35},{35,3},{4,36},{36... | collective-permute-start | bytes 4718600 | tf_op jit(solution)/shard_map/ppermute | solution.py:257
  4.0 1.0 collective-permute-start
  5.0 1.4 %copy-done.1 = bf16[1024,768]{1,0:T(8,128)(2,1)S(1)} copy-done((bf16[1024,768]{1,0:T(8,128)(2,1)S(1)}, bf16[1024,768]{1,0:T(8,128)(2,1)}, u32[]{:S(2)}) %copy-start.1) | copy-done | bytes 1572888
  7.1 2.4 %shard_map.58.own_sums = f32[1024,768]{1,0:T(8,128)S(1)} custom-call(s32[3]{0:T(128)S(1)} %pad_add_fusion.place, s32[1,1024]{1,0:T(1,128)S(1)} %bitcast.11, bf16[1024,768]{1,0:T(8,128)(2,1)S(1)} %copy-done.1), custom_call_target="tpu_custom_call" | custom-call | flops 1610612736 | bytes 5242880 | tf_op jit(solution)/shard_map/pallas_call | solution.py:244
  9.6 3.8 %shard_map.59 = s16[32,208,128]{2,1,0:T(8,128)(2,1)S(1)} custom-call(s32[3]{0:T(128)S(1)} %pad_add_fusion.place, s32[1,1024]{1,0:T(1,128)S(1)} %bitcast.12, s32[1,1024]{1,0:T(1,128)S(1)} %collective-permute-done.labels, f32[1024,768]{1,0:T(8,128)S(1)} %shard_map.58.own_sums, bf16[1024,768]{1,0:T(8,128)(2,1)S(1)} %collective-permute-done.1.rows), custom_call_target="tpu_custom_call" | custom-call | flops 1610612736 | bytes 6291456 | tf_op jit(solution)/shard_map/pallas_call | solution.py:244
  13.5 17.4 %all_to_all.15 = s16[4,1664,128]{2,1,0:T(8,128)(2,1)S(1)} all-to-all(s16[4,1664,128]{2,1,0:T(8,128)(2,1)S(1)} %bitcast.8), channel_id=1, replica_groups={{0,2,4,6},{8,10,12,14},{16,18,20,22},{24,26,28,30},{32,40,48,56},{34,42..., dimensions={0} | all-to-all | bytes 3407872 | tf_op jit(solution)/shard_map/all_to_all | solution.py:289
  30.8 1.6 %shard_map.60 = s16[8,208,128]{2,1,0:T(8,128)(2,1)} custom-call(s16[32,208,128]{2,1,0:T(8,128)(2,1)S(1)} %bitcast.9), custom_call_target="tpu_custom_call" | custom-call | flops 4194304 | bytes 3145728 | tf_op jit(solution)/shard_map/pallas_call | solution.py:244
  32.4 3.9 %all-to-all-start.1 = ((s16[8,208,128]{2,1,0:T(8,128)(2,1)}), s16[8,208,128]{2,1,0:T(8,128)(2,1)S(1)}, u32[]{:S(2)}, u32[]{:S(2)}) async-start(s16[8,208,128]{2,1,0:T(8,128)(2,1)} %shard_map.60), calls=%async_computation.1 | async-start | bytes 851968 | tf_op jit(solution)/shard_map/all_to_all | solution.py:295
  36.6 2.4 %collective-permute-start.4 = (bf16[64,768]{1,0:T(8,128)(2,1)S(1)}, bf16[64,768]{1,0:T(8,128)(2,1)S(1)}, u32[]{:S(2)}, u32[]{:S(2)}) collective-permute-start(bf16[64,768]{1,0:T(8,128)(2,1)S(1)} %pad_maximum_fusion.c0), channel_id=1, source_target_pairs={{0,6},{8,14},{16,22},{24,30},{2,0},{10,8},{18,16},{26,24},{4,2},{1... | collective-permute-start | bytes 294920 | tf_op jit(solution)/shard_map/ppermute | solution.py:307
  39.6 1.2 %copy-done.4 = bf16[768,1024]{1,0:T(8,128)(2,1)} copy-done((bf16[768,1024]{1,0:T(8,128)(2,1)}, bf16[768,1024]{1,0:T(8,128)(2,1)S(1)}, u32[]{:S(2)}) %copy-start.4) | copy-done | bytes 1572888
  40.8 4.5 %all-to-all-done.1.in_ref = s16[8,208,128]{2,1,0:T(8,128)(2,1)S(1)} async-done(((s16[8,208,128]{2,1,0:T(8,128)(2,1)}), s16[8,208,128]{2,1,0:T(8,128)(2,1)S(1)}, u32[]{:S(2)}, u32[]{:S(2)}) %all-to-all-start.1) | async-done | bytes 426016 | tf_op jit(solution)/shard_map/all_to_all | solution.py:295
  45.2 0.9 collective-permute-done.5.c3
  46.5 1.0 %collective-permute-start.10 = (bf16[256,768]{1,0:T(8,128)(2,1)S(1)}, bf16[256,768]{1,0:T(8,128)(2,1)S(1)}, u32[]{:S(2)}, u32[]{:S(2)}) collective-permute-start(bf16[256,768]{1,0:T(8,128)(2,1)S(1)} %get-tuple-element.58.refs_0_), channel_id=1, source_target_pairs={{0,24},{8,0},{16,8},{24,16},{2,26},{10,2},{18,10},{26,18},{4,28},{... | collective-permute-start | bytes 1179656 | tf_op jit(solution)/shard_map/ppermute | solution.py:307
  47.5 1.1 %collective-permute-start.11 = (bf16[256,768]{1,0:T(8,128)(2,1)S(1)}, bf16[256,768]{1,0:T(8,128)(2,1)S(1)}, u32[]{:S(2)}, u32[]{:S(2)}) collective-permute-start(bf16[256,768]{1,0:T(8,128)(2,1)S(1)} %get-tuple-element.58.refs_0_), channel_id=1, source_target_pairs={{0,16},{8,24},{16,0},{24,8},{2,18},{10,26},{18,2},{26,10},{4,20},{... | collective-permute-start | bytes 1179656 | tf_op jit(solution)/shard_map/ppermute | solution.py:307
  48.7 3.0 %collective-permute-start.6 = (s16[1,208,128]{2,1,0:T(8,128)(2,1)S(1)}, s16[1,208,128]{2,1,0:T(8,128)(2,1)S(1)}, u32[]{:S(2)}, u32[]{:S(2)}) collective-permute-start(s16[1,208,128]{2,1,0:T(8,128)(2,1)S(1)} %get-tuple-element.48.own), channel_id=1, source_target_pairs={{0,64},{64,128},{128,192},{192,0},{1,65},{65,129},{129,193},{193,1... | collective-permute-start | bytes 159752 | tf_op jit(solution)/shard_map/ppermute | solution.py:262
  51.7 4.7 %collective-permute-start.7 = (s16[1,208,128]{2,1,0:T(8,128)(2,1)S(1)}, s16[1,208,128]{2,1,0:T(8,128)(2,1)S(1)}, u32[]{:S(2)}, u32[]{:S(2)}) collective-permute-start(s16[1,208,128]{2,1,0:T(8,128)(2,1)S(1)} %get-tuple-element.48.own), channel_id=1, source_target_pairs={{0,128},{64,192},{128,0},{192,64},{1,129},{65,193},{129,1},{193,65... | collective-permute-start | bytes 159752 | tf_op jit(solution)/shard_map/ppermute | solution.py:262
  56.3 2.4 %collective-permute-start.8 = (s16[1,208,128]{2,1,0:T(8,128)(2,1)S(1)}, s16[1,208,128]{2,1,0:T(8,128)(2,1)S(1)}, u32[]{:S(2)}, u32[]{:S(2)}) collective-permute-start(s16[1,208,128]{2,1,0:T(8,128)(2,1)S(1)} %get-tuple-element.48.own), channel_id=1, source_target_pairs={{0,192},{64,0},{128,64},{192,128},{1,193},{65,1},{129,65},{193,129... | collective-permute-start | bytes 159752 | tf_op jit(solution)/shard_map/ppermute | solution.py:262
  58.7 1.9 %collective-permute-done.8.three = s16[1,208,128]{2,1,0:T(8,128)(2,1)S(1)} collective-permute-done((s16[1,208,128]{2,1,0:T(8,128)(2,1)S(1)}, s16[1,208,128]{2,1,0:T(8,128)(2,1)S(1)}, u32[]{:S(2)}, u32[]{:S(2)}) %collective-permute-start.8) | collective-permute-done | bytes 53280 | tf_op jit(solution)/shard_map/ppermute | solution.py:262
  60.6 1.0 shard_map.63
  61.7 5.9 %all-to-all-start.2 = ((s16[8,208,128]{2,1,0:T(8,128)(2,1)}), s16[8,208,128]{2,1,0:T(8,128)(2,1)S(1)}, u32[]{:S(2)}, u32[]{:S(2)}) async-start(s16[8,208,128]{2,1,0:T(8,128)(2,1)} %get-tuple-element.52), calls=%async_computation.2 | async-start | bytes 851968 | tf_op jit(solution)/shard_map/all_to_all | solution.py:295
  67.6 5.3 %collective-permute-start.14 = (bf16[256,768]{1,0:T(8,128)(2,1)S(1)}, bf16[256,768]{1,0:T(8,128)(2,1)}, u32[]{:S(2)}, u32[]{:S(2)}) collective-permute-start(bf16[256,768]{1,0:T(8,128)(2,1)S(1)} %get-tuple-element.58.refs_0_), channel_id=1, source_target_pairs={{0,32},{32,0},{1,33},{33,1},{2,34},{34,2},{3,35},{35,3},{4,36},{36... | collective-permute-start | bytes 1179656 | tf_op jit(solution)/shard_map/ppermute | solution.py:257
  73.9 2.8 %shard_map.64.least_ref = f32[8,1024]{1,0:T(8,128)S(1)} custom-call(bf16[768,1024]{1,0:T(8,128)(2,1)S(1)} %copy-done.5, bf16[256,768]{1,0:T(8,128)(2,1)S(1)} %get-tuple-element.58.refs_0_, bf16[256,768]{1,0:T(8,128)(2,1)} %collective-permute-done.9.refs_1_, bf16[256,768]{1,0:T(8,128)(2,1)S(1)} %collective-permute-done.10.refs_2_, ...), custom_call_target="tpu_custom_call" | custom-call | flops 1610612736 | bytes 3145728 | tf_op jit(solution)/shard_map/pallas_call | solution.py:244
  76.8 4.3 %collective-permute-start.12 = (s16[8,208,128]{2,1,0:T(8,128)(2,1)S(1)}, s16[8,208,128]{2,1,0:T(8,128)(2,1)S(1)}, u32[]{:S(2)}, u32[]{:S(2)}) collective-permute-start(s16[8,208,128]{2,1,0:T(8,128)(2,1)S(1)} %all-to-all-done.2.refs_0_), channel_id=1, source_target_pairs={{0,32},{32,0},{1,33},{33,1},{2,34},{34,2},{3,35},{35,3},{4,36},{36... | collective-permute-start | bytes 1277960 | tf_op jit(solution)/shard_map/ppermute | solution.py:257
  81.0 2.7 %collective-permute-start.19 = (s16[8,208,128]{2,1,0:T(8,128)(2,1)S(1)}, s16[8,208,128]{2,1,0:T(8,128)(2,1)S(1)}, u32[]{:S(2)}, u32[]{:S(2)}) collective-permute-start(s16[8,208,128]{2,1,0:T(8,128)(2,1)S(1)} %all-to-all-done.2.refs_0_), channel_id=1, source_target_pairs={{0,6},{8,14},{16,22},{24,30},{2,0},{10,8},{18,16},{26,24},{4,2},{1... | collective-permute-start | bytes 1277960 | tf_op jit(solution)/shard_map/ppermute | solution.py:307
  83.7 3.8 %shard_map.66 = (f32[1,1024]{1,0:T(1,128)}, f32[64,768]{1,0:T(8,128)}) custom-call(s32[3]{0:T(128)S(1)} %pad_add_fusion.place, f32[1,1024]{1,0:T(1,128)S(1)} %get-tuple-element.63.norms_ref, bf16[768,1024]{1,0:T(8,128)(2,1)S(1)} %copy-done.5, f32[8,1024]{1,0:T(8,128)S(1)} %shard_map.64.least_ref, f32[32,768]{1,0:T(8,128)S(1)} %get-tuple-element.53.own, ...), custom_call_target="tpu_custom_call" | custom-call | flops 1610612736 | bytes 3145728 | tf_op jit(solution)/shard_map/pallas_call | solution.py:244
  87.5 1.9 %shard_map.65.least_ref = f32[8,1024]{1,0:T(8,128)S(1)} custom-call(bf16[768,1024]{1,0:T(8,128)(2,1)S(1)} %copy-done.5, f32[8,1024]{1,0:T(8,128)S(1)} %broadcast_in_dim.3.least_ref, s16[8,208,128]{2,1,0:T(8,128)(2,1)S(1)} %all-to-all-done.2.refs_0_, s16[8,208,128]{2,1,0:T(8,128)(2,1)S(1)} %collective-permute-done.12.refs_1_), custom_call_target="tpu_custom_call" | custom-call | flops 1610612736 | bytes 1048576 | tf_op jit(solution)/shard_map/pallas_call | solution.py:244
  91.2 1.9 %shard_map.67.least_ref = f32[8,1024]{1,0:T(8,128)S(1)} custom-call(bf16[768,1024]{1,0:T(8,128)(2,1)S(1)} %copy-done.5, f32[8,1024]{1,0:T(8,128)S(1)} %shard_map.65.least_ref, s16[8,208,128]{2,1,0:T(8,128)(2,1)S(1)} %collective-permute-done.18.refs_0_, s16[8,208,128]{2,1,0:T(8,128)(2,1)S(1)} %collective-permute-done.19.refs_1_), custom_call_target="tpu_custom_call" | custom-call | flops 1610612736 | bytes 1048576 | tf_op jit(solution)/shard_map/pallas_call | solution.py:244
  93.1 1.9 %shard_map.68.least_ref = f32[8,1024]{1,0:T(8,128)S(1)} custom-call(bf16[768,1024]{1,0:T(8,128)(2,1)S(1)} %copy-done.5, f32[8,1024]{1,0:T(8,128)S(1)} %shard_map.67.least_ref, s16[8,208,128]{2,1,0:T(8,128)(2,1)S(1)} %collective-permute-done.20.refs_0_, s16[8,208,128]{2,1,0:T(8,128)(2,1)S(1)} %collective-permute-done.21.refs_1_), custom_call_target="tpu_custom_call" | custom-call | flops 1610612736 | bytes 1048576 | tf_op jit(solution)/shard_map/pallas_call | solution.py:244
  95.0 4.3 %collective-permute-done.22.refs_0_ = s16[8,208,128]{2,1,0:T(8,128)(2,1)S(1)} collective-permute-done((s16[8,208,128]{2,1,0:T(8,128)(2,1)S(1)}, s16[8,208,128]{2,1,0:T(8,128)(2,1)S(1)}, u32[]{:S(2)}, u32[]{:S(2)}) %collective-permute-start.22) | collective-permute-done | bytes 426016 | tf_op jit(solution)/shard_map/ppermute | solution.py:307
  99.3 1.3 %collective-permute-start.23 = (s16[8,208,128]{2,1,0:T(8,128)(2,1)S(1)}, s16[8,208,128]{2,1,0:T(8,128)(2,1)S(1)}, u32[]{:S(2)}, u32[]{:S(2)}) collective-permute-start(s16[8,208,128]{2,1,0:T(8,128)(2,1)S(1)} %collective-permute-done.22.refs_0_), channel_id=1, source_target_pairs={{0,32},{32,0},{1,33},{33,1},{2,34},{34,2},{3,35},{35,3},{4,36},{36... | collective-permute-start | bytes 1277960 | tf_op jit(solution)/shard_map/ppermute | solution.py:257
  100.6 1.1 %shard_map.69.least_ref = f32[8,1024]{1,0:T(8,128)S(1)} custom-call(bf16[768,1024]{1,0:T(8,128)(2,1)S(1)} %copy-done.5, f32[8,1024]{1,0:T(8,128)S(1)} %shard_map.68.least_ref, s16[8,208,128]{2,1,0:T(8,128)(2,1)S(1)} %collective-permute-done.22.refs_0_), custom_call_target="tpu_custom_call" | custom-call | flops 805306368 | bytes 524288 | tf_op jit(solution)/shard_map/pallas_call | solution.py:244
  102.0 1.7 %shard_map.70 = f32[1,1024]{1,0:T(1,128)} custom-call(bf16[768,1024]{1,0:T(8,128)(2,1)S(1)} %copy-done.5, f32[8,1024]{1,0:T(8,128)S(1)} %shard_map.69.least_ref, f32[1,1024]{1,0:T(1,128)S(1)} %get-tuple-element.63.norms_ref, s16[8,208,128]{2,1,0:T(8,128)(2,1)S(1)} %collective-permute-done.23.piece), custom_call_target="tpu_custom_call" | custom-call | flops 805306368 | bytes 524288 | tf_op jit(solution)/shard_map/pallas_call | solution.py:244
  (50 shorter events, 5.2 us)
Async XLA Ops:
  0.6 3.3 %copy-start = (bf16[64,768]{1,0:T(8,128)(2,1)S(1)}, bf16[64,768]{1,0:T(8,128)(2,1)}, u32[]{:S(2)}) copy-start(bf16[64,768]{1,0:T(8,128)(2,1)} %param.4) | copy-start | bytes 294916
  0.6 8.9 %collective-permute-start.1 = (bf16[1024,768]{1,0:T(8,128)(2,1)}, bf16[1024,768]{1,0:T(8,128)(2,1)S(1)}, u32[]{:S(2)}, u32[]{:S(2)}) collective-permute-start(bf16[1024,768]{1,0:T(8,128)(2,1)} %rows_ref), channel_id=1, source_target_pairs={{0,32},{32,0},{1,33},{33,1},{2,34},{34,2},{3,35},{35,3},{4,36},{36... | collective-permute-start | bytes 4718600 | tf_op jit(solution)/shard_map/ppermute | solution.py:257
  4.0 5.6 %collective-permute-start.2 = (bf16[32,768]{1,0:T(8,128)(2,1)S(1)}, bf16[32,768]{1,0:T(8,128)(2,1)S(1)}, u32[]{:S(2)}, u32[]{:S(2)}) collective-permute-start(bf16[32,768]{1,0:T(8,128)(2,1)S(1)} %constant_dynamic-slice_fusion), channel_id=1, source_target_pairs={{0,1},{1,0},{2,3},{3,2},{4,5},{5,4},{6,7},{7,6},{8,9},{9,8},{10,11... | collective-permute-start | bytes 147464 | tf_op jit(solution)/shard_map/ppermute | solution.py:257
  4.0 5.6 %collective-permute-start = (s32[1,1024]{1,0:T(1,128)}, s32[1,1024]{1,0:T(1,128)S(1)}, u32[]{:S(2)}, u32[]{:S(2)}) collective-permute-start(s32[1,1024]{1,0:T(1,128)} %bitcast.10), channel_id=1, source_target_pairs={{0,32},{32,0},{1,33},{33,1},{2,34},{34,2},{3,35},{35,3},{4,36},{36... | collective-permute-start | bytes 12296 | tf_op jit(solution)/shard_map/ppermute | solution.py:257
  5.0 1.4 %copy-start.1 = (bf16[1024,768]{1,0:T(8,128)(2,1)S(1)}, bf16[1024,768]{1,0:T(8,128)(2,1)}, u32[]{:S(2)}) copy-start(bf16[1024,768]{1,0:T(8,128)(2,1)} %rows_ref) | copy-start | bytes 4718596
  6.4 0.7 copy-start.3
  30.8 8.1 %copy-start.2 = (bf16[1024,768]{1,0:T(8,128)(2,1)S(1)}, bf16[1024,768]{1,0:T(8,128)(2,1)}, u32[]{:S(2)}) copy-start(bf16[1024,768]{1,0:T(8,128)(2,1)} %rows_ref) | copy-start | bytes 4718596
  32.4 12.8 %all-to-all-start.1 = ((s16[8,208,128]{2,1,0:T(8,128)(2,1)}), s16[8,208,128]{2,1,0:T(8,128)(2,1)S(1)}, u32[]{:S(2)}, u32[]{:S(2)}) async-start(s16[8,208,128]{2,1,0:T(8,128)(2,1)} %shard_map.60), calls=%async_computation.1 | async-start | bytes 851968 | tf_op jit(solution)/shard_map/all_to_all | solution.py:295
  36.3 9.0 %collective-permute-start.3 = (bf16[64,768]{1,0:T(8,128)(2,1)S(1)}, bf16[64,768]{1,0:T(8,128)(2,1)S(1)}, u32[]{:S(2)}, u32[]{:S(2)}) collective-permute-start(bf16[64,768]{1,0:T(8,128)(2,1)S(1)} %pad_maximum_fusion.c0), channel_id=1, source_target_pairs={{0,2},{8,10},{16,18},{24,26},{2,4},{10,12},{18,20},{26,28},{4,6},{... | collective-permute-start | bytes 294920 | tf_op jit(solution)/shard_map/ppermute | solution.py:307
  36.6 8.7 %collective-permute-start.4 = (bf16[64,768]{1,0:T(8,128)(2,1)S(1)}, bf16[64,768]{1,0:T(8,128)(2,1)S(1)}, u32[]{:S(2)}, u32[]{:S(2)}) collective-permute-start(bf16[64,768]{1,0:T(8,128)(2,1)S(1)} %pad_maximum_fusion.c0), channel_id=1, source_target_pairs={{0,6},{8,14},{16,22},{24,30},{2,0},{10,8},{18,16},{26,24},{4,2},{1... | collective-permute-start | bytes 294920 | tf_op jit(solution)/shard_map/ppermute | solution.py:307
  38.9 7.2 %collective-permute-start.5 = (bf16[64,768]{1,0:T(8,128)(2,1)S(1)}, bf16[64,768]{1,0:T(8,128)(2,1)S(1)}, u32[]{:S(2)}, u32[]{:S(2)}) collective-permute-start(bf16[64,768]{1,0:T(8,128)(2,1)S(1)} %pad_maximum_fusion.c0), channel_id=1, source_target_pairs={{0,4},{8,12},{16,20},{24,28},{2,6},{10,14},{18,22},{26,30},{4,0},{... | collective-permute-start | bytes 294920 | tf_op jit(solution)/shard_map/ppermute | solution.py:307
  39.6 1.2 %copy-start.4 = (bf16[768,1024]{1,0:T(8,128)(2,1)}, bf16[768,1024]{1,0:T(8,128)(2,1)S(1)}, u32[]{:S(2)}) copy-start(bf16[768,1024]{1,0:T(8,128)(2,1)S(1)} %get-tuple-element.43.turned_ref) | copy-start | bytes 4718596
  45.2 28.7 %copy-start.5 = (bf16[768,1024]{1,0:T(8,128)(2,1)S(1)}, bf16[768,1024]{1,0:T(8,128)(2,1)}, u32[]{:S(2)}) copy-start(bf16[768,1024]{1,0:T(8,128)(2,1)} %copy-done.4) | copy-start | bytes 4718596
  46.5 14.2 %collective-permute-start.10 = (bf16[256,768]{1,0:T(8,128)(2,1)S(1)}, bf16[256,768]{1,0:T(8,128)(2,1)S(1)}, u32[]{:S(2)}, u32[]{:S(2)}) collective-permute-start(bf16[256,768]{1,0:T(8,128)(2,1)S(1)} %get-tuple-element.58.refs_0_), channel_id=1, source_target_pairs={{0,24},{8,0},{16,8},{24,16},{2,26},{10,2},{18,10},{26,18},{4,28},{... | collective-permute-start | bytes 1179656 | tf_op jit(solution)/shard_map/ppermute | solution.py:307
  47.5 13.1 %collective-permute-start.11 = (bf16[256,768]{1,0:T(8,128)(2,1)S(1)}, bf16[256,768]{1,0:T(8,128)(2,1)S(1)}, u32[]{:S(2)}, u32[]{:S(2)}) collective-permute-start(bf16[256,768]{1,0:T(8,128)(2,1)S(1)} %get-tuple-element.58.refs_0_), channel_id=1, source_target_pairs={{0,16},{8,24},{16,0},{24,8},{2,18},{10,26},{18,2},{26,10},{4,20},{... | collective-permute-start | bytes 1179656 | tf_op jit(solution)/shard_map/ppermute | solution.py:307
  48.6 12.0 %collective-permute-start.9 = (bf16[256,768]{1,0:T(8,128)(2,1)S(1)}, bf16[256,768]{1,0:T(8,128)(2,1)}, u32[]{:S(2)}, u32[]{:S(2)}) collective-permute-start(bf16[256,768]{1,0:T(8,128)(2,1)S(1)} %get-tuple-element.58.refs_0_), channel_id=1, source_target_pairs={{0,8},{8,16},{16,24},{24,0},{2,10},{10,18},{18,26},{26,2},{4,12},{... | collective-permute-start | bytes 1179656 | tf_op jit(solution)/shard_map/ppermute | solution.py:307
  48.7 7.7 %collective-permute-start.6 = (s16[1,208,128]{2,1,0:T(8,128)(2,1)S(1)}, s16[1,208,128]{2,1,0:T(8,128)(2,1)S(1)}, u32[]{:S(2)}, u32[]{:S(2)}) collective-permute-start(s16[1,208,128]{2,1,0:T(8,128)(2,1)S(1)} %get-tuple-element.48.own), channel_id=1, source_target_pairs={{0,64},{64,128},{128,192},{192,0},{1,65},{65,129},{129,193},{193,1... | collective-permute-start | bytes 159752 | tf_op jit(solution)/shard_map/ppermute | solution.py:262
  51.7 7.1 %collective-permute-start.7 = (s16[1,208,128]{2,1,0:T(8,128)(2,1)S(1)}, s16[1,208,128]{2,1,0:T(8,128)(2,1)S(1)}, u32[]{:S(2)}, u32[]{:S(2)}) collective-permute-start(s16[1,208,128]{2,1,0:T(8,128)(2,1)S(1)} %get-tuple-element.48.own), channel_id=1, source_target_pairs={{0,128},{64,192},{128,0},{192,64},{1,129},{65,193},{129,1},{193,65... | collective-permute-start | bytes 159752 | tf_op jit(solution)/shard_map/ppermute | solution.py:262
  56.3 4.3 %collective-permute-start.8 = (s16[1,208,128]{2,1,0:T(8,128)(2,1)S(1)}, s16[1,208,128]{2,1,0:T(8,128)(2,1)S(1)}, u32[]{:S(2)}, u32[]{:S(2)}) collective-permute-start(s16[1,208,128]{2,1,0:T(8,128)(2,1)S(1)} %get-tuple-element.48.own), channel_id=1, source_target_pairs={{0,192},{64,0},{128,64},{192,128},{1,193},{65,1},{129,65},{193,129... | collective-permute-start | bytes 159752 | tf_op jit(solution)/shard_map/ppermute | solution.py:262
  61.7 15.1 %all-to-all-start.2 = ((s16[8,208,128]{2,1,0:T(8,128)(2,1)}), s16[8,208,128]{2,1,0:T(8,128)(2,1)S(1)}, u32[]{:S(2)}, u32[]{:S(2)}) async-start(s16[8,208,128]{2,1,0:T(8,128)(2,1)} %get-tuple-element.52), calls=%async_computation.2 | async-start | bytes 851968 | tf_op jit(solution)/shard_map/all_to_all | solution.py:295
  67.6 13.5 %collective-permute-start.14 = (bf16[256,768]{1,0:T(8,128)(2,1)S(1)}, bf16[256,768]{1,0:T(8,128)(2,1)}, u32[]{:S(2)}, u32[]{:S(2)}) collective-permute-start(bf16[256,768]{1,0:T(8,128)(2,1)S(1)} %get-tuple-element.58.refs_0_), channel_id=1, source_target_pairs={{0,32},{32,0},{1,33},{33,1},{2,34},{34,2},{3,35},{35,3},{4,36},{36... | collective-permute-start | bytes 1179656 | tf_op jit(solution)/shard_map/ppermute | solution.py:257
  72.9 8.2 %collective-permute-start.15 = (bf16[256,768]{1,0:T(8,128)(2,1)}, bf16[256,768]{1,0:T(8,128)(2,1)}, u32[]{:S(2)}, u32[]{:S(2)}) collective-permute-start(bf16[256,768]{1,0:T(8,128)(2,1)} %collective-permute-done.9.refs_1_), channel_id=1, source_target_pairs={{0,32},{32,0},{1,33},{33,1},{2,34},{34,2},{3,35},{35,3},{4,36},{36... | collective-permute-start | bytes 1179656 | tf_op jit(solution)/shard_map/ppermute | solution.py:257
  73.0 3.8 %collective-permute-start.13 = (f32[32,768]{1,0:T(8,128)S(1)}, f32[32,768]{1,0:T(8,128)S(1)}, u32[]{:S(2)}, u32[]{:S(2)}) collective-permute-start(f32[32,768]{1,0:T(8,128)S(1)} %get-tuple-element.53.own), channel_id=1, source_target_pairs={{0,32},{32,0},{1,33},{33,1},{2,34},{34,2},{3,35},{35,3},{4,36},{36... | collective-permute-start | bytes 294920 | tf_op jit(solution)/shard_map/ppermute | solution.py:257
  73.4 10.3 %collective-permute-start.16 = (bf16[256,768]{1,0:T(8,128)(2,1)S(1)}, bf16[256,768]{1,0:T(8,128)(2,1)}, u32[]{:S(2)}, u32[]{:S(2)}) collective-permute-start(bf16[256,768]{1,0:T(8,128)(2,1)S(1)} %collective-permute-done.10.refs_2_), channel_id=1, source_target_pairs={{0,32},{32,0},{1,33},{33,1},{2,34},{34,2},{3,35},{35,3},{4,36},{36... | collective-permute-start | bytes 1179656 | tf_op jit(solution)/shard_map/ppermute | solution.py:257
  73.5 10.2 %collective-permute-start.17 = (bf16[256,768]{1,0:T(8,128)(2,1)S(1)}, bf16[256,768]{1,0:T(8,128)(2,1)}, u32[]{:S(2)}, u32[]{:S(2)}) collective-permute-start(bf16[256,768]{1,0:T(8,128)(2,1)S(1)} %collective-permute-done.11.refs_3_), channel_id=1, source_target_pairs={{0,32},{32,0},{1,33},{33,1},{2,34},{34,2},{3,35},{35,3},{4,36},{36... | collective-permute-start | bytes 1179656 | tf_op jit(solution)/shard_map/ppermute | solution.py:257
  76.8 10.8 %collective-permute-start.12 = (s16[8,208,128]{2,1,0:T(8,128)(2,1)S(1)}, s16[8,208,128]{2,1,0:T(8,128)(2,1)S(1)}, u32[]{:S(2)}, u32[]{:S(2)}) collective-permute-start(s16[8,208,128]{2,1,0:T(8,128)(2,1)S(1)} %all-to-all-done.2.refs_0_), channel_id=1, source_target_pairs={{0,32},{32,0},{1,33},{33,1},{2,34},{34,2},{3,35},{35,3},{4,36},{36... | collective-permute-start | bytes 1277960 | tf_op jit(solution)/shard_map/ppermute | solution.py:257
  81.0 8.5 %collective-permute-start.18 = (s16[8,208,128]{2,1,0:T(8,128)(2,1)S(1)}, s16[8,208,128]{2,1,0:T(8,128)(2,1)S(1)}, u32[]{:S(2)}, u32[]{:S(2)}) collective-permute-start(s16[8,208,128]{2,1,0:T(8,128)(2,1)S(1)} %all-to-all-done.2.refs_0_), channel_id=1, source_target_pairs={{0,2},{8,10},{16,18},{24,26},{2,4},{10,12},{18,20},{26,28},{4,6},{... | collective-permute-start | bytes 1277960 | tf_op jit(solution)/shard_map/ppermute | solution.py:307
  81.0 8.5 %collective-permute-start.19 = (s16[8,208,128]{2,1,0:T(8,128)(2,1)S(1)}, s16[8,208,128]{2,1,0:T(8,128)(2,1)S(1)}, u32[]{:S(2)}, u32[]{:S(2)}) collective-permute-start(s16[8,208,128]{2,1,0:T(8,128)(2,1)S(1)} %all-to-all-done.2.refs_0_), channel_id=1, source_target_pairs={{0,6},{8,14},{16,22},{24,30},{2,0},{10,8},{18,16},{26,24},{4,2},{1... | collective-permute-start | bytes 1277960 | tf_op jit(solution)/shard_map/ppermute | solution.py:307
  89.5 3.5 %collective-permute-start.20 = (s16[8,208,128]{2,1,0:T(8,128)(2,1)S(1)}, s16[8,208,128]{2,1,0:T(8,128)(2,1)S(1)}, u32[]{:S(2)}, u32[]{:S(2)}) collective-permute-start(s16[8,208,128]{2,1,0:T(8,128)(2,1)S(1)} %collective-permute-done.18.refs_0_), channel_id=1, source_target_pairs={{0,32},{32,0},{1,33},{33,1},{2,34},{34,2},{3,35},{35,3},{4,36},{36... | collective-permute-start | bytes 1277960 | tf_op jit(solution)/shard_map/ppermute | solution.py:257
  90.5 2.6 %collective-permute-start.21 = (s16[8,208,128]{2,1,0:T(8,128)(2,1)S(1)}, s16[8,208,128]{2,1,0:T(8,128)(2,1)S(1)}, u32[]{:S(2)}, u32[]{:S(2)}) collective-permute-start(s16[8,208,128]{2,1,0:T(8,128)(2,1)S(1)} %collective-permute-done.19.refs_1_), channel_id=1, source_target_pairs={{0,32},{32,0},{1,33},{33,1},{2,34},{34,2},{3,35},{35,3},{4,36},{36... | collective-permute-start | bytes 1277960 | tf_op jit(solution)/shard_map/ppermute | solution.py:257
  90.5 8.8 %collective-permute-start.22 = (s16[8,208,128]{2,1,0:T(8,128)(2,1)S(1)}, s16[8,208,128]{2,1,0:T(8,128)(2,1)S(1)}, u32[]{:S(2)}, u32[]{:S(2)}) collective-permute-start(s16[8,208,128]{2,1,0:T(8,128)(2,1)S(1)} %all-to-all-done.2.refs_0_), channel_id=1, source_target_pairs={{0,4},{8,12},{16,20},{24,28},{2,6},{10,14},{18,22},{26,30},{4,0},{... | collective-permute-start | bytes 1277960 | tf_op jit(solution)/shard_map/ppermute | solution.py:307
  99.3 2.7 %collective-permute-start.23 = (s16[8,208,128]{2,1,0:T(8,128)(2,1)S(1)}, s16[8,208,128]{2,1,0:T(8,128)(2,1)S(1)}, u32[]{:S(2)}, u32[]{:S(2)}) collective-permute-start(s16[8,208,128]{2,1,0:T(8,128)(2,1)S(1)} %collective-permute-done.22.refs_0_), channel_id=1, source_target_pairs={{0,32},{32,0},{1,33},{33,1},{2,34},{34,2},{3,35},{35,3},{4,36},{36... | collective-permute-start | bytes 1277960 | tf_op jit(solution)/shard_map/ppermute | solution.py:257

commit v8 on v6

--- a/solution.py
+++ b/solution.py
@@ -146,11 +146,12 @@
         centers_ref[i * n : (i + 1) * n] = ref[...]
 
 
-def refine_kernel(own, one, two, three, refined_ref, coded_ref):
-    even = add_coded(two, 0, *add_coded(own, 0, *nothing()))
-    odd = add_coded(three, 0, *add_coded(one, 0, *nothing()))
-    counts = to_column(even[1] + odd[1])
-    refined = [(even[0][b] + odd[0][b]) / counts for b in range(COLS)]
+def refine_kernel(groups, refined_ref, coded_ref):
+    blocks, counts = nothing()
+    for g in range(groups.shape[0]):
+        blocks, counts = add_coded(groups, g, blocks, counts)
+    counts = to_column(counts)
+    refined = [blocks[b] / counts for b in range(COLS)]
     for b in range(COLS):
         refined_ref[:, b * 128 : (b + 1) * 128] = refined[b]
     coded, codes = code_blocks(refined)
@@ -257,11 +258,8 @@
     return lax.ppermute(value, axis, [(0, 1), (1, 0)])
 
 
-def around_z(part):
-    return [part] + [
-        lax.ppermute(part, "zh", [(i, (i + k) % 4) for i in range(4)])
-        for k in (1, 2, 3)
-    ]
+def all_of_z(part):
+    return lax.all_to_all(jnp.broadcast_to(part, (4, *part.shape[1:])), "zh", 0, 0)
 
 
 def spot(core, a, b, zl):
@@ -370,11 +368,11 @@
         flops=1 << 20, moved=1 << 20,
     )
     (current,) = after(group, (current,))
-    groups, current = lax.optimization_barrier((around_z(group), around(current, 1)))
+    groups, current = lax.optimization_barrier((all_of_z(group), around(current, 1)))
     refined, code = call(
         refine_kernel,
         (shape((HALF, D), f32), coded(EACH)),
-        *groups,
+        groups,
         flops=1 << 20, moved=1 << 20,
     )
 

time: 102 us -> 106 us (1.039)
  blocking collectives: 17.4 us -> 33.2 us
  starting transfers between devices: 43.8 us -> 32.5 us
  waiting for transfers between devices: 12 us -> 10.1 us
  local copies, waits for them, and re-layouts: 3.3 us -> 5.05 us
    all_to_all x0 -> x1, blocking collectives: none -> 15.8 us  [all_of_z(): lax.all_to_all(jnp.broadcast_to(part, (4, *part.shape[1:])), 'zh', 0, 0)]
    ppermute x3 -> x0, starting transfers between devices: 10 us -> none  [around_z(): lax.ppermute(part, 'zh', [(i, (i + k) % 4) for i in range(4)])]
    ppermute x3 -> x0, waiting for transfers between devices: 1.9 us -> none  [around_z(): lax.ppermute(part, 'zh', [(i, (i + k) % 4) for i in range(4)])]
    unnamed x12 -> x16, local copies, waits for them, and re-layouts: 3.29 us -> 5.02 us
    ppermute x12, starting transfers between devices: 16.4 us -> 15.3 us  [swap(): return lax.ppermute(value, axis, [(0, 1), (1, 0)])]
  transfers between devices with their start and end apart: 26 -> 23, of which waited for: 4 -> 3; matrix products, arithmetic and copies ran while one was open for 0% -> 0% of each run, Pallas kernels for 16% -> 14%
where the time goes in v8:
time: 106 us; the launch traced here: 105 us
  blocking collectives  33.2 us (31%)
  starting transfers between devices  32.5 us (31%)
  Pallas kernels  23.5 us (22%)
  waiting for transfers between devices  10.1 us (10%)
  local copies, waits for them, and re-layouts  5.05 us (5%)
    pallas_call x12, Pallas kernels, call(): pl.pallas_call(kernel, out_shape=out_shape, in_specs=specs, out_specs=tup...  23.5 us
    all_to_all x1, blocking collectives, exchange_four(): lax.all_to_all(value.reshape(4, -1, 128), ('core', 'y', 'x'), 0, 0, axis_...  17.4 us
    all_to_all x1, blocking collectives, all_of_z(): lax.all_to_all(jnp.broadcast_to(part, (4, *part.shape[1:])), 'zh', 0, 0)  15.8 us
    ppermute x12, starting transfers between devices, swap(): return lax.ppermute(value, axis, [(0, 1), (1, 0)])  15.3 us
    all_to_all x2, starting transfers between devices, exchange_eight(): lax.all_to_all(value, ('core', 'y', 'x', 'zl'), 0, 0, axis_index_groups=e...  9.03 us
    ppermute x9, starting transfers between devices, around(): parts.append(lax.ppermute(part, ('core', 'y', 'x'), pairs))  8.19 us
    ppermute x9, waiting for transfers between devices, around(): parts.append(lax.ppermute(part, ('core', 'y', 'x'), pairs))  5.59 us
    unnamed x16, local copies, waits for them, and re-layouts  5.02 us
  transfers between devices with their start and end apart: 23, of which 3 were waited for; matrix products, arithmetic and copies ran while one was open for 0% of the time, Pallas kernels for 14%

profile of v8, /device:TPU:1, one launch (start us, length us, event | category | flops | bytes accessed | tf_op | source)
XLA Modules:
  0.0 105.2 jit_solution(1043057691520687235)
XLA Ops:
  0.6 3.3 %collective-permute-start.1 = (bf16[1024,768]{1,0:T(8,128)(2,1)}, bf16[1024,768]{1,0:T(8,128)(2,1)S(1)}, u32[]{:S(2)}, u32[]{:S(2)}) collective-permute-start(bf16[1024,768]{1,0:T(8,128)(2,1)} %rows_ref), channel_id=1, source_target_pairs={{0,32},{32,0},{1,33},{33,1},{2,34},{34,2},{3,35},{35,3},{4,36},{36... | collective-permute-start | bytes 4718600 | tf_op jit(solution)/shard_map/ppermute | solution.py:258
  4.0 1.0 collective-permute-start
  5.0 1.4 %copy-done.1 = bf16[1024,768]{1,0:T(8,128)(2,1)S(1)} copy-done((bf16[1024,768]{1,0:T(8,128)(2,1)S(1)}, bf16[1024,768]{1,0:T(8,128)(2,1)}, u32[]{:S(2)}) %copy-start.1) | copy-done | bytes 1572888
  6.4 0.7 copy-done.3
  7.1 2.4 %shard_map.58.own_sums = f32[1024,768]{1,0:T(8,128)S(1)} custom-call(s32[3]{0:T(128)S(1)} %pad_add_fusion.place, s32[1,1024]{1,0:T(1,128)S(1)} %bitcast.13, bf16[1024,768]{1,0:T(8,128)(2,1)S(1)} %copy-done.1), custom_call_target="tpu_custom_call" | custom-call | flops 1610612736 | bytes 5242880 | tf_op jit(solution)/shard_map/pallas_call | solution.py:245
  9.6 3.8 %shard_map.59 = s16[32,208,128]{2,1,0:T(8,128)(2,1)S(1)} custom-call(s32[3]{0:T(128)S(1)} %pad_add_fusion.place, s32[1,1024]{1,0:T(1,128)S(1)} %bitcast.14, s32[1,1024]{1,0:T(1,128)S(1)} %collective-permute-done.labels, f32[1024,768]{1,0:T(8,128)S(1)} %shard_map.58.own_sums, bf16[1024,768]{1,0:T(8,128)(2,1)S(1)} %collective-permute-done.1.rows), custom_call_target="tpu_custom_call" | custom-call | flops 1610612736 | bytes 6291456 | tf_op jit(solution)/shard_map/pallas_call | solution.py:245
  13.4 17.4 %all_to_all.20 = s16[4,1664,128]{2,1,0:T(8,128)(2,1)S(1)} all-to-all(s16[4,1664,128]{2,1,0:T(8,128)(2,1)S(1)} %bitcast.9), channel_id=1, replica_groups={{0,2,4,6},{8,10,12,14},{16,18,20,22},{24,26,28,30},{32,40,48,56},{34,42..., dimensions={0} | all-to-all | bytes 3407872 | tf_op jit(solution)/shard_map/all_to_all | solution.py:287
  30.8 1.6 %shard_map.60 = s16[8,208,128]{2,1,0:T(8,128)(2,1)} custom-call(s16[32,208,128]{2,1,0:T(8,128)(2,1)S(1)} %bitcast.10), custom_call_target="tpu_custom_call" | custom-call | flops 4194304 | bytes 3145728 | tf_op jit(solution)/shard_map/pallas_call | solution.py:245
  32.4 3.9 %all-to-all-start.1 = ((s16[8,208,128]{2,1,0:T(8,128)(2,1)}), s16[8,208,128]{2,1,0:T(8,128)(2,1)S(1)}, u32[]{:S(2)}, u32[]{:S(2)}) async-start(s16[8,208,128]{2,1,0:T(8,128)(2,1)} %shard_map.60), calls=%async_computation.1 | async-start | bytes 851968 | tf_op jit(solution)/shard_map/all_to_all | solution.py:293
  36.6 2.4 %collective-permute-start.4 = (bf16[64,768]{1,0:T(8,128)(2,1)S(1)}, bf16[64,768]{1,0:T(8,128)(2,1)S(1)}, u32[]{:S(2)}, u32[]{:S(2)}) collective-permute-start(bf16[64,768]{1,0:T(8,128)(2,1)S(1)} %pad_maximum_fusion.c0), channel_id=1, source_target_pairs={{0,6},{8,14},{16,22},{24,30},{2,0},{10,8},{18,16},{26,24},{4,2},{1... | collective-permute-start | bytes 294920 | tf_op jit(solution)/shard_map/ppermute | solution.py:307
  38.9 0.6 shard_map.61
  39.6 1.2 %copy-done.4 = bf16[768,1024]{1,0:T(8,128)(2,1)} copy-done((bf16[768,1024]{1,0:T(8,128)(2,1)}, bf16[768,1024]{1,0:T(8,128)(2,1)S(1)}, u32[]{:S(2)}) %copy-start.4) | copy-done | bytes 1572888
  40.7 4.5 %all-to-all-done.1.in_ref = s16[8,208,128]{2,1,0:T(8,128)(2,1)S(1)} async-done(((s16[8,208,128]{2,1,0:T(8,128)(2,1)}), s16[8,208,128]{2,1,0:T(8,128)(2,1)S(1)}, u32[]{:S(2)}, u32[]{:S(2)}) %all-to-all-start.1) | async-done | bytes 426016 | tf_op jit(solution)/shard_map/all_to_all | solution.py:293
  45.2 0.9 collective-permute-done.5.c3
  46.8 2.4 %collective-permute-start.7 = (bf16[256,768]{1,0:T(8,128)(2,1)S(1)}, bf16[256,768]{1,0:T(8,128)(2,1)S(1)}, u32[]{:S(2)}, u32[]{:S(2)}) collective-permute-start(bf16[256,768]{1,0:T(8,128)(2,1)S(1)} %get-tuple-element.51.refs_0_), channel_id=1, source_target_pairs={{0,24},{8,0},{16,8},{24,16},{2,26},{10,2},{18,10},{26,18},{4,28},{... | collective-permute-start | bytes 1179656 | tf_op jit(solution)/shard_map/ppermute | solution.py:307
  49.3 15.8 %all_to_all.21.groups = s16[4,208,128]{2,1,0:T(8,128)(2,1)S(1)} all-to-all(s16[4,208,128]{2,1,0:T(8,128)(2,1)S(1)} %broadcast_in_dim.12), channel_id=1, replica_groups=mesh['zh'=4,'core'=2,'y'=4,'x'=4,'zl'=2] {'zh'}, dimensions={0} | all-to-all | bytes 425984 | tf_op jit(solution)/shard_map/all_to_all | solution.py:262
  65.1 0.7 copy-done.6
  65.8 1.0 shard_map.63
  66.8 5.2 %all-to-all-start.3 = ((s16[8,208,128]{2,1,0:T(8,128)(2,1)}), s16[8,208,128]{2,1,0:T(8,128)(2,1)S(1)}, u32[]{:S(2)}, u32[]{:S(2)}) async-start(s16[8,208,128]{2,1,0:T(8,128)(2,1)} %get-tuple-element.45), calls=%async_computation.3 | async-start | bytes 851968 | tf_op jit(solution)/shard_map/all_to_all | solution.py:293
  72.0 4.1 %collective-permute-start.11 = (bf16[256,768]{1,0:T(8,128)(2,1)S(1)}, bf16[256,768]{1,0:T(8,128)(2,1)}, u32[]{:S(2)}, u32[]{:S(2)}) collective-permute-start(bf16[256,768]{1,0:T(8,128)(2,1)S(1)} %get-tuple-element.51.refs_0_), channel_id=1, source_target_pairs={{0,32},{32,0},{1,33},{33,1},{2,34},{34,2},{3,35},{35,3},{4,36},{36... | collective-permute-start | bytes 1179656 | tf_op jit(solution)/shard_map/ppermute | solution.py:258
  77.2 1.0 copy-done.7
  78.2 1.8 %shard_map.64.least_ref = f32[8,1024]{1,0:T(8,128)S(1)} custom-call(bf16[768,1024]{1,0:T(8,128)(2,1)S(1)} %copy-done.5, bf16[256,768]{1,0:T(8,128)(2,1)S(1)} %get-tuple-element.51.refs_0_, bf16[256,768]{1,0:T(8,128)(2,1)S(1)} %copy-done.7, bf16[256,768]{1,0:T(8,128)(2,1)S(1)} %collective-permute-done.7.refs_2_, ...), custom_call_target="tpu_custom_call" | custom-call | flops 1610612736 | bytes 3145728 | tf_op jit(solution)/shard_map/pallas_call | solution.py:245
  80.1 4.3 %collective-permute-start.9 = (s16[8,208,128]{2,1,0:T(8,128)(2,1)S(1)}, s16[8,208,128]{2,1,0:T(8,128)(2,1)S(1)}, u32[]{:S(2)}, u32[]{:S(2)}) collective-permute-start(s16[8,208,128]{2,1,0:T(8,128)(2,1)S(1)} %all-to-all-done.3.refs_0_), channel_id=1, source_target_pairs={{0,32},{32,0},{1,33},{33,1},{2,34},{34,2},{3,35},{35,3},{4,36},{36... | collective-permute-start | bytes 1277960 | tf_op jit(solution)/shard_map/ppermute | solution.py:258
  84.3 2.7 %collective-permute-start.16 = (s16[8,208,128]{2,1,0:T(8,128)(2,1)S(1)}, s16[8,208,128]{2,1,0:T(8,128)(2,1)S(1)}, u32[]{:S(2)}, u32[]{:S(2)}) collective-permute-start(s16[8,208,128]{2,1,0:T(8,128)(2,1)S(1)} %all-to-all-done.3.refs_0_), channel_id=1, source_target_pairs={{0,6},{8,14},{16,22},{24,30},{2,0},{10,8},{18,16},{26,24},{4,2},{1... | collective-permute-start | bytes 1277960 | tf_op jit(solution)/shard_map/ppermute | solution.py:307
  87.0 3.8 %shard_map.66 = (f32[1,1024]{1,0:T(1,128)}, f32[64,768]{1,0:T(8,128)}) custom-call(s32[3]{0:T(128)S(1)} %pad_add_fusion.place, f32[1,1024]{1,0:T(1,128)S(1)} %get-tuple-element.56.norms_ref, bf16[768,1024]{1,0:T(8,128)(2,1)S(1)} %copy-done.5, f32[8,1024]{1,0:T(8,128)S(1)} %shard_map.64.least_ref, f32[32,768]{1,0:T(8,128)S(1)} %get-tuple-element.46.own, ...), custom_call_target="tpu_custom_call" | custom-call | flops 1610612736 | bytes 3145728 | tf_op jit(solution)/shard_map/pallas_call | solution.py:245
  90.9 1.9 %shard_map.65.least_ref = f32[8,1024]{1,0:T(8,128)S(1)} custom-call(bf16[768,1024]{1,0:T(8,128)(2,1)S(1)} %copy-done.5, f32[8,1024]{1,0:T(8,128)S(1)} %broadcast_in_dim.10.least_ref, s16[8,208,128]{2,1,0:T(8,128)(2,1)S(1)} %all-to-all-done.3.refs_0_, s16[8,208,128]{2,1,0:T(8,128)(2,1)S(1)} %collective-permute-done.9.refs_1_), custom_call_target="tpu_custom_call" | custom-call | flops 1610612736 | bytes 1048576 | tf_op jit(solution)/shard_map/pallas_call | solution.py:245
  92.7 4.6 %collective-permute-done.15.refs_0_ = s16[8,208,128]{2,1,0:T(8,128)(2,1)S(1)} collective-permute-done((s16[8,208,128]{2,1,0:T(8,128)(2,1)S(1)}, s16[8,208,128]{2,1,0:T(8,128)(2,1)S(1)}, u32[]{:S(2)}, u32[]{:S(2)}) %collective-permute-start.15) | collective-permute-done | bytes 426016 | tf_op jit(solution)/shard_map/ppermute | solution.py:307
  97.4 0.9 collective-permute-start.18
  98.3 1.9 %shard_map.67.least_ref = f32[8,1024]{1,0:T(8,128)S(1)} custom-call(bf16[768,1024]{1,0:T(8,128)(2,1)S(1)} %copy-done.5, f32[8,1024]{1,0:T(8,128)S(1)} %shard_map.65.least_ref, s16[8,208,128]{2,1,0:T(8,128)(2,1)S(1)} %collective-permute-done.15.refs_0_, s16[8,208,128]{2,1,0:T(8,128)(2,1)S(1)} %collective-permute-done.16.refs_1_), custom_call_target="tpu_custom_call" | custom-call | flops 1610612736 | bytes 1048576 | tf_op jit(solution)/shard_map/pallas_call | solution.py:245
  100.2 0.6 collective-permute-start.20
  100.8 2.7 %shard_map.68.least_ref = f32[8,1024]{1,0:T(8,128)S(1)} custom-call(bf16[768,1024]{1,0:T(8,128)(2,1)S(1)} %copy-done.5, f32[8,1024]{1,0:T(8,128)S(1)} %shard_map.67.least_ref, s16[8,208,128]{2,1,0:T(8,128)(2,1)S(1)} %collective-permute-done.18.refs_0_, s16[8,208,128]{2,1,0:T(8,128)(2,1)S(1)} %collective-permute-done.19.refs_1_, ...), custom_call_target="tpu_custom_call" | custom-call | flops 2415919104 | bytes 1572864 | tf_op jit(solution)/shard_map/pallas_call | solution.py:245
  103.5 1.7 %shard_map.69 = f32[1,1024]{1,0:T(1,128)} custom-call(bf16[768,1024]{1,0:T(8,128)(2,1)S(1)} %copy-done.5, f32[8,1024]{1,0:T(8,128)S(1)} %shard_map.68.least_ref, f32[1,1024]{1,0:T(1,128)S(1)} %get-tuple-element.56.norms_ref, s16[8,208,128]{2,1,0:T(8,128)(2,1)S(1)} %collective-permute-done.20.piece), custom_call_target="tpu_custom_call" | custom-call | flops 805306368 | bytes 524288 | tf_op jit(solution)/shard_map/pallas_call | solution.py:245
  (49 shorter events, 2.3 us)
Async XLA Ops:
  0.6 3.3 %copy-start = (bf16[64,768]{1,0:T(8,128)(2,1)S(1)}, bf16[64,768]{1,0:T(8,128)(2,1)}, u32[]{:S(2)}) copy-start(bf16[64,768]{1,0:T(8,128)(2,1)} %param.4) | copy-start | bytes 294916
  0.6 8.9 %collective-permute-start.1 = (bf16[1024,768]{1,0:T(8,128)(2,1)}, bf16[1024,768]{1,0:T(8,128)(2,1)S(1)}, u32[]{:S(2)}, u32[]{:S(2)}) collective-permute-start(bf16[1024,768]{1,0:T(8,128)(2,1)} %rows_ref), channel_id=1, source_target_pairs={{0,32},{32,0},{1,33},{33,1},{2,34},{34,2},{3,35},{35,3},{4,36},{36... | collective-permute-start | bytes 4718600 | tf_op jit(solution)/shard_map/ppermute | solution.py:258
  4.0 5.6 %collective-permute-start.2 = (bf16[32,768]{1,0:T(8,128)(2,1)S(1)}, bf16[32,768]{1,0:T(8,128)(2,1)S(1)}, u32[]{:S(2)}, u32[]{:S(2)}) collective-permute-start(bf16[32,768]{1,0:T(8,128)(2,1)S(1)} %constant_dynamic-slice_fusion), channel_id=1, source_target_pairs={{0,1},{1,0},{2,3},{3,2},{4,5},{5,4},{6,7},{7,6},{8,9},{9,8},{10,11... | collective-permute-start | bytes 147464 | tf_op jit(solution)/shard_map/ppermute | solution.py:258
  4.0 5.6 %collective-permute-start = (s32[1,1024]{1,0:T(1,128)}, s32[1,1024]{1,0:T(1,128)S(1)}, u32[]{:S(2)}, u32[]{:S(2)}) collective-permute-start(s32[1,1024]{1,0:T(1,128)} %bitcast.12), channel_id=1, source_target_pairs={{0,32},{32,0},{1,33},{33,1},{2,34},{34,2},{3,35},{35,3},{4,36},{36... | collective-permute-start | bytes 12296 | tf_op jit(solution)/shard_map/ppermute | solution.py:258
  5.0 1.4 %copy-start.1 = (bf16[1024,768]{1,0:T(8,128)(2,1)S(1)}, bf16[1024,768]{1,0:T(8,128)(2,1)}, u32[]{:S(2)}) copy-start(bf16[1024,768]{1,0:T(8,128)(2,1)} %rows_ref) | copy-start | bytes 4718596
  6.4 0.7 copy-start.3
  30.8 8.1 %copy-start.2 = (bf16[1024,768]{1,0:T(8,128)(2,1)S(1)}, bf16[1024,768]{1,0:T(8,128)(2,1)}, u32[]{:S(2)}) copy-start(bf16[1024,768]{1,0:T(8,128)(2,1)} %rows_ref) | copy-start | bytes 4718596
  32.4 12.8 %all-to-all-start.1 = ((s16[8,208,128]{2,1,0:T(8,128)(2,1)}), s16[8,208,128]{2,1,0:T(8,128)(2,1)S(1)}, u32[]{:S(2)}, u32[]{:S(2)}) async-start(s16[8,208,128]{2,1,0:T(8,128)(2,1)} %shard_map.60), calls=%async_computation.1 | async-start | bytes 851968 | tf_op jit(solution)/shard_map/all_to_all | solution.py:293
  36.3 9.0 %collective-permute-start.3 = (bf16[64,768]{1,0:T(8,128)(2,1)S(1)}, bf16[64,768]{1,0:T(8,128)(2,1)S(1)}, u32[]{:S(2)}, u32[]{:S(2)}) collective-permute-start(bf16[64,768]{1,0:T(8,128)(2,1)S(1)} %pad_maximum_fusion.c0), channel_id=1, source_target_pairs={{0,2},{8,10},{16,18},{24,26},{2,4},{10,12},{18,20},{26,28},{4,6},{... | collective-permute-start | bytes 294920 | tf_op jit(solution)/shard_map/ppermute | solution.py:307
  36.6 8.7 %collective-permute-start.4 = (bf16[64,768]{1,0:T(8,128)(2,1)S(1)}, bf16[64,768]{1,0:T(8,128)(2,1)S(1)}, u32[]{:S(2)}, u32[]{:S(2)}) collective-permute-start(bf16[64,768]{1,0:T(8,128)(2,1)S(1)} %pad_maximum_fusion.c0), channel_id=1, source_target_pairs={{0,6},{8,14},{16,22},{24,30},{2,0},{10,8},{18,16},{26,24},{4,2},{1... | collective-permute-start | bytes 294920 | tf_op jit(solution)/shard_map/ppermute | solution.py:307
  38.9 7.2 %collective-permute-start.5 = (bf16[64,768]{1,0:T(8,128)(2,1)S(1)}, bf16[64,768]{1,0:T(8,128)(2,1)S(1)}, u32[]{:S(2)}, u32[]{:S(2)}) collective-permute-start(bf16[64,768]{1,0:T(8,128)(2,1)S(1)} %pad_maximum_fusion.c0), channel_id=1, source_target_pairs={{0,4},{8,12},{16,20},{24,28},{2,6},{10,14},{18,22},{26,30},{4,0},{... | collective-permute-start | bytes 294920 | tf_op jit(solution)/shard_map/ppermute | solution.py:307
  39.6 1.2 %copy-start.4 = (bf16[768,1024]{1,0:T(8,128)(2,1)}, bf16[768,1024]{1,0:T(8,128)(2,1)S(1)}, u32[]{:S(2)}) copy-start(bf16[768,1024]{1,0:T(8,128)(2,1)S(1)} %get-tuple-element.39.turned_ref) | copy-start | bytes 4718596
  45.2 32.0 %copy-start.5 = (bf16[768,1024]{1,0:T(8,128)(2,1)S(1)}, bf16[768,1024]{1,0:T(8,128)(2,1)}, u32[]{:S(2)}) copy-start(bf16[768,1024]{1,0:T(8,128)(2,1)} %copy-done.4) | copy-start | bytes 4718596
  46.5 18.6 %collective-permute-start.6 = (bf16[256,768]{1,0:T(8,128)(2,1)S(1)}, bf16[256,768]{1,0:T(8,128)(2,1)S(1)}, u32[]{:S(2)}, u32[]{:S(2)}) collective-permute-start(bf16[256,768]{1,0:T(8,128)(2,1)S(1)} %get-tuple-element.51.refs_0_), channel_id=1, source_target_pairs={{0,8},{8,16},{16,24},{24,0},{2,10},{10,18},{18,26},{26,2},{4,12},{... | collective-permute-start | bytes 1179656 | tf_op jit(solution)/shard_map/ppermute | solution.py:307
  46.8 18.2 %collective-permute-start.7 = (bf16[256,768]{1,0:T(8,128)(2,1)S(1)}, bf16[256,768]{1,0:T(8,128)(2,1)S(1)}, u32[]{:S(2)}, u32[]{:S(2)}) collective-permute-start(bf16[256,768]{1,0:T(8,128)(2,1)S(1)} %get-tuple-element.51.refs_0_), channel_id=1, source_target_pairs={{0,24},{8,0},{16,8},{24,16},{2,26},{10,2},{18,10},{26,18},{4,28},{... | collective-permute-start | bytes 1179656 | tf_op jit(solution)/shard_map/ppermute | solution.py:307
  49.2 16.6 %collective-permute-start.8 = (bf16[256,768]{1,0:T(8,128)(2,1)S(1)}, bf16[256,768]{1,0:T(8,128)(2,1)S(1)}, u32[]{:S(2)}, u32[]{:S(2)}) collective-permute-start(bf16[256,768]{1,0:T(8,128)(2,1)S(1)} %get-tuple-element.51.refs_0_), channel_id=1, source_target_pairs={{0,16},{8,24},{16,0},{24,8},{2,18},{10,26},{18,2},{26,10},{4,20},{... | collective-permute-start | bytes 1179656 | tf_op jit(solution)/shard_map/ppermute | solution.py:307
  65.1 0.7 copy-start.6
  66.8 13.2 %all-to-all-start.3 = ((s16[8,208,128]{2,1,0:T(8,128)(2,1)}), s16[8,208,128]{2,1,0:T(8,128)(2,1)S(1)}, u32[]{:S(2)}, u32[]{:S(2)}) async-start(s16[8,208,128]{2,1,0:T(8,128)(2,1)} %get-tuple-element.45), calls=%async_computation.3 | async-start | bytes 851968 | tf_op jit(solution)/shard_map/all_to_all | solution.py:293
  72.0 12.3 %collective-permute-start.11 = (bf16[256,768]{1,0:T(8,128)(2,1)S(1)}, bf16[256,768]{1,0:T(8,128)(2,1)}, u32[]{:S(2)}, u32[]{:S(2)}) collective-permute-start(bf16[256,768]{1,0:T(8,128)(2,1)S(1)} %get-tuple-element.51.refs_0_), channel_id=1, source_target_pairs={{0,32},{32,0},{1,33},{33,1},{2,34},{34,2},{3,35},{35,3},{4,36},{36... | collective-permute-start | bytes 1179656 | tf_op jit(solution)/shard_map/ppermute | solution.py:258
  76.2 8.2 %collective-permute-start.12 = (bf16[256,768]{1,0:T(8,128)(2,1)}, bf16[256,768]{1,0:T(8,128)(2,1)}, u32[]{:S(2)}, u32[]{:S(2)}) collective-permute-start(bf16[256,768]{1,0:T(8,128)(2,1)} %copy-done.6), channel_id=1, source_target_pairs={{0,32},{32,0},{1,33},{33,1},{2,34},{34,2},{3,35},{35,3},{4,36},{36... | collective-permute-start | bytes 1179656 | tf_op jit(solution)/shard_map/ppermute | solution.py:258
  76.3 3.8 %collective-permute-start.10 = (f32[32,768]{1,0:T(8,128)S(1)}, f32[32,768]{1,0:T(8,128)S(1)}, u32[]{:S(2)}, u32[]{:S(2)}) collective-permute-start(f32[32,768]{1,0:T(8,128)S(1)} %get-tuple-element.46.own), channel_id=1, source_target_pairs={{0,32},{32,0},{1,33},{33,1},{2,34},{34,2},{3,35},{35,3},{4,36},{36... | collective-permute-start | bytes 294920 | tf_op jit(solution)/shard_map/ppermute | solution.py:258
  76.7 10.3 %collective-permute-start.13 = (bf16[256,768]{1,0:T(8,128)(2,1)S(1)}, bf16[256,768]{1,0:T(8,128)(2,1)}, u32[]{:S(2)}, u32[]{:S(2)}) collective-permute-start(bf16[256,768]{1,0:T(8,128)(2,1)S(1)} %collective-permute-done.7.refs_2_), channel_id=1, source_target_pairs={{0,32},{32,0},{1,33},{33,1},{2,34},{34,2},{3,35},{35,3},{4,36},{36... | collective-permute-start | bytes 1179656 | tf_op jit(solution)/shard_map/ppermute | solution.py:258
  76.8 10.3 %collective-permute-start.14 = (bf16[256,768]{1,0:T(8,128)(2,1)S(1)}, bf16[256,768]{1,0:T(8,128)(2,1)}, u32[]{:S(2)}, u32[]{:S(2)}) collective-permute-start(bf16[256,768]{1,0:T(8,128)(2,1)S(1)} %collective-permute-done.8.refs_3_), channel_id=1, source_target_pairs={{0,32},{32,0},{1,33},{33,1},{2,34},{34,2},{3,35},{35,3},{4,36},{36... | collective-permute-start | bytes 1179656 | tf_op jit(solution)/shard_map/ppermute | solution.py:258
  77.2 1.0 copy-start.7
  80.1 10.8 %collective-permute-start.9 = (s16[8,208,128]{2,1,0:T(8,128)(2,1)S(1)}, s16[8,208,128]{2,1,0:T(8,128)(2,1)S(1)}, u32[]{:S(2)}, u32[]{:S(2)}) collective-permute-start(s16[8,208,128]{2,1,0:T(8,128)(2,1)S(1)} %all-to-all-done.3.refs_0_), channel_id=1, source_target_pairs={{0,32},{32,0},{1,33},{33,1},{2,34},{34,2},{3,35},{35,3},{4,36},{36... | collective-permute-start | bytes 1277960 | tf_op jit(solution)/shard_map/ppermute | solution.py:258
  84.3 13.0 %collective-permute-start.15 = (s16[8,208,128]{2,1,0:T(8,128)(2,1)S(1)}, s16[8,208,128]{2,1,0:T(8,128)(2,1)S(1)}, u32[]{:S(2)}, u32[]{:S(2)}) collective-permute-start(s16[8,208,128]{2,1,0:T(8,128)(2,1)S(1)} %all-to-all-done.3.refs_0_), channel_id=1, source_target_pairs={{0,2},{8,10},{16,18},{24,26},{2,4},{10,12},{18,20},{26,28},{4,6},{... | collective-permute-start | bytes 1277960 | tf_op jit(solution)/shard_map/ppermute | solution.py:307
  84.3 13.0 %collective-permute-start.16 = (s16[8,208,128]{2,1,0:T(8,128)(2,1)S(1)}, s16[8,208,128]{2,1,0:T(8,128)(2,1)S(1)}, u32[]{:S(2)}, u32[]{:S(2)}) collective-permute-start(s16[8,208,128]{2,1,0:T(8,128)(2,1)S(1)} %all-to-all-done.3.refs_0_), channel_id=1, source_target_pairs={{0,6},{8,14},{16,22},{24,30},{2,0},{10,8},{18,16},{26,24},{4,2},{1... | collective-permute-start | bytes 1277960 | tf_op jit(solution)/shard_map/ppermute | solution.py:307
  87.0 13.2 %collective-permute-start.17 = (s16[8,208,128]{2,1,0:T(8,128)(2,1)S(1)}, s16[8,208,128]{2,1,0:T(8,128)(2,1)S(1)}, u32[]{:S(2)}, u32[]{:S(2)}) collective-permute-start(s16[8,208,128]{2,1,0:T(8,128)(2,1)S(1)} %all-to-all-done.3.refs_0_), channel_id=1, source_target_pairs={{0,4},{8,12},{16,20},{24,28},{2,6},{10,14},{18,22},{26,30},{4,0},{... | collective-permute-start | bytes 1277960 | tf_op jit(solution)/shard_map/ppermute | solution.py:307
  97.4 3.4 %collective-permute-start.18 = (s16[8,208,128]{2,1,0:T(8,128)(2,1)S(1)}, s16[8,208,128]{2,1,0:T(8,128)(2,1)S(1)}, u32[]{:S(2)}, u32[]{:S(2)}) collective-permute-start(s16[8,208,128]{2,1,0:T(8,128)(2,1)S(1)} %collective-permute-done.15.refs_0_), channel_id=1, source_target_pairs={{0,32},{32,0},{1,33},{33,1},{2,34},{34,2},{3,35},{35,3},{4,36},{36... | collective-permute-start | bytes 1277960 | tf_op jit(solution)/shard_map/ppermute | solution.py:258
  98.3 2.5 %collective-permute-start.19 = (s16[8,208,128]{2,1,0:T(8,128)(2,1)S(1)}, s16[8,208,128]{2,1,0:T(8,128)(2,1)S(1)}, u32[]{:S(2)}, u32[]{:S(2)}) collective-permute-start(s16[8,208,128]{2,1,0:T(8,128)(2,1)S(1)} %collective-permute-done.16.refs_1_), channel_id=1, source_target_pairs={{0,32},{32,0},{1,33},{33,1},{2,34},{34,2},{3,35},{35,3},{4,36},{36... | collective-permute-start | bytes 1277960 | tf_op jit(solution)/shard_map/ppermute | solution.py:258
  100.2 3.3 %collective-permute-start.20 = (s16[8,208,128]{2,1,0:T(8,128)(2,1)S(1)}, s16[8,208,128]{2,1,0:T(8,128)(2,1)S(1)}, u32[]{:S(2)}, u32[]{:S(2)}) collective-permute-start(s16[8,208,128]{2,1,0:T(8,128)(2,1)S(1)} %collective-permute-done.17.refs_2_), channel_id=1, source_target_pairs={{0,32},{32,0},{1,33},{33,1},{2,34},{34,2},{3,35},{35,3},{4,36},{36... | collective-permute-start | bytes 1277960 | tf_op jit(solution)/shard_map/ppermute | solution.py:258
